TPU v7x, 256 devices: a whole 4x4x8 slice. The times are simulated.
256 devices in a mesh: blk: 64 (over x, z_lo, y, core), pair: 4 (over z_hi).
Axes of the slice: x: 4, y: 4, z: 8 (z_hi: 4, z_lo: 2; z = z_hi * 2 + z_lo), core: 2. Of those that a mesh axis runs over, the one named last changes fastest.
Arguments:
- features: bfloat16 [4, 8192, 256], P('pair', 'blk'), may hold values from -4 to 4
- last_features: bfloat16 [8192, 256], P('blk'), may hold values from -4 to 4
- growth: float32 [4, 8192], P('pair', 'blk'), may hold values from 0.5 to 2
- cell_counts: int32 [5], replicated, may hold values from 4096 to 8192
Outputs:
- source_potential: float32 [4, 8192], P('pair', 'blk')
- target_potential: float32 [4, 8192], P('pair', 'blk')
- row_mass: float32 [4, 8192], P('pair', 'blk')
Inputs may be any that keep to these rules, and one draw needn't show every extreme that they name: Time point t holds cell_counts[t] cells, in its first slots.
All inputs are finite; a program needn't handle non-finite values.
Results may differ from a plain program's by a relative error of at most 0.0003.
Values may be sent and summed in bfloat16 or wider, within the bound.
No kernel may reach another device: no remote copies, remote signals or barrier semaphores. Data moves between devices by JAX's collectives and lax.ppermute only.
A program may use at most 64 MiB of HBM per device.

v0:
```python
import math

import jax
import jax.numpy as jnp
from jax import lax
from jax.sharding import PartitionSpec as P

ITERS = 2


EPSILON = 0.1
PENALTY = 1.0


def passed_along(value, axis, steps):
    count = lax.axis_size(axis)
    leading, last = (max(0, -steps), min(count, count - steps))
    return lax.ppermute(value, axis, [(source, source + steps) for source in range(leading, last)])


def from_everyone(array, axis):
    copies = jnp.broadcast_to(array, (lax.axis_size(axis), *array.shape))
    return lax.all_to_all(copies, axis, split_axis=0, concat_axis=0, tiled=True)


def over_copies(array, axis):
    everything = from_everyone(array, axis)
    return jnp.sum(everything, axis=0)


def in_one(arrays, axis):
    ends = [0]
    for a in arrays:
        ends.append(ends[-1] + a.size)
    total = over_copies(jnp.concatenate([a.ravel() for a in arrays]), axis)
    return tuple((total[b:e].reshape(a.shape) for a, b, e in zip(arrays, ends, ends[1:])))


def in_one_piece(arrays, axis, dim, along):
    both = jnp.concatenate(arrays, axis=along)
    result, at, finished = (lax.all_gather(both, axis, axis=dim, tiled=True), 0, [])
    for a in arrays:
        finished.append(lax.slice_in_dim(result, at, at + a.shape[along], axis=along))
        at += a.shape[along]
    return tuple(finished)


def in_order(blocks, dim):
    blocks = jnp.moveaxis(blocks, 0, dim)
    lengths = blocks.shape
    return blocks.reshape(*lengths[:dim], lengths[dim] * lengths[dim + 1], *lengths[dim + 2 :])


def gathered_copies(array, axis, dim):
    blocks = from_everyone(array, axis)
    return in_order(blocks, dim)


def cost_tile(row_block, row_norms, columns, inverse_scale):
    widened = columns.astype(jnp.float32)
    column_norms = jnp.sum(widened * widened, axis=1)
    products = lax.dot_general(
        row_block, columns, (((1,), (1,)), ((), ())), preferred_element_type=jnp.float32
    )
    return inverse_scale * (row_norms[:, None] + column_norms[None, :] - 2.0 * products)


def summing(row_block, row_norms, potentials, admitted, inverse_scale):

    def accumulate(running, shards, anchor):
        span_cols = math.gcd(shards.shape[0], 512)

        def advance(partial_value, number):
            leading = number * span_cols
            columns = lax.dynamic_slice_in_dim(shards, leading, span_cols, 0)
            weights = lax.dynamic_slice_in_dim(potentials, leading, span_cols, 0)
            present = leading + jnp.arange(span_cols, dtype=jnp.int32) < admitted
            scores = cost_tile(row_block, row_norms, columns, inverse_scale)
            summands = jnp.where(present[None, :], jnp.exp(weights[None, :] - scores), 0.0)
            return (partial_value + jnp.sum(summands, axis=1), None)

        result, _ = lax.scan(
            advance, running, jnp.arange(shards.shape[0] // span_cols, dtype=jnp.int32)
        )
        return result

    return accumulate


def local(features, last_features, growth, cell_counts):
    sources = features[0]
    rows_here = sources.shape[0]
    cell_total = rows_here * lax.axis_size("blk")
    pair_place = lax.axis_index("pair")
    shifted = passed_along(sources, "pair", -1)
    targets = jnp.where(pair_place == lax.axis_size("pair") - 1, last_features, shifted)
    count_source = lax.dynamic_index_in_dim(cell_counts, pair_place, 0, keepdims=False)
    count_target = lax.dynamic_index_in_dim(cell_counts, pair_place + 1, 0, keepdims=False)
    position = lax.axis_index("blk") * rows_here + jnp.arange(rows_here, dtype=jnp.int32)
    source_present = position < count_source
    target_present = position < count_target
    source_widened = sources.astype(jnp.float32)
    target_widened = targets.astype(jnp.float32)
    source_norms = jnp.sum(source_widened * source_widened, axis=1)
    target_norms = jnp.sum(target_widened * target_widened, axis=1)
    moment_sums = in_one(
        (
            jnp.sum(jnp.where(source_present[:, None], source_widened, 0.0), axis=0),
            jnp.sum(jnp.where(source_present, source_norms, 0.0)),
            jnp.sum(jnp.where(target_present[:, None], target_widened, 0.0), axis=0),
            jnp.sum(jnp.where(target_present, target_norms, 0.0)),
        ),
        "blk",
    )
    source_count = count_source.astype(jnp.float32)
    target_count = count_target.astype(jnp.float32)
    source_mean = moment_sums[0] / source_count
    target_mean = moment_sums[2] / target_count
    spread = (
        moment_sums[1] / source_count
        + moment_sums[3] / target_count
        - 2.0 * jnp.sum(source_mean * target_mean)
    )
    inverse_scale = 1.0 / (EPSILON * spread)
    exponent = PENALTY / (PENALTY + EPSILON)
    log_source = jnp.log(growth[0] / source_count)
    log_target = -jnp.log(target_count)
    row_zeros = jnp.zeros((rows_here,), jnp.float32)
    zero_anchor = jnp.zeros((), jnp.int32)
    every_target, every_source = in_one_piece((targets, sources), "blk", 0, 1)

    def fold_rows(accumulate, initial):
        return accumulate(initial, every_target, zero_anchor)

    def row_sums(target_all):
        accumulate = summing(sources, source_norms, target_all, count_target, inverse_scale)
        return fold_rows(accumulate, row_zeros)

    target_all = jnp.zeros((cell_total,), jnp.float32)
    source_pot = row_zeros
    target_pot = row_zeros
    for repeat in range(ITERS):
        sums_rows = row_sums(target_all)
        source_pot = jnp.where(source_present, exponent * (log_source - jnp.log(sums_rows)), 0.0)
        source_all = gathered_copies(source_pot, "blk", 0)
        accumulate = summing(targets, target_norms, source_all, count_source, inverse_scale)
        sums_cols = accumulate(row_zeros, every_source, zero_anchor)
        target_pot = jnp.where(target_present, exponent * (log_target - jnp.log(sums_cols)), 0.0)
        target_all = gathered_copies(target_pot, "blk", 0)
    sums_rows = row_sums(target_all)
    row_mass = jnp.where(source_present, source_count * jnp.exp(source_pot) * sums_rows, 0.0)
    return (source_pot[None, :], target_pot[None, :], row_mass[None, :])


def solution(mesh):
    placed = (P("pair", "blk", None), P("blk", None), P("pair", "blk"), P())
    return jax.shard_map(
        local,
        mesh=mesh,
        in_specs=placed,
        out_specs=(P("pair", "blk"), P("pair", "blk"), P("pair", "blk")),
        check_vma=False,
    )
```

profile of v0, /device:TPU:1, one launch (start us, length us, event | category | flops | bytes accessed | tf_op | source)
XLA Modules:
  0.0 555.7 jit_solution(601829802275578046)
XLA Ops:
  7.2 1.3 collective-permute-start
  8.5 1.4 fusion.63
  10.6 4.2 collective-permute-done
  14.9 1.5 pad_maximum_fusion
  19.2 1.3 select_reduce_fusion
  20.5 1.4 pad_maximum_fusion.1
  22.6 10.4 %all-to-all-start = ((f32[64,1,514]{2,1,0:T(1,128)}), f32[64,1,514]{2,1,0:T(1,128)S(1)}, u32[]{:S(2)}, u32[]{:S(2)}) async-start(f32[64,1,514]{2,1,0:T(1,128)} %broadcast_in_dim.120), calls=%async_computation | async-start | bytes 327680 | tf_op jit(solution)/shard_map/all_to_all | solution.py:23
  34.3 7.6 %all-to-all-done = f32[64,1,514]{2,1,0:T(1,128)S(1)} async-done(((f32[64,1,514]{2,1,0:T(1,128)}), f32[64,1,514]{2,1,0:T(1,128)S(1)}, u32[]{:S(2)}, u32[]{:S(2)}) %all-to-all-start) | async-done | bytes 131616 | tf_op jit(solution)/shard_map/all_to_all | solution.py:23
  45.3 91.6 %all-gather.2.cloned.1.call-done = bf16[8192,512]{1,0:T(8,128)(2,1)} async-done(((bf16[128,512]{1,0:T(8,128)(2,1)}), bf16[8192,512]{1,0:T(8,128)(2,1)}) %all-gather.2.cloned.1.call-update) | async-done | bytes 8388624 | tf_op jit(solution)/shard_map/all_gather | solution.py:41
  136.9 5.7 %fusion.61 = (bf16[8192,256]{1,0:T(8,128)(2,1)}, bf16[8192,256]{1,0:T(8,128)(2,1)}) fusion(bf16[8192,512]{1,0:T(8,128)(2,1)} %all-gather.2.cloned.1.call-done), kind=kLoop, calls=%fused_computation.98 | loop fusion | bytes 16777216 | tf_op jit(solution)/shard_map/slice | solution.py:43
  142.6 69.3 %while.55 = (s32[]{:T(128)}, f32[128]{0:T(128)S(1)}, s32[16]{0:T(128)S(1)}, s32[]{:T(128)}, f32[]{:T(128)}, /*index=5*/f32[128]{0:T(128)S(1)}, bf16[8192,256]{1,...) while((s32[]{:T(128)}, f32[128]{0:T(128)S(1)}, ...), condition=%wide.region_11.12_spmd.clone, body=%wide.region_8.11_spmd.clone.sunk | while | flops 34407044 | bytes 598217 | solution.py:82
  213.1 5.9 %all-to-all-start.1 = ((f32[64,1,128]{2,1,0:T(1,128)}), f32[64,1,128]{2,1,0:T(1,128)S(1)}, u32[]{:S(2)}, u32[]{:S(2)}) async-start(f32[64,1,128]{2,1,0:T(1,128)} %broadcast_in_dim.121), calls=%async_computation.1 | async-start | bytes 65536 | tf_op jit(solution)/shard_map/all_to_all | solution.py:23
  219.1 7.7 %all-to-all-done.1 = f32[64,1,128]{2,1,0:T(1,128)S(1)} async-done(((f32[64,1,128]{2,1,0:T(1,128)}), f32[64,1,128]{2,1,0:T(1,128)S(1)}, u32[]{:S(2)}, u32[]{:S(2)}) %all-to-all-start.1) | async-done | bytes 32800 | tf_op jit(solution)/shard_map/all_to_all | solution.py:23
  226.8 68.8 %while.56 = (s32[]{:T(128)}, f32[128]{0:T(128)S(1)}, s32[16]{0:T(128)S(1)}, s32[]{:T(128)}, f32[8192]{0:T(1024)S(1)}, /*index=5*/f32[]{:T(128)}, f32[128]{0:T(12...) while((s32[]{:T(128)}, f32[128]{0:T(128)S(1)}, ...), condition=%wide.region_15.16_spmd.clone, body=%wide.region_12.15_spmd.clone.sunk | while | flops 34407044 | bytes 604373 | solution.py:82
  238.4 1.3 fusion.96
  247.0 1.3 fusion.96
  255.6 1.3 fusion.96
  264.2 1.3 fusion.96
  272.8 1.3 fusion.96
  281.4 1.3 fusion.96
  290.0 1.3 fusion.96
  296.9 4.7 all-to-all-start.2
  301.6 7.9 %all-to-all-done.2 = f32[64,1,128]{2,1,0:T(1,128)S(1)} async-done(((f32[64,1,128]{2,1,0:T(1,128)}), f32[64,1,128]{2,1,0:T(1,128)S(1)}, u32[]{:S(2)}, u32[]{:S(2)}) %all-to-all-start.2) | async-done | bytes 32800 | tf_op jit(solution)/shard_map/all_to_all | solution.py:23
  309.5 70.9 %while.57 = (s32[]{:T(128)}, f32[128]{0:T(128)S(1)}, s32[16]{0:T(128)S(1)}, s32[]{:T(128)}, f32[8192]{0:T(1024)S(1)}, /*index=5*/f32[]{:T(128)}, f32[128]{0:T(12...) while((s32[]{:T(128)}, f32[128]{0:T(128)S(1)}, ...), condition=%wide.region_19.20_spmd.clone, body=%wide.region_16.19_spmd.clone.sunk | while | flops 34407044 | bytes 604373 | solution.py:82
  312.7 1.3 fusion.100
  317.1 1.3 fusion.100
  321.5 1.3 fusion.100
  326.0 1.3 fusion.100
  330.4 1.3 fusion.100
  334.8 1.3 fusion.100
  339.2 1.3 fusion.100
  343.7 1.3 fusion.100
  348.1 1.3 fusion.100
  352.5 1.3 fusion.100
  357.0 1.3 fusion.100
  361.4 1.3 fusion.100
  365.8 1.3 fusion.100
  370.3 1.3 fusion.100
  374.7 1.3 fusion.100
  379.1 1.3 fusion.100
  381.6 4.7 all-to-all-start.3
  386.3 7.9 %all-to-all-done.3 = f32[64,1,128]{2,1,0:T(1,128)S(1)} async-done(((f32[64,1,128]{2,1,0:T(1,128)}), f32[64,1,128]{2,1,0:T(1,128)S(1)}, u32[]{:S(2)}, u32[]{:S(2)}) %all-to-all-start.3) | async-done | bytes 32800 | tf_op jit(solution)/shard_map/all_to_all | solution.py:23
  394.2 68.8 %while.58 = (s32[]{:T(128)}, f32[128]{0:T(128)S(1)}, s32[16]{0:T(128)S(1)}, s32[]{:T(128)}, f32[8192]{0:T(1024)S(1)}, /*index=5*/f32[]{:T(128)}, f32[128]{0:T(12...) while((s32[]{:T(128)}, f32[128]{0:T(128)S(1)}, ...), condition=%wide.region_23.24_spmd.clone, body=%wide.region_20.23_spmd.clone.sunk | while | flops 34407044 | bytes 604373 | solution.py:82
  431.6 1.3 fusion.104
  464.4 4.7 all-to-all-start.4
  470.3 6.7 %all-to-all-done.4 = f32[64,1,128]{2,1,0:T(1,128)S(1)} async-done(((f32[64,1,128]{2,1,0:T(1,128)}), f32[64,1,128]{2,1,0:T(1,128)S(1)}, u32[]{:S(2)}, u32[]{:S(2)}) %all-to-all-start.4) | async-done | bytes 32800 | tf_op jit(solution)/shard_map/all_to_all | solution.py:23
  477.0 70.8 %while.59 = (s32[]{:T(128)}, f32[128]{0:T(128)S(1)}, s32[16]{0:T(128)S(1)}, s32[]{:T(128)}, f32[8192]{0:T(1024)S(1)}, /*index=5*/f32[]{:T(128)}, f32[128]{0:T(12...) while((s32[]{:T(128)}, f32[128]{0:T(128)S(1)}, ...), condition=%wide.region_27.28_spmd.clone, body=%wide.region_24.27_spmd.clone.sunk | while | flops 34407044 | bytes 604373 | solution.py:82
  502.2 1.3 fusion.108
  (476 shorter events, 274.9 us)
Async XLA Ops:
  7.2 129.7 %all-gather.2.cloned.1.call-start = ((), (), s32[]{:S(2)}) async-start(), calls=%async_computation.5 | async-start | bytes 8519680 | tf_op jit(solution)/shard_map/all_gather | solution.py:41
  7.2 7.6 %collective-permute-start = (bf16[128,256]{1,0:T(8,128)(2,1)}, bf16[128,256]{1,0:T(8,128)(2,1)S(1)}, u32[]{:S(2)}, u32[]{:S(2)}) collective-permute-start(bf16[128,256]{1,0:T(8,128)(2,1)} %bitcast.139), channel_id=1, source_target_pairs={{1,0},{2,1},{3,2},{5,4},{6,5},{7,6},{9,8},{10,9},{11,10},{13,12},{... | collective-permute-start | bytes 196616 | tf_op jit(solution)/shard_map/ppermute | solution.py:18
  22.6 19.3 %all-to-all-start = ((f32[64,1,514]{2,1,0:T(1,128)}), f32[64,1,514]{2,1,0:T(1,128)S(1)}, u32[]{:S(2)}, u32[]{:S(2)}) async-start(f32[64,1,514]{2,1,0:T(1,128)} %broadcast_in_dim.120), calls=%async_computation | async-start | bytes 327680 | tf_op jit(solution)/shard_map/all_to_all | solution.py:23
  45.3 97.3 %copy-start = (bf16[1,128,256]{2,1,0:T(8,128)(2,1)S(1)}, bf16[1,128,256]{2,1,0:T(8,128)(2,1)}, u32[]{:S(2)}) copy-start(bf16[1,128,256]{2,1,0:T(8,128)(2,1)} %param.14) | copy-start | bytes 196612
  142.6 69.3 %copy-start.2 = (f32[1,128]{1,0:T(1,128)S(1)}, f32[1,128]{1,0:T(1,128)}, u32[]{:S(2)}) copy-start(f32[1,128]{1,0:T(1,128)} %param.16) | copy-start | bytes 1540
  213.1 13.7 %all-to-all-start.1 = ((f32[64,1,128]{2,1,0:T(1,128)}), f32[64,1,128]{2,1,0:T(1,128)S(1)}, u32[]{:S(2)}, u32[]{:S(2)}) async-start(f32[64,1,128]{2,1,0:T(1,128)} %broadcast_in_dim.121), calls=%async_computation.1 | async-start | bytes 65536 | tf_op jit(solution)/shard_map/all_to_all | solution.py:23
  296.9 12.6 %all-to-all-start.2 = ((f32[64,1,128]{2,1,0:T(1,128)}), f32[64,1,128]{2,1,0:T(1,128)S(1)}, u32[]{:S(2)}, u32[]{:S(2)}) async-start(f32[64,1,128]{2,1,0:T(1,128)} %broadcast_in_dim.122), calls=%async_computation.2 | async-start | bytes 65536 | tf_op jit(solution)/shard_map/all_to_all | solution.py:23
  381.0 166.8 %copy-start.1 = (f32[128]{0:T(128)}, f32[128]{0:T(128)S(1)}, u32[]{:S(2)}) copy-start(f32[128]{0:T(128)S(1)} %fusion.58) | copy-start | bytes 1540
  381.6 12.6 %all-to-all-start.3 = ((f32[64,1,128]{2,1,0:T(1,128)}), f32[64,1,128]{2,1,0:T(1,128)S(1)}, u32[]{:S(2)}, u32[]{:S(2)}) async-start(f32[64,1,128]{2,1,0:T(1,128)} %broadcast_in_dim.124), calls=%async_computation.3 | async-start | bytes 65536 | tf_op jit(solution)/shard_map/all_to_all | solution.py:23
  464.4 12.6 %all-to-all-start.4 = ((f32[64,1,128]{2,1,0:T(1,128)}), f32[64,1,128]{2,1,0:T(1,128)S(1)}, u32[]{:S(2)}, u32[]{:S(2)}) async-start(f32[64,1,128]{2,1,0:T(1,128)} %broadcast_in_dim.126), calls=%async_computation.4 | async-start | bytes 65536 | tf_op jit(solution)/shard_map/all_to_all | solution.py:23
Sparse Core Ops, SparseCore 0:
  16.6 120.2 all-gather.1
where the time goes:
time: 563 us; the launch traced here: 556 us
  other arithmetic  154 us (27%)
  waiting for transfers between devices  134 us (24%)
  matrix products  101 us (18%)
  local copies, waits for them, and re-layouts  63 us (11%)
  loops' own time  55.1 us (10%)
  starting transfers between devices  31.7 us (6%)
  between operations  17.6 us (3%)
    dot_general x80, matrix products, cost_tile(): lax.dot_general(row_block, columns, (((1,), (1,)), ((), ())), preferred_e...  101 us
    all_gather x1, waiting for transfers between devices, in_one_piece(): lax.all_gather(both, axis, axis=dim, tiled=True)  91.6 us
    reduce_sum x80, other arithmetic, cost_tile(): column_norms = jnp.sum(widened * widened, axis=1)  88.1 us
    another operation x5, loops' own time, accumulate(): lax.scan(advance, running, jnp.arange(shards.shape[0] // span_cols, dtype...  55.1 us
    lt x80, other arithmetic, advance(): present = leading + jnp.arange(span_cols, dtype=jnp.int32) < admitted  51.3 us
    dynamic_slice x80, local copies, waits for them, and re-layouts, accumulate(): lax.scan(advance, running, jnp.arange(shards.shape[0] // span_cols, dtype...  46.9 us
    all_to_all x5, waiting for transfers between devices, from_everyone(): return lax.all_to_all(copies, axis, split_axis=0, concat_axis=0, tiled=True)  37.8 us
    all_to_all x5, starting transfers between devices, from_everyone(): return lax.all_to_all(copies, axis, split_axis=0, concat_axis=0, tiled=True)  30.4 us
  transfers between devices with their start and end apart: 7, of which 7 were waited for; matrix products, arithmetic and copies ran while one was open for 2% of the time, Pallas kernels for 0%

commit v1 on v0

v1 whole, which is shorter than its diff:
```python
import functools
import math

import jax
import jax.numpy as jnp
from jax import lax
from jax.experimental import pallas as pl
from jax.experimental.pallas import tpu as pltpu
from jax.sharding import Mesh
from jax.sharding import PartitionSpec as P

AXES = ("x", "z", "y", "c", "g")
SIZES = (4, 2, 4, 2, 4)
ROW_AXES = ("z", "c")
COLUMN_AXES = ("x", "y")
BACK_AXES = ("z", "c", "g")

EPSILON = 0.1
PENALTY = 1.0
TAU = PENALTY / (PENALTY + EPSILON)
LOG2E = math.log2(math.e)
ABSENT = -1e30

CELLS = 128
ROW_BLOCKS = 4
COLUMN_BLOCKS = 16
ROWS = ROW_BLOCKS * CELLS
COLUMNS = COLUMN_BLOCKS * CELLS
STRIP = 64

F32 = jnp.float32


def shape(*dims, dtype=F32):
    return jax.ShapeDtypeStruct(dims, dtype)


def call(kernel, out_shape, n_inputs, scratch=(), flops=0, name=None):
    vmem = pl.BlockSpec(memory_space=pltpu.VMEM)
    return pl.pallas_call(
        kernel,
        out_shape=out_shape,
        in_specs=[pl.BlockSpec(memory_space=pltpu.SMEM)] + [vmem] * n_inputs,
        out_specs=jax.tree.map(lambda _: vmem, out_shape),
        scratch_shapes=list(scratch),
        compiler_params=pltpu.CompilerParams(vmem_limit_bytes=20 * 1024 * 1024),
        name=name,
    )


def lanes():
    return lax.broadcasted_iota(jnp.int32, (1, CELLS), 1)


def block_start(x, z, y, c):
    return (((x * 2 + z) * 4 + y) * 2 + c) * CELLS


def counts_of(counts):
    t = lax.rem(lax.axis_index("g") + 3, 4)
    return counts[t], counts[t + 1]


def row_positions(k):
    place = (lax.axis_index("z") * 2 + lax.axis_index("c")) ^ k
    return block_start(lax.axis_index("x"), place >> 1, lax.axis_index("y"), place & 1) + lanes()


def column_positions():
    block = lax.broadcasted_iota(jnp.int32, (COLUMN_BLOCKS, CELLS), 0)
    lane = lax.broadcasted_iota(jnp.int32, (COLUMN_BLOCKS, CELLS), 1)
    return block_start(block >> 2, lax.axis_index("z"), block & 3, lax.axis_index("c")) + lane


def own_start():
    return block_start(*(lax.axis_index(a) for a in ("x", "z", "y", "c")))


def local_sums(counts, features, last, growth, x_message, y_message):
    g = lax.axis_index("g")
    row = own_start() + lax.broadcasted_iota(jnp.int32, (CELLS, 1), 0)
    wide = features[0].astype(F32)
    targets = jnp.where(g == 0, last[...].astype(F32), wide)
    _, count_target = counts_of(counts)
    for cells, count, message in ((wide, counts[g], x_message), (targets, count_target, y_message)):
        present = row < count
        squares = cells * cells
        halves = squares[:, :CELLS] + squares[:, CELLS:]
        kept = jnp.where(present, cells, 0.0)
        total = jnp.sum(kept, axis=0, keepdims=True)
        message[0:1, :] = total[:, :CELLS]
        message[1:2, :] = total[:, CELLS:]
        norms = jnp.sum(halves.T, axis=0, keepdims=True)
        here = own_start() + lanes() < count
        norm_total = jnp.sum(jnp.where(here, norms, 0.0), axis=1, keepdims=True)
        message[2:3, :] = jnp.broadcast_to(norm_total, (1, CELLS))
        message[3:4, :] = growth[...] if message is x_message else norms
        message[4:8, :] = jnp.zeros((4, CELLS), F32)


def merged_sums(counts, x0, x1, x2, x3, y0, y1, y2, y3, out):
    x = x0[...] + x1[...] + x2[...] + x3[...]
    y = y0[...] + y1[...] + y2[...] + y3[...]
    row = lax.broadcasted_iota(jnp.int32, (8, CELLS), 0)
    shifted = jnp.concatenate([y[4:8], y[0:4]], axis=0)
    both = jnp.where(row < 4, x, shifted)
    both = jnp.where(row == 7, y0[3:4, :], both)
    out[...] = jnp.broadcast_to(both[None], out.shape)


def lane_sums(part, k):
    return jnp.sum(part[k * CELLS : (k + 1) * CELLS, :].T, axis=0, keepdims=True)


def first_pass(counts, moments, x0, x1, x2, x3, targets, scores, sums, rows, weights, part, limits):
    count_source, count_target = counts_of(counts)
    total = jnp.sum(moments[...], axis=0)
    n_s = count_source.astype(F32)
    n_t = count_target.astype(F32)
    products = (total[0:2] / n_s) * (total[4:6] / n_t)
    dot = jnp.sum(jnp.sum(products, axis=0, keepdims=True), axis=1, keepdims=True)
    spread = total[2:3, 0:1] / n_s + total[6:7, 0:1] / n_t - 2.0 * dot
    scale = LOG2E / (EPSILON * spread)
    for k, block in enumerate((x0, x1, x2, x3)):
        rows[k * CELLS : (k + 1) * CELLS, :] = block[0]
        wide = block[0].astype(F32)
        norms = jnp.sum(wide * wide, axis=1, keepdims=True)
        weights[k * CELLS : (k + 1) * CELLS, :] = jnp.broadcast_to(norms * scale, (CELLS, CELLS))
    part[...] = jnp.zeros_like(part)
    limits[...] = jnp.where(column_positions() < count_target, 0.0, ABSENT)
    twice = 2.0 * scale

    @pl.loop(0, COLUMN_BLOCKS // 2)
    def _(pair):
        first = pair * 2
        block = targets[pl.ds(first, 2)].reshape(2 * CELLS, 256)
        products = lax.dot_general(
            rows[...], block, (((1,), (1,)), ((), ())), preferred_element_type=F32
        )
        running = part[...]
        for half in range(2):
            norms = moments[first + half, 7:8, :] * scale
            limit = limits[pl.ds(first + half, 1), :]
            tile = (weights[...] + norms) - twice * products[:, half * CELLS : (half + 1) * CELLS]
            scores[first + half] = tile
            running = running + jnp.exp2(limit - tile)
        part[...] = running

    for k in range(ROW_BLOCKS):
        sums[k : k + 1, :] = lane_sums(part, k)


def column_pass(counts, own, p1, p2, p3, m0, m1, m2, m3, scores, alphas, out, spread_out, gathered):
    count_source, _ = counts_of(counts)
    n_s = count_source.astype(F32)
    for k, message in enumerate((m0, m1, m2, m3)):
        total = own[k : k + 1, :]
        for j, other in ((1, p1), (2, p2), (3, p3)):
            total = total + other[(k ^ j) : (k ^ j) + 1, :]
        alpha = TAU * (jnp.log(message[3:4, :] / n_s) - jnp.log(total))
        present = row_positions(k) < count_source
        alphas[k : k + 1, :] = jnp.where(present, alpha, 0.0)
        limit = jnp.where(present, alpha * LOG2E, ABSENT)
        spread_out[k * CELLS : (k + 1) * CELLS, :] = jnp.broadcast_to(limit, (CELLS, CELLS)).T

    @pl.loop(0, COLUMN_BLOCKS)
    def _(block):
        def strip(number, running):
            at = pl.ds(number * STRIP, STRIP)
            terms = jnp.exp2(spread_out[at, :] - scores[block, at, :])
            return running + jnp.sum(terms.reshape(STRIP // 8, 8, CELLS), axis=0)

        total = lax.fori_loop(0, ROWS // STRIP, strip, jnp.zeros((8, CELLS), F32), unroll=True)
        gathered[pl.ds(block, 1), :] = jnp.sum(total, axis=0, keepdims=True)

    out[...] = jnp.broadcast_to(gathered[...][None], out.shape)


def row_sums(counts, parts, scores, part, limits):
    _, count_target = counts_of(counts)
    n_t = jnp.full((1, CELLS), 1, F32) * count_target.astype(F32)
    total = jnp.sum(parts[...], axis=0)
    beta = TAU * (-jnp.log(n_t) - jnp.log(total))
    present = column_positions() < count_target
    limits[...] = jnp.where(present, beta * LOG2E, ABSENT)
    part[...] = jnp.zeros_like(part)

    @pl.loop(0, COLUMN_BLOCKS // 2)
    def _(pair):
        first = pair * 2
        terms = jnp.exp2(limits[pl.ds(first, 1), :] - scores[first])
        more = jnp.exp2(limits[pl.ds(first + 1, 1), :] - scores[first + 1])
        part[...] += terms + more

    return jnp.where(present, beta, 0.0)


def row_pass(counts, parts, scores, sums, part, limits):
    row_sums(counts, parts, scores, part, limits)
    for k in range(ROW_BLOCKS):
        sums[k : k + 1, :] = lane_sums(part, k)


def last_row_pass(counts, parts, scores, alphas, beta_out, q0, q1, q2, q3, part, limits, betas):
    betas[...] = row_sums(counts, parts, scores, part, limits)
    place = lax.axis_index("x") * 4 + lax.axis_index("y")
    beta_out[...] = betas[pl.ds(place, 1), :]
    count_source, _ = counts_of(counts)
    n_s = count_source.astype(F32)
    for k, out in enumerate((q0, q1, q2, q3)):
        mass = n_s * jnp.exp(alphas[k : k + 1, :]) * lane_sums(part, k)
        out[...] = jnp.where(row_positions(k) < count_source, mass, 0.0)


def forward(value, k):
    moves = [(d * 4 + g, (d ^ k) * 4 + (g + 1) % 4) for d in range(4) for g in range(4)]
    return lax.ppermute(value, BACK_AXES, moves)


def backward(value, k):
    moves = [(d * 4 + g, (d ^ k) * 4 + (g - 1) % 4) for d in range(4) for g in range(4)]
    return lax.ppermute(value, BACK_AXES, moves)


def across(value, k):
    return lax.ppermute(value, ROW_AXES, [(d, d ^ k) for d in range(4)])


def exchanged(copies):
    return lax.all_to_all(copies, COLUMN_AXES, split_axis=0, concat_axis=0, tiled=True)


def local(features, last_features, growth, cell_counts):
    part = pltpu.VMEM((ROWS, CELLS), F32)
    limits = pltpu.VMEM((COLUMN_BLOCKS, CELLS), F32)
    every_score = shape(COLUMN_BLOCKS, ROWS, CELLS)

    with jax.named_scope("gather"):
        targets = jnp.where(lax.axis_index("g") == 0, last_features, features[0])
        targets = exchanged(jnp.broadcast_to(targets[None], (COLUMN_BLOCKS, CELLS, 256)))
        sources = [forward(features, k) for k in range(ROW_BLOCKS)]

    with jax.named_scope("moments"):
        x_message, y_message = call(
            local_sums, (shape(8, CELLS), shape(8, CELLS)), 3, name="local_sums"
        )(cell_counts, features, last_features, growth)
        x_messages = [forward(x_message, k) for k in range(ROW_BLOCKS)]
        y_messages = [y_message] + [across(y_message, k) for k in range(1, ROW_BLOCKS)]
        moments = exchanged(
            call(merged_sums, shape(COLUMN_BLOCKS, 8, CELLS), 8, name="merged_sums")(
                cell_counts, *x_messages, *y_messages
            )
        )

    def row_exchange(sums):
        return [sums] + [across(sums, k) for k in range(1, ROW_BLOCKS)]

    columns = call(
        column_pass,
        (shape(ROW_BLOCKS, CELLS), shape(COLUMN_BLOCKS, COLUMN_BLOCKS, CELLS)),
        9,
        (part, limits),
        name="column_pass",
    )
    with jax.named_scope("first_rows"):
        scores, sums = call(
            first_pass,
            (every_score, shape(ROW_BLOCKS, CELLS)),
            6,
            (pltpu.VMEM((ROWS, 256), jnp.bfloat16), part, part, limits),
            name="first_pass",
        )(cell_counts, moments, *sources, targets)
    with jax.named_scope("first_columns"):
        _, copies = columns(cell_counts, *row_exchange(sums), *x_messages, scores)
        parts = exchanged(copies)
    with jax.named_scope("second_rows"):
        sums = call(
            row_pass, shape(ROW_BLOCKS, CELLS), 2, (part, limits), name="row_pass"
        )(cell_counts, parts, scores)
    with jax.named_scope("second_columns"):
        alphas, copies = columns(cell_counts, *row_exchange(sums), *x_messages, scores)
        source_pot = backward(alphas[0:1], 0)
        parts = exchanged(copies)
    with jax.named_scope("mass"):
        target_pot, *masses = call(
            last_row_pass,
            (shape(1, CELLS),) * 5,
            3,
            (part, limits, limits),
            name="last_row_pass",
        )(cell_counts, parts, scores, alphas)
        target_pot = backward(target_pot, 0)
        masses = [backward(mass, k) for k, mass in enumerate(masses)]
        row_mass = (masses[0] + masses[1]) + (masses[2] + masses[3])
    return source_pot, target_pot, row_mass


def solution(mesh):
    fine = Mesh(mesh.devices.reshape(SIZES), AXES)
    blk = ("x", "z", "y", "c")
    return jax.shard_map(
        local,
        mesh=fine,
        in_specs=(P("g", blk, None), P(blk, None), P("g", blk), P()),
        out_specs=(P("g", blk),) * 3,
        check_vma=False,
    )
```

time: 563 us -> 117 us (0.21); the launches traced: 556 us -> 117 us
  other arithmetic: 154 us -> 1.4 us
  waiting for transfers between devices: 134 us -> 26.9 us
  matrix products: 101 us -> 0 us
  loops' own time: 55.1 us -> 0 us
  local copies, waits for them, and re-layouts: 63 us -> 8.61 us
  starting transfers between devices: 31.7 us -> 54 us
  between operations: 17.6 us -> 0.75 us
  Pallas kernels: 0 us -> 12.5 us
  blocking collectives: 0 us -> 12.5 us
    dot_general x80 -> x0, matrix products: 101 us -> none  [cost_tile(): lax.dot_general(row_block, columns, (((1,), (1,)), ((), ())), preferred_e...]
    reduce_sum x86 -> x0, other arithmetic: 92.5 us -> none  [the longest x80 88.1 us: cost_tile(): column_norms = jnp.sum(widened * widened, axis=1)]
    all_gather x1 -> x0, waiting for transfers between devices: 91.6 us -> none  [in_one_piece(): lax.all_gather(both, axis, axis=dim, tiled=True)]
    another operation x5 -> x0, loops' own time: 55.1 us -> none  [accumulate(): lax.scan(advance, running, jnp.arange(shards.shape[0] // span_cols, dtype...]
    dynamic_slice x145 -> x0, local copies, waits for them, and re-layouts: 53.4 us -> none  [the longest x80 46.9 us: accumulate(): lax.scan(advance, running, jnp.arange(shards.shape[0] // span_cols, dtype...]
    lt x82 -> x0, other arithmetic: 52.6 us -> none  [the longest x80 51.3 us: advance(): present = leading + jnp.arange(span_cols, dtype=jnp.int32) < admitted]
    ppermute x1 -> x23, starting transfers between devices: 1.29 us -> 39.9 us  [the longest x8 18.8 us: forward(): return lax.ppermute(value, BACK_AXES, moves)]
    all_to_all x5 -> x3, waiting for transfers between devices: 37.8 us -> 9.77 us  [exchanged(): lax.all_to_all(copies, COLUMN_AXES, split_axis=0, concat_axis=0, tiled=True)]
  transfers between devices with their start and end apart: 7 -> 26, of which waited for: 7 -> 12; matrix products, arithmetic and copies ran while one was open for 2% -> 1% of each run, Pallas kernels for 0% -> 1%
where the time goes in v1:
time: 117 us
  starting transfers between devices  54 us (46%)
  waiting for transfers between devices  26.9 us (23%)
  Pallas kernels  12.5 us (11%)
  blocking collectives  12.5 us (11%)
  local copies, waits for them, and re-layouts  8.61 us (7%)
  other arithmetic  1.4 us (1%)
    ppermute x8, starting transfers between devices, forward(): return lax.ppermute(value, BACK_AXES, moves)  18.8 us
    all_to_all x3, starting transfers between devices, exchanged(): lax.all_to_all(copies, COLUMN_AXES, split_axis=0, concat_axis=0, tiled=True)  14 us
    all_to_all x1, blocking collectives, exchanged(): lax.all_to_all(copies, COLUMN_AXES, split_axis=0, concat_axis=0, tiled=True)  12.5 us
    ppermute x6, starting transfers between devices, backward(): return lax.ppermute(value, BACK_AXES, moves)  11.8 us
    ppermute x8, waiting for transfers between devices, forward(): return lax.ppermute(value, BACK_AXES, moves)  10.8 us
    all_to_all x3, waiting for transfers between devices, exchanged(): lax.all_to_all(copies, COLUMN_AXES, split_axis=0, concat_axis=0, tiled=True)  9.77 us
    ppermute x9, starting transfers between devices, across(): return lax.ppermute(value, ROW_AXES, [(d, d ^ k) for d in range(4)])  9.3 us
    unnamed x20, local copies, waits for them, and re-layouts  7.51 us
  transfers between devices with their start and end apart: 26, of which 12 were waited for; matrix products, arithmetic and copies ran while one was open for 1% of the time, Pallas kernels for 1%

profile of v1, /device:TPU:1, one launch (start us, length us, event | category | flops | bytes accessed | tf_op | source)
XLA Modules:
  0.0 116.6 jit_solution(17659627820770633807)
XLA Ops:
  0.6 0.8 copy-done.2
  1.5 0.8 copy-done.3
  2.3 0.7 copy-done.4
  3.0 0.7 copy-done.8
  3.6 0.7 local_sums.1
  4.4 5.7 %collective-permute-start.3 = (f32[8,128]{1,0:T(8,128)S(1)}, f32[8,128]{1,0:T(8,128)S(1)}, u32[]{:S(2)}, u32[]{:S(2)}) collective-permute-start(f32[8,128]{1,0:T(8,128)S(1)} %get-tuple-element.15), channel_id=1, source_target_pairs={{0,37},{1,38},{2,39},{3,36},{4,33},{5,34},{6,35},{7,32},{32,5},{33... | collective-permute-start | bytes 12296 | tf_op jit(solution)/shard_map/moments/ppermute | solution.py:217
  10.1 2.8 %collective-permute-start.2 = (f32[8,128]{1,0:T(8,128)S(1)}, f32[8,128]{1,0:T(8,128)S(1)}, u32[]{:S(2)}, u32[]{:S(2)}) collective-permute-start(f32[8,128]{1,0:T(8,128)S(1)} %get-tuple-element.15), channel_id=1, source_target_pairs={{0,33},{1,34},{2,35},{3,32},{4,37},{5,38},{6,39},{7,36},{32,1},{33... | collective-permute-start | bytes 12296 | tf_op jit(solution)/shard_map/moments/ppermute | solution.py:217
  13.0 1.2 %collective-permute-start.1 = (f32[8,128]{1,0:T(8,128)S(1)}, f32[8,128]{1,0:T(8,128)S(1)}, u32[]{:S(2)}, u32[]{:S(2)}) collective-permute-start(f32[8,128]{1,0:T(8,128)S(1)} %get-tuple-element.15), channel_id=1, source_target_pairs={{0,5},{1,6},{2,7},{3,4},{4,1},{5,2},{6,3},{7,0},{32,37},{33,38},{3... | collective-permute-start | bytes 12296 | tf_op jit(solution)/shard_map/moments/ppermute | solution.py:217
  14.2 0.8 collective-permute-start
  15.2 1.4 %collective-permute-start.5 = (f32[8,128]{1,0:T(8,128)S(1)}, f32[8,128]{1,0:T(8,128)S(1)}, u32[]{:S(2)}, u32[]{:S(2)}) collective-permute-start(f32[8,128]{1,0:T(8,128)S(1)} %get-tuple-element.16.y0), channel_id=1, source_target_pairs={{0,32},{4,36},{32,0},{36,4},{1,33},{5,37},{33,1},{37,5},{2,34},{6,... | collective-permute-start | bytes 12296 | tf_op jit(solution)/shard_map/moments/ppermute | solution.py:226
  17.1 1.0 collective-permute-done.1.x1.m1
  18.1 0.6 collective-permute-done.x0.m0
  18.7 0.6 copy-done.5
  19.4 1.2 %merged_sums.1 = f32[16,8,128]{2,1,0:T(8,128)} custom-call(s32[5]{0:T(128)S(1)} %copy-done.5, f32[8,128]{1,0:T(8,128)S(1)} %collective-permute-done.x0.m0, f32[8,128]{1,0:T(8,128)S(1)} %collective-permute-done.1.x1.m1, f32[8,128]{1,0:T(8,128)S(1)} %collective-permute-done.2.x2.m2, f32[8,128]{1,0:T(8,128)S(1)} %collective-permute-done.3.x3.m3, ...), custom_call_target="tpu_custom_call" | custom-call | tf_op jit(solution)/shard_map/moments/merged_sums/pallas_call | solution.py:250
  20.6 6.8 %all-to-all-start = ((f32[16,8,128]{2,1,0:T(8,128)}), f32[16,8,128]{2,1,0:T(8,128)S(1)}, u32[]{:S(2)}, u32[]{:S(2)}) async-start(f32[16,8,128]{2,1,0:T(8,128)} %merged_sums.1), calls=%async_computation | async-start | bytes 131072 | tf_op jit(solution)/shard_map/moments/all_to_all | solution.py:230
  27.3 0.9 bitcast_select_fusion
  28.2 5.6 %all-to-all-done.moments = f32[16,8,128]{2,1,0:T(8,128)S(1)} async-done(((f32[16,8,128]{2,1,0:T(8,128)}), f32[16,8,128]{2,1,0:T(8,128)S(1)}, u32[]{:S(2)}, u32[]{:S(2)}) %all-to-all-start) | async-done | bytes 65568 | tf_op jit(solution)/shard_map/moments/all_to_all | solution.py:230
  33.8 1.1 broadcast_in_dim.2
  34.9 3.8 %all-to-all-start.1 = ((bf16[16,128,256]{2,1,0:T(8,128)(2,1)}), bf16[16,128,256]{2,1,0:T(8,128)(2,1)S(1)}, u32[]{:S(2)}, u32[]{:S(2)}) async-start(bf16[16,128,256]{2,1,0:T(8,128)(2,1)} %broadcast_in_dim.2), calls=%async_computation.1 | async-start | bytes 2097152 | tf_op jit(solution)/shard_map/gather/all_to_all | solution.py:230
  38.7 0.8 collective-permute-start.9
  39.5 6.3 %collective-permute-start.8 = (bf16[1,128,256]{2,1,0:T(8,128)(2,1)}, bf16[1,128,256]{2,1,0:T(8,128)(2,1)S(1)}, u32[]{:S(2)}, u32[]{:S(2)}) collective-permute-start(bf16[1,128,256]{2,1,0:T(8,128)(2,1)} %features.1), channel_id=1, source_target_pairs={{0,5},{1,6},{2,7},{3,4},{4,1},{5,2},{6,3},{7,0},{32,37},{33,38},{3... | collective-permute-start | bytes 196616 | tf_op jit(solution)/shard_map/gather/ppermute | solution.py:217
  45.8 1.2 %collective-permute-start.7 = (bf16[1,128,256]{2,1,0:T(8,128)(2,1)}, bf16[1,128,256]{2,1,0:T(8,128)(2,1)S(1)}, u32[]{:S(2)}, u32[]{:S(2)}) collective-permute-start(bf16[1,128,256]{2,1,0:T(8,128)(2,1)} %features.1), channel_id=1, source_target_pairs={{0,1},{1,2},{2,3},{3,0},{4,5},{5,6},{6,7},{7,4},{32,33},{33,34},{3... | collective-permute-start | bytes 196616 | tf_op jit(solution)/shard_map/gather/ppermute | solution.py:217
  47.0 6.2 %collective-permute-done.8.x1 = bf16[1,128,256]{2,1,0:T(8,128)(2,1)S(1)} collective-permute-done((bf16[1,128,256]{2,1,0:T(8,128)(2,1)}, bf16[1,128,256]{2,1,0:T(8,128)(2,1)S(1)}, u32[]{:S(2)}, u32[]{:S(2)}) %collective-permute-start.8) | collective-permute-done | bytes 65568 | tf_op jit(solution)/shard_map/gather/ppermute | solution.py:217
  53.7 2.5 %collective-permute-done.10.x3 = bf16[1,128,256]{2,1,0:T(8,128)(2,1)S(1)} collective-permute-done((bf16[1,128,256]{2,1,0:T(8,128)(2,1)}, bf16[1,128,256]{2,1,0:T(8,128)(2,1)S(1)}, u32[]{:S(2)}, u32[]{:S(2)}) %collective-permute-start.10) | collective-permute-done | bytes 65568 | tf_op jit(solution)/shard_map/gather/ppermute | solution.py:217
  56.2 0.7 copy-done.6
  56.9 3.4 %first_pass.1 = (f32[16,512,128]{2,1,0:T(8,128)S(1)}, f32[4,128]{1,0:T(4,128)S(1)}) custom-call(s32[5]{0:T(128)S(1)} %copy-done.6, f32[16,8,128]{2,1,0:T(8,128)S(1)} %all-to-all-done.moments, bf16[1,128,256]{2,1,0:T(8,128)(2,1)S(1)} %collective-permute-done.7.x0, bf16[1,128,256]{2,1,0:T(8,128)(2,1)S(1)} %collective-permute-done.8.x1, ...), custom_call_target="tpu_custom_call" | custom-call | tf_op jit(solution)/shard_map/first_rows/first_pass/pallas_call | solution.py:266
  60.3 1.3 %collective-permute-start.13 = (f32[4,128]{1,0:T(4,128)S(1)}, f32[4,128]{1,0:T(4,128)S(1)}, u32[]{:S(2)}, u32[]{:S(2)}) collective-permute-start(f32[4,128]{1,0:T(4,128)S(1)} %get-tuple-element.17.own), channel_id=1, source_target_pairs={{0,36},{4,32},{32,4},{36,0},{1,37},{5,33},{33,5},{37,1},{2,38},{6,... | collective-permute-start | bytes 6152 | tf_op jit(solution)/shard_map/first_columns/ppermute | solution.py:226
  61.7 0.8 collective-permute-start.12
  62.6 1.2 collective-permute-done.13.p3
  64.1 2.1 %column_pass.2 = (f32[4,128]{1,0:T(4,128)}, f32[16,16,128]{2,1,0:T(8,128)S(1)}) custom-call(s32[5]{0:T(128)S(1)} %copy-done.6, f32[4,128]{1,0:T(4,128)S(1)} %get-tuple-element.17.own, f32[4,128]{1,0:T(4,128)S(1)} %collective-permute-done.11.p1, f32[4,128]{1,0:T(4,128)S(1)} %collective-permute-done.12.p2, f32[4,128]{1,0:T(4,128)S(1)} %collective-permute-done.13.p3, ...), custom_call_target="tpu_custom_call" | custom-call | tf_op jit(solution)/shard_map/first_columns/column_pass/pallas_call | solution.py:274
  66.2 12.5 %all_to_all.20.parts = f32[16,16,128]{2,1,0:T(8,128)S(1)} all-to-all(f32[16,16,128]{2,1,0:T(8,128)S(1)} %get-tuple-element.19), channel_id=1, replica_groups=mesh['x'=4,'z'=2,'y'=4,'c'=2,'g'=4] {'x','y'}, dimensions={0} | all-to-all | bytes 262144 | tf_op jit(solution)/shard_map/first_columns/all_to_all | solution.py:230
  78.7 1.4 %row_pass.1.own = f32[4,128]{1,0:T(4,128)S(1)} custom-call(s32[5]{0:T(128)S(1)} %copy-done.7, f32[16,16,128]{2,1,0:T(8,128)S(1)} %all_to_all.20.parts, f32[16,512,128]{2,1,0:T(8,128)S(1)} %get-tuple-element.18.scores), custom_call_target="tpu_custom_call" | custom-call | tf_op jit(solution)/shard_map/second_rows/row_pass/pallas_call | solution.py:277
  80.1 3.6 %collective-permute-start.16 = (f32[4,128]{1,0:T(4,128)S(1)}, f32[4,128]{1,0:T(4,128)S(1)}, u32[]{:S(2)}, u32[]{:S(2)}) collective-permute-start(f32[4,128]{1,0:T(4,128)S(1)} %row_pass.1.own), channel_id=1, source_target_pairs={{0,36},{4,32},{32,4},{36,0},{1,37},{5,33},{33,5},{37,1},{2,38},{6,... | collective-permute-start | bytes 6152 | tf_op jit(solution)/shard_map/second_columns/ppermute | solution.py:226
  83.7 1.3 %collective-permute-start.15 = (f32[4,128]{1,0:T(4,128)S(1)}, f32[4,128]{1,0:T(4,128)S(1)}, u32[]{:S(2)}, u32[]{:S(2)}) collective-permute-start(f32[4,128]{1,0:T(4,128)S(1)} %row_pass.1.own), channel_id=1, source_target_pairs={{0,32},{4,36},{32,0},{36,4},{1,33},{5,37},{33,1},{37,5},{2,34},{6,... | collective-permute-start | bytes 6152 | tf_op jit(solution)/shard_map/second_columns/ppermute | solution.py:226
  85.0 1.3 %collective-permute-done.15.p2 = f32[4,128]{1,0:T(4,128)S(1)} collective-permute-done((f32[4,128]{1,0:T(4,128)S(1)}, f32[4,128]{1,0:T(4,128)S(1)}, u32[]{:S(2)}, u32[]{:S(2)}) %collective-permute-start.15) | collective-permute-done | bytes 2080 | tf_op jit(solution)/shard_map/second_columns/ppermute | solution.py:226
  86.3 2.2 %column_pass.3 = (f32[4,128]{1,0:T(4,128)S(1)}, f32[16,16,128]{2,1,0:T(8,128)}) custom-call(s32[5]{0:T(128)S(1)} %copy-done.7, f32[4,128]{1,0:T(4,128)S(1)} %row_pass.1.own, f32[4,128]{1,0:T(4,128)S(1)} %collective-permute-done.14.p1, f32[4,128]{1,0:T(4,128)S(1)} %collective-permute-done.15.p2, f32[4,128]{1,0:T(4,128)S(1)} %collective-permute-done.16.p3, ...), custom_call_target="tpu_custom_call" | custom-call | tf_op jit(solution)/shard_map/second_columns/column_pass/pallas_call | solution.py:281
  88.5 3.5 %all-to-all-start.3 = ((f32[16,16,128]{2,1,0:T(8,128)}), f32[16,16,128]{2,1,0:T(8,128)S(1)}, u32[]{:S(2)}, u32[]{:S(2)}) async-start(f32[16,16,128]{2,1,0:T(8,128)} %get-tuple-element.21), calls=%async_computation.3 | async-start | bytes 262144 | tf_op jit(solution)/shard_map/second_columns/all_to_all | solution.py:230
  92.0 2.5 %collective-permute-start.17 = (f32[1,128]{1,0:T(1,128)S(1)}, f32[1,128]{1,0:T(1,128)S(1)}, u32[]{:S(2)}, u32[]{:S(2)}) collective-permute-start(f32[1,128]{1,0:T(1,128)S(1)} %slice.3), channel_id=1, source_target_pairs={{0,3},{1,0},{2,1},{3,2},{4,7},{5,4},{6,5},{7,6},{32,35},{33,32},{3... | collective-permute-start | bytes 1544 | tf_op jit(solution)/shard_map/second_columns/ppermute | solution.py:222
  94.5 4.1 %all-to-all-done.3.parts = f32[16,16,128]{2,1,0:T(8,128)S(1)} async-done(((f32[16,16,128]{2,1,0:T(8,128)}), f32[16,16,128]{2,1,0:T(8,128)S(1)}, u32[]{:S(2)}, u32[]{:S(2)}) %all-to-all-start.3) | async-done | bytes 131104 | tf_op jit(solution)/shard_map/second_columns/all_to_all | solution.py:230
  98.7 2.2 %copy-done.1 = f32[16,512,128]{2,1,0:T(8,128)S(1)} copy-done((f32[16,512,128]{2,1,0:T(8,128)S(1)}, f32[16,512,128]{2,1,0:T(8,128)}, u32[]{:S(2)}) %copy-start.1) | copy-done | bytes 4194328
  100.8 1.4 %last_row_pass.1 = (f32[1,128]{1,0:T(1,128)S(1)}, f32[1,128]{1,0:T(1,128)S(1)}, f32[1,128]{1,0:T(1,128)S(1)}, f32[1,128]{1,0:T(1,128)S(1)}, f32[1,128]{1,0:T(1,128)S(1)}) custom-call(s32[5]{0:T(128)S(1)} %copy-done.7, f32[16,16,128]{2,1,0:T(8,128)S(1)} %all-to-all-done.3.parts, f32[16,512,128]{2,1,0:T(8,128)S(1)} %copy-done.1, ...), custom_call_target="tpu_custom_call" | custom-call | tf_op jit(solution)/shard_map/mass/last_row_pass/pallas_call | solution.py:285
  102.3 2.5 %collective-permute-start.18 = (f32[1,128]{1,0:T(1,128)S(1)}, f32[1,128]{1,0:T(1,128)S(1)}, u32[]{:S(2)}, u32[]{:S(2)}) collective-permute-start(f32[1,128]{1,0:T(1,128)S(1)} %get-tuple-element.22), channel_id=1, source_target_pairs={{0,3},{1,0},{2,1},{3,2},{4,7},{5,4},{6,5},{7,6},{32,35},{33,32},{3... | collective-permute-start | bytes 1544 | tf_op jit(solution)/shard_map/mass/ppermute | solution.py:222
  104.7 1.0 collective-permute-start.19
  105.7 3.1 %collective-permute-start.20 = (f32[1,128]{1,0:T(1,128)S(1)}, f32[1,128]{1,0:T(1,128)S(1)}, u32[]{:S(2)}, u32[]{:S(2)}) collective-permute-start(f32[1,128]{1,0:T(1,128)S(1)} %get-tuple-element.24), channel_id=1, source_target_pairs={{0,7},{1,4},{2,5},{3,6},{4,3},{5,0},{6,1},{7,2},{32,39},{33,36},{3... | collective-permute-start | bytes 1544 | tf_op jit(solution)/shard_map/mass/ppermute | solution.py:222
  108.8 1.5 %collective-permute-start.21 = (f32[1,128]{1,0:T(1,128)S(1)}, f32[1,128]{1,0:T(1,128)S(1)}, u32[]{:S(2)}, u32[]{:S(2)}) collective-permute-start(f32[1,128]{1,0:T(1,128)S(1)} %get-tuple-element.25), channel_id=1, source_target_pairs={{0,35},{1,32},{2,33},{3,34},{4,39},{5,36},{6,37},{7,38},{32,3},{33... | collective-permute-start | bytes 1544 | tf_op jit(solution)/shard_map/mass/ppermute | solution.py:222
  110.3 1.3 %collective-permute-start.22 = (f32[1,128]{1,0:T(1,128)S(1)}, f32[1,128]{1,0:T(1,128)S(1)}, u32[]{:S(2)}, u32[]{:S(2)}) collective-permute-start(f32[1,128]{1,0:T(1,128)S(1)} %get-tuple-element.26), channel_id=1, source_target_pairs={{0,39},{1,36},{2,37},{3,38},{4,35},{5,32},{6,33},{7,34},{32,7},{33... | collective-permute-start | bytes 1544 | tf_op jit(solution)/shard_map/mass/ppermute | solution.py:222
  111.6 1.4 %collective-permute-done.21 = f32[1,128]{1,0:T(1,128)S(1)} collective-permute-done((f32[1,128]{1,0:T(1,128)S(1)}, f32[1,128]{1,0:T(1,128)S(1)}, u32[]{:S(2)}, u32[]{:S(2)}) %collective-permute-start.21) | collective-permute-done | bytes 544 | tf_op jit(solution)/shard_map/mass/ppermute | solution.py:222
  113.0 2.1 %collective-permute-done.22 = f32[1,128]{1,0:T(1,128)S(1)} collective-permute-done((f32[1,128]{1,0:T(1,128)S(1)}, f32[1,128]{1,0:T(1,128)S(1)}, u32[]{:S(2)}, u32[]{:S(2)}) %collective-permute-start.22) | collective-permute-done | bytes 544 | tf_op jit(solution)/shard_map/mass/ppermute | solution.py:222
  (36 shorter events, 3.4 us)
Async XLA Ops:
  0.6 0.8 copy-start.2
  1.5 0.8 copy-start.3
  2.3 0.7 copy-start.4
  3.0 0.7 copy-start.8
  4.4 10.9 %collective-permute-start.3 = (f32[8,128]{1,0:T(8,128)S(1)}, f32[8,128]{1,0:T(8,128)S(1)}, u32[]{:S(2)}, u32[]{:S(2)}) collective-permute-start(f32[8,128]{1,0:T(8,128)S(1)} %get-tuple-element.15), channel_id=1, source_target_pairs={{0,37},{1,38},{2,39},{3,36},{4,33},{5,34},{6,35},{7,32},{32,5},{33... | collective-permute-start | bytes 12296 | tf_op jit(solution)/shard_map/moments/ppermute | solution.py:217
  10.1 6.5 %collective-permute-start.2 = (f32[8,128]{1,0:T(8,128)S(1)}, f32[8,128]{1,0:T(8,128)S(1)}, u32[]{:S(2)}, u32[]{:S(2)}) collective-permute-start(f32[8,128]{1,0:T(8,128)S(1)} %get-tuple-element.15), channel_id=1, source_target_pairs={{0,33},{1,34},{2,35},{3,32},{4,37},{5,38},{6,39},{7,36},{32,1},{33... | collective-permute-start | bytes 12296 | tf_op jit(solution)/shard_map/moments/ppermute | solution.py:217
  13.0 5.2 %collective-permute-start.1 = (f32[8,128]{1,0:T(8,128)S(1)}, f32[8,128]{1,0:T(8,128)S(1)}, u32[]{:S(2)}, u32[]{:S(2)}) collective-permute-start(f32[8,128]{1,0:T(8,128)S(1)} %get-tuple-element.15), channel_id=1, source_target_pairs={{0,5},{1,6},{2,7},{3,4},{4,1},{5,2},{6,3},{7,0},{32,37},{33,38},{3... | collective-permute-start | bytes 12296 | tf_op jit(solution)/shard_map/moments/ppermute | solution.py:217
  14.2 4.6 %collective-permute-start = (f32[8,128]{1,0:T(8,128)S(1)}, f32[8,128]{1,0:T(8,128)S(1)}, u32[]{:S(2)}, u32[]{:S(2)}) collective-permute-start(f32[8,128]{1,0:T(8,128)S(1)} %get-tuple-element.15), channel_id=1, source_target_pairs={{0,1},{1,2},{2,3},{3,0},{4,5},{5,6},{6,7},{7,4},{32,33},{33,34},{3... | collective-permute-start | bytes 12296 | tf_op jit(solution)/shard_map/moments/ppermute | solution.py:217
  15.0 3.7 %collective-permute-start.6 = (f32[8,128]{1,0:T(8,128)S(1)}, f32[8,128]{1,0:T(8,128)S(1)}, u32[]{:S(2)}, u32[]{:S(2)}) collective-permute-start(f32[8,128]{1,0:T(8,128)S(1)} %get-tuple-element.16.y0), channel_id=1, source_target_pairs={{0,36},{4,32},{32,4},{36,0},{1,37},{5,33},{33,5},{37,1},{2,38},{6,... | collective-permute-start | bytes 12296 | tf_op jit(solution)/shard_map/moments/ppermute | solution.py:226
  15.2 3.5 %collective-permute-start.5 = (f32[8,128]{1,0:T(8,128)S(1)}, f32[8,128]{1,0:T(8,128)S(1)}, u32[]{:S(2)}, u32[]{:S(2)}) collective-permute-start(f32[8,128]{1,0:T(8,128)S(1)} %get-tuple-element.16.y0), channel_id=1, source_target_pairs={{0,32},{4,36},{32,0},{36,4},{1,33},{5,37},{33,1},{37,5},{2,34},{6,... | collective-permute-start | bytes 12296 | tf_op jit(solution)/shard_map/moments/ppermute | solution.py:226
  16.6 2.1 %collective-permute-start.4 = (f32[8,128]{1,0:T(8,128)S(1)}, f32[8,128]{1,0:T(8,128)S(1)}, u32[]{:S(2)}, u32[]{:S(2)}) collective-permute-start(f32[8,128]{1,0:T(8,128)S(1)} %get-tuple-element.16.y0), channel_id=1, source_target_pairs={{0,4},{4,0},{32,36},{36,32},{1,5},{5,1},{33,37},{37,33},{2,6},{6,2... | collective-permute-start | bytes 12296 | tf_op jit(solution)/shard_map/moments/ppermute | solution.py:226
  18.7 0.7 copy-start.5
  20.6 13.3 %all-to-all-start = ((f32[16,8,128]{2,1,0:T(8,128)}), f32[16,8,128]{2,1,0:T(8,128)S(1)}, u32[]{:S(2)}, u32[]{:S(2)}) async-start(f32[16,8,128]{2,1,0:T(8,128)} %merged_sums.1), calls=%async_computation | async-start | bytes 131072 | tf_op jit(solution)/shard_map/moments/all_to_all | solution.py:230
  34.9 43.8 %copy-start.7 = (s32[5]{0:T(128)S(1)}, s32[5]{0:T(128)}, u32[]{:S(2)}) copy-start(s32[5]{0:T(128)} %counts.13) | copy-start | bytes 64
  34.9 21.3 %all-to-all-start.1 = ((bf16[16,128,256]{2,1,0:T(8,128)(2,1)}), bf16[16,128,256]{2,1,0:T(8,128)(2,1)S(1)}, u32[]{:S(2)}, u32[]{:S(2)}) async-start(bf16[16,128,256]{2,1,0:T(8,128)(2,1)} %broadcast_in_dim.2), calls=%async_computation.1 | async-start | bytes 2097152 | tf_op jit(solution)/shard_map/gather/all_to_all | solution.py:230
  38.7 8.2 %collective-permute-start.9 = (bf16[1,128,256]{2,1,0:T(8,128)(2,1)}, bf16[1,128,256]{2,1,0:T(8,128)(2,1)S(1)}, u32[]{:S(2)}, u32[]{:S(2)}) collective-permute-start(bf16[1,128,256]{2,1,0:T(8,128)(2,1)} %features.1), channel_id=1, source_target_pairs={{0,33},{1,34},{2,35},{3,32},{4,37},{5,38},{6,39},{7,36},{32,1},{33... | collective-permute-start | bytes 196616 | tf_op jit(solution)/shard_map/gather/ppermute | solution.py:217
  39.5 13.7 %collective-permute-start.8 = (bf16[1,128,256]{2,1,0:T(8,128)(2,1)}, bf16[1,128,256]{2,1,0:T(8,128)(2,1)S(1)}, u32[]{:S(2)}, u32[]{:S(2)}) collective-permute-start(bf16[1,128,256]{2,1,0:T(8,128)(2,1)} %features.1), channel_id=1, source_target_pairs={{0,5},{1,6},{2,7},{3,4},{4,1},{5,2},{6,3},{7,0},{32,37},{33,38},{3... | collective-permute-start | bytes 196616 | tf_op jit(solution)/shard_map/gather/ppermute | solution.py:217
  45.8 7.9 %collective-permute-start.7 = (bf16[1,128,256]{2,1,0:T(8,128)(2,1)}, bf16[1,128,256]{2,1,0:T(8,128)(2,1)S(1)}, u32[]{:S(2)}, u32[]{:S(2)}) collective-permute-start(bf16[1,128,256]{2,1,0:T(8,128)(2,1)} %features.1), channel_id=1, source_target_pairs={{0,1},{1,2},{2,3},{3,0},{4,5},{5,6},{6,7},{7,4},{32,33},{33,34},{3... | collective-permute-start | bytes 196616 | tf_op jit(solution)/shard_map/gather/ppermute | solution.py:217
  47.0 9.2 %collective-permute-start.10 = (bf16[1,128,256]{2,1,0:T(8,128)(2,1)}, bf16[1,128,256]{2,1,0:T(8,128)(2,1)S(1)}, u32[]{:S(2)}, u32[]{:S(2)}) collective-permute-start(bf16[1,128,256]{2,1,0:T(8,128)(2,1)} %features.1), channel_id=1, source_target_pairs={{0,37},{1,38},{2,39},{3,36},{4,33},{5,34},{6,35},{7,32},{32,5},{33... | collective-permute-start | bytes 196616 | tf_op jit(solution)/shard_map/gather/ppermute | solution.py:217
  56.2 0.7 copy-start.6
  60.3 26.0 %copy-start = (f32[16,512,128]{2,1,0:T(8,128)}, f32[16,512,128]{2,1,0:T(8,128)S(1)}, u32[]{:S(2)}) copy-start(f32[16,512,128]{2,1,0:T(8,128)S(1)} %get-tuple-element.18.scores) | copy-start | bytes 12582916
  60.3 3.4 %collective-permute-start.13 = (f32[4,128]{1,0:T(4,128)S(1)}, f32[4,128]{1,0:T(4,128)S(1)}, u32[]{:S(2)}, u32[]{:S(2)}) collective-permute-start(f32[4,128]{1,0:T(4,128)S(1)} %get-tuple-element.17.own), channel_id=1, source_target_pairs={{0,36},{4,32},{32,4},{36,0},{1,37},{5,33},{33,5},{37,1},{2,38},{6,... | collective-permute-start | bytes 6152 | tf_op jit(solution)/shard_map/first_columns/ppermute | solution.py:226
  61.7 2.4 %collective-permute-start.12 = (f32[4,128]{1,0:T(4,128)S(1)}, f32[4,128]{1,0:T(4,128)S(1)}, u32[]{:S(2)}, u32[]{:S(2)}) collective-permute-start(f32[4,128]{1,0:T(4,128)S(1)} %get-tuple-element.17.own), channel_id=1, source_target_pairs={{0,32},{4,36},{32,0},{36,4},{1,33},{5,37},{33,1},{37,5},{2,34},{6,... | collective-permute-start | bytes 6152 | tf_op jit(solution)/shard_map/first_columns/ppermute | solution.py:226
  62.4 1.7 %collective-permute-start.11 = (f32[4,128]{1,0:T(4,128)S(1)}, f32[4,128]{1,0:T(4,128)S(1)}, u32[]{:S(2)}, u32[]{:S(2)}) collective-permute-start(f32[4,128]{1,0:T(4,128)S(1)} %get-tuple-element.17.own), channel_id=1, source_target_pairs={{0,4},{4,0},{32,36},{36,32},{1,5},{5,1},{33,37},{37,33},{2,6},{6,2... | collective-permute-start | bytes 6152 | tf_op jit(solution)/shard_map/first_columns/ppermute | solution.py:226
  80.1 4.9 %collective-permute-start.16 = (f32[4,128]{1,0:T(4,128)S(1)}, f32[4,128]{1,0:T(4,128)S(1)}, u32[]{:S(2)}, u32[]{:S(2)}) collective-permute-start(f32[4,128]{1,0:T(4,128)S(1)} %row_pass.1.own), channel_id=1, source_target_pairs={{0,36},{4,32},{32,4},{36,0},{1,37},{5,33},{33,5},{37,1},{2,38},{6,... | collective-permute-start | bytes 6152 | tf_op jit(solution)/shard_map/second_columns/ppermute | solution.py:226
  83.7 2.5 %collective-permute-start.15 = (f32[4,128]{1,0:T(4,128)S(1)}, f32[4,128]{1,0:T(4,128)S(1)}, u32[]{:S(2)}, u32[]{:S(2)}) collective-permute-start(f32[4,128]{1,0:T(4,128)S(1)} %row_pass.1.own), channel_id=1, source_target_pairs={{0,32},{4,36},{32,0},{36,4},{1,33},{5,37},{33,1},{37,5},{2,34},{6,... | collective-permute-start | bytes 6152 | tf_op jit(solution)/shard_map/second_columns/ppermute | solution.py:226
  85.0 1.3 %collective-permute-start.14 = (f32[4,128]{1,0:T(4,128)S(1)}, f32[4,128]{1,0:T(4,128)S(1)}, u32[]{:S(2)}, u32[]{:S(2)}) collective-permute-start(f32[4,128]{1,0:T(4,128)S(1)} %row_pass.1.own), channel_id=1, source_target_pairs={{0,4},{4,0},{32,36},{36,32},{1,5},{5,1},{33,37},{37,33},{2,6},{6,2... | collective-permute-start | bytes 6152 | tf_op jit(solution)/shard_map/second_columns/ppermute | solution.py:226
  88.5 10.1 %all-to-all-start.3 = ((f32[16,16,128]{2,1,0:T(8,128)}), f32[16,16,128]{2,1,0:T(8,128)S(1)}, u32[]{:S(2)}, u32[]{:S(2)}) async-start(f32[16,16,128]{2,1,0:T(8,128)} %get-tuple-element.21), calls=%async_computation.3 | async-start | bytes 262144 | tf_op jit(solution)/shard_map/second_columns/all_to_all | solution.py:230
  92.0 18.2 %collective-permute-start.17 = (f32[1,128]{1,0:T(1,128)S(1)}, f32[1,128]{1,0:T(1,128)S(1)}, u32[]{:S(2)}, u32[]{:S(2)}) collective-permute-start(f32[1,128]{1,0:T(1,128)S(1)} %slice.3), channel_id=1, source_target_pairs={{0,3},{1,0},{2,1},{3,2},{4,7},{5,4},{6,5},{7,6},{32,35},{33,32},{3... | collective-permute-start | bytes 1544 | tf_op jit(solution)/shard_map/second_columns/ppermute | solution.py:222
  98.7 2.2 %copy-start.1 = (f32[16,512,128]{2,1,0:T(8,128)S(1)}, f32[16,512,128]{2,1,0:T(8,128)}, u32[]{:S(2)}) copy-start(f32[16,512,128]{2,1,0:T(8,128)} %copy-done) | copy-start | bytes 12582916
  102.3 9.3 %collective-permute-start.18 = (f32[1,128]{1,0:T(1,128)S(1)}, f32[1,128]{1,0:T(1,128)S(1)}, u32[]{:S(2)}, u32[]{:S(2)}) collective-permute-start(f32[1,128]{1,0:T(1,128)S(1)} %get-tuple-element.22), channel_id=1, source_target_pairs={{0,3},{1,0},{2,1},{3,2},{4,7},{5,4},{6,5},{7,6},{32,35},{33,32},{3... | collective-permute-start | bytes 1544 | tf_op jit(solution)/shard_map/mass/ppermute | solution.py:222
  104.7 6.8 %collective-permute-start.19 = (f32[1,128]{1,0:T(1,128)S(1)}, f32[1,128]{1,0:T(1,128)S(1)}, u32[]{:S(2)}, u32[]{:S(2)}) collective-permute-start(f32[1,128]{1,0:T(1,128)S(1)} %get-tuple-element.23), channel_id=1, source_target_pairs={{0,3},{1,0},{2,1},{3,2},{4,7},{5,4},{6,5},{7,6},{32,35},{33,32},{3... | collective-permute-start | bytes 1544 | tf_op jit(solution)/shard_map/mass/ppermute | solution.py:222
  105.7 5.9 %collective-permute-start.20 = (f32[1,128]{1,0:T(1,128)S(1)}, f32[1,128]{1,0:T(1,128)S(1)}, u32[]{:S(2)}, u32[]{:S(2)}) collective-permute-start(f32[1,128]{1,0:T(1,128)S(1)} %get-tuple-element.24), channel_id=1, source_target_pairs={{0,7},{1,4},{2,5},{3,6},{4,3},{5,0},{6,1},{7,2},{32,39},{33,36},{3... | collective-permute-start | bytes 1544 | tf_op jit(solution)/shard_map/mass/ppermute | solution.py:222
  108.8 4.2 %collective-permute-start.21 = (f32[1,128]{1,0:T(1,128)S(1)}, f32[1,128]{1,0:T(1,128)S(1)}, u32[]{:S(2)}, u32[]{:S(2)}) collective-permute-start(f32[1,128]{1,0:T(1,128)S(1)} %get-tuple-element.25), channel_id=1, source_target_pairs={{0,35},{1,32},{2,33},{3,34},{4,39},{5,36},{6,37},{7,38},{32,3},{33... | collective-permute-start | bytes 1544 | tf_op jit(solution)/shard_map/mass/ppermute | solution.py:222
  110.3 4.8 %collective-permute-start.22 = (f32[1,128]{1,0:T(1,128)S(1)}, f32[1,128]{1,0:T(1,128)S(1)}, u32[]{:S(2)}, u32[]{:S(2)}) collective-permute-start(f32[1,128]{1,0:T(1,128)S(1)} %get-tuple-element.26), channel_id=1, source_target_pairs={{0,39},{1,36},{2,37},{3,38},{4,35},{5,32},{6,33},{7,34},{32,7},{33... | collective-permute-start | bytes 1544 | tf_op jit(solution)/shard_map/mass/ppermute | solution.py:222

commit v2 on v1

v2 whole, which is shorter than its diff:
```python
import math

import jax
import jax.numpy as jnp
from jax import lax
from jax.experimental import pallas as pl
from jax.experimental.pallas import tpu as pltpu
from jax.sharding import Mesh
from jax.sharding import PartitionSpec as P

AXES = ("x", "z", "y", "c", "g")
SIZES = (4, 2, 4, 2, 4)
ROW_AXES = ("z", "c")
COLUMN_AXES = ("x", "y")

EPSILON = 0.1
PENALTY = 1.0
TAU = PENALTY / (PENALTY + EPSILON)
LOG2E = math.log2(math.e)
ABSENT = -1e30

CELLS = 128
WIDTH = 256
ROW_BLOCKS = 4
COLUMN_BLOCKS = 16
ROWS = ROW_BLOCKS * CELLS
EXTRA = 16
STRIP = 64

COLUMNS_AT = 0
ROWS_AT = 16
N_S = 20
N_T = 21
GROWTH = 22
LAST_GROUP = 23
FRAME = 24

F32 = jnp.float32
BF16 = jnp.bfloat16


def shape(*dims, dtype=F32):
    return jax.ShapeDtypeStruct(dims, dtype)


def call(kernel, out_shape, n_inputs, scratch=(), space=pltpu.VMEM, name=None):
    return pl.pallas_call(
        kernel,
        out_shape=out_shape,
        in_specs=[pl.BlockSpec(memory_space=space)] * n_inputs,
        out_specs=jax.tree.map(lambda _: pl.BlockSpec(memory_space=pltpu.VMEM), out_shape),
        scratch_shapes=list(scratch),
        compiler_params=pltpu.CompilerParams(vmem_limit_bytes=16 * 1024 * 1024),
        name=name,
    )


def block_start(x, z, y, c):
    return (((x * 2 + z) * 4 + y) * 2 + c) * CELLS


def across_sums(cells, present):
    kept = jnp.where(present, cells, 0.0)
    total = jnp.sum(kept, axis=0, keepdims=True)
    squares = jnp.sum(kept * kept, axis=0, keepdims=True)
    norm = jnp.sum(squares, axis=1, keepdims=True)
    return total[:, :CELLS], total[:, CELLS:], jnp.broadcast_to(norm, (1, CELLS))


def local_sums(
    features, last, growth, counts, message, own_out, last_out, frame, own, final, rates, numbers, sems
):
    copies = [
        pltpu.make_async_copy(source, target, sems.at[i])
        for i, (source, target) in enumerate(
            ((features, own), (last, final), (growth, rates), (counts, numbers))
        )
    ]
    for copy in copies:
        copy.start()
    x, z, y, c, g = (lax.axis_index(a) for a in AXES)
    start = block_start(x, z, y, c)
    for copy in reversed(copies):
        copy.wait()
    count_source = numbers[g]
    count_target = numbers[g + 1]
    row = start + lax.broadcasted_iota(jnp.int32, (CELLS, 1), 0)
    pieces = [
        *across_sums(own[0].astype(F32), row < count_source),
        jnp.zeros((1, CELLS), F32),
        *across_sums(final[...].astype(F32), row < numbers[4]),
        jnp.zeros((1, CELLS), F32),
    ]
    for i, piece in enumerate(pieces):
        message[i : i + 1, :] = piece
    own_out[...] = own[0]
    last_out[...] = final[...]
    block = lax.broadcasted_iota(jnp.int32, (COLUMN_BLOCKS, CELLS), 0)
    lane = lax.broadcasted_iota(jnp.int32, (COLUMN_BLOCKS, CELLS), 1)
    target = block_start(block >> 2, z, block & 3, c) + lane
    frame[COLUMNS_AT : COLUMNS_AT + COLUMN_BLOCKS, :] = jnp.where(target < count_target, 1.0, 0.0)
    for k in range(ROW_BLOCKS):
        place = (z * 2 + c) ^ k
        source = block_start(x, place >> 1, y, place & 1) + lane[:1]
        frame[ROWS_AT + k : ROWS_AT + k + 1, :] = jnp.where(source < count_source, 1.0, 0.0)
    ones = jnp.ones((1, CELLS), F32)
    frame[N_S : N_S + 1, :] = ones * count_source.astype(F32)
    frame[N_T : N_T + 1, :] = ones * count_target.astype(F32)
    frame[GROWTH : GROWTH + 1, :] = rates[...]
    frame[LAST_GROUP : LAST_GROUP + 1, :] = ones * (g == 3).astype(F32)


def core_sums(mine, other, out):
    out[...] = mine[...] + other[...]


def three_terms(value):
    high = value.astype(BF16).astype(F32)
    rest = value - high
    middle = rest.astype(BF16).astype(F32)
    return high, middle, rest - middle


def parcel(frame, mine, across, back, back_across, shifted, last, out):
    is_last = frame[LAST_GROUP : LAST_GROUP + 1, :] > 0.0
    here = mine[...] + across[...]
    there = back[...] + back_across[...]
    wide_last = jnp.concatenate([is_last, is_last], axis=1)
    targets = jnp.where(wide_last, last[...].astype(F32), shifted[0].astype(F32))
    squares = targets * targets
    norms = jnp.sum((squares[:, :CELLS] + squares[:, CELLS:]).T, axis=0, keepdims=True)
    target_sums = jnp.where(is_last, here[4:8], there[0:4])
    extra = jnp.concatenate(
        [
            jnp.concatenate([here[0:1], here[1:2]], axis=1),
            jnp.concatenate([target_sums[0:1], target_sums[1:2]], axis=1),
            jnp.concatenate([here[2:3], target_sums[2:3]], axis=1),
            jnp.concatenate([norms, norms], axis=1),
        ],
        axis=0,
    )
    rows = jnp.concatenate([*three_terms(extra), jnp.zeros((4, WIDTH), F32)], axis=0)
    whole = jnp.concatenate([targets.astype(BF16), rows.astype(BF16)], axis=0)
    for i in range(COLUMN_BLOCKS):
        out[i] = whole


def lane_sums(part, k):
    return jnp.sum(part[k * CELLS : (k + 1) * CELLS, :].T, axis=0, keepdims=True)


def first_pass(frame, targets, x0, x1, x2, x3, scores, sums, rows, weights, part, limits, norms):
    extra = targets[:, CELLS:, :].astype(F32)
    extra = extra[:, 0:4] + extra[:, 4:8] + extra[:, 8:12]
    total = jnp.sum(extra, axis=0)
    n_s = frame[N_S : N_S + 1, :]
    n_t = frame[N_T : N_T + 1, :]
    means = total[0:1] * total[1:2]
    dot = jnp.sum(means, axis=1, keepdims=True) / n_s / n_t
    spread = total[2:3, :CELLS] / n_s + total[2:3, CELLS:] / n_t - 2.0 * dot
    scale = LOG2E / (EPSILON * spread)
    for k, block in enumerate((x0[...], x1[0], x2[0], x3[0])):
        at = slice(k * CELLS, (k + 1) * CELLS)
        rows[at, :] = block
        wide = block.astype(F32)
        weights[at, :] = jnp.sum(wide * wide, axis=1, keepdims=True) * scale
    for i in range(COLUMN_BLOCKS):
        norms[i : i + 1, :] = extra[i, 3:4, :CELLS] * scale
    part[...] = jnp.zeros_like(part)
    limits[...] = jnp.where(frame[COLUMNS_AT : COLUMNS_AT + COLUMN_BLOCKS, :] > 0.0, 0.0, ABSENT)
    twice = 2.0 * scale

    @pl.loop(0, COLUMN_BLOCKS // 2)
    def _(pair):
        first = pair * 2
        block = targets[pl.ds(first, 2), :CELLS, :].reshape(2 * CELLS, WIDTH)
        products = lax.dot_general(
            rows[...], block, (((1,), (1,)), ((), ())), preferred_element_type=F32
        )
        running = part[...]
        for half in range(2):
            at = pl.ds(first + half, 1)
            tile = (weights[...] + norms[at, :]) - twice * products[
                :, half * CELLS : (half + 1) * CELLS
            ]
            scores[first + half] = tile
            running = running + jnp.exp2(limits[at, :] - tile)
        part[...] = running

    for k in range(ROW_BLOCKS):
        sums[k : k + 1, :] = lane_sums(part, k)
    sums[4:5, :] = frame[GROWTH : GROWTH + 1, :]
    sums[5:8, :] = jnp.zeros((3, CELLS), F32)


def column_pass(frame, alpha, scores, out, spread_out, gathered):
    for k in range(ROW_BLOCKS):
        present = frame[ROWS_AT + k : ROWS_AT + k + 1, :] > 0.0
        limit = jnp.where(present, alpha[k] * LOG2E, ABSENT)
        spread_out[k * CELLS : (k + 1) * CELLS, :] = jnp.broadcast_to(limit, (CELLS, CELLS)).T

    def strip(number, running):
        at = pl.ds(pl.multiple_of(number * STRIP, STRIP), STRIP)
        limit = spread_out[at, :]
        more = []
        for i, total in enumerate(running):
            terms = jnp.exp2(limit - scores[i, at, :])
            more.append(total + jnp.sum(terms.reshape(STRIP // 8, 8, CELLS), axis=0))
        return tuple(more)

    zeros = (jnp.zeros((8, CELLS), F32),) * COLUMN_BLOCKS
    for i, total in enumerate(lax.fori_loop(0, ROWS // STRIP, strip, zeros)):
        gathered[i : i + 1, :] = jnp.sum(total, axis=0, keepdims=True)
    out[...] = jnp.broadcast_to(gathered[...][None], out.shape)


def new_alphas(frame, parts, log_p):
    alphas = []
    for k in range(ROW_BLOCKS):
        total = parts[0][k : k + 1, :]
        for j in range(1, ROW_BLOCKS):
            total = total + parts[j][(k ^ j) : (k ^ j) + 1, :]
        present = frame[ROWS_AT + k : ROWS_AT + k + 1, :] > 0.0
        alphas.append(jnp.where(present, TAU * (log_p[k] - jnp.log(total)), 0.0))
    return alphas


def first_columns(frame, p0, p1, p2, p3, scores, log_out, out, spread_out, gathered):
    n_s = frame[N_S : N_S + 1, :]
    parts = (p0, p1, p2, p3)
    log_p = [jnp.log(part[4:5, :] / n_s) for part in parts]
    for k in range(ROW_BLOCKS):
        log_out[k : k + 1, :] = log_p[k]
    column_pass(frame, new_alphas(frame, parts, log_p), scores, out, spread_out, gathered)


def last_columns(
    frame, log_p, p0, p1, p2, p3, scores, weights, alpha_out, out, spread_out, gathered
):
    n_s = frame[N_S : N_S + 1, :]
    log_rows = [log_p[k : k + 1, :] for k in range(ROW_BLOCKS)]
    alphas = new_alphas(frame, (p0, p1, p2, p3), log_rows)
    alpha_out[...] = alphas[0]
    for k in range(ROW_BLOCKS):
        present = frame[ROWS_AT + k : ROWS_AT + k + 1, :]
        weights[k : k + 1, :] = present * n_s * jnp.exp(alphas[k])
    column_pass(frame, alphas, scores, out, spread_out, gathered)


def row_pass(frame, parts, scores, part, limits):
    n_t = frame[N_T : N_T + 1, :]
    total = jnp.sum(parts[...], axis=0)
    beta = TAU * (-jnp.log(n_t) - jnp.log(total))
    present = frame[COLUMNS_AT : COLUMNS_AT + COLUMN_BLOCKS, :] > 0.0
    limits[...] = jnp.where(present, beta * LOG2E, ABSENT)

    @pl.loop(0, ROWS // STRIP)
    def _(number):
        at = pl.ds(pl.multiple_of(number * STRIP, STRIP), STRIP)
        running = jnp.exp2(limits[0:1, :] - scores[0, at, :])
        for i in range(1, COLUMN_BLOCKS):
            running = running + jnp.exp2(limits[i : i + 1, :] - scores[i, at, :])
        part[at, :] = running

    return jnp.where(present, beta, 0.0)


def second_rows(frame, parts, scores, sums, part, limits):
    row_pass(frame, parts, scores, part, limits)
    for k in range(ROW_BLOCKS):
        sums[k : k + 1, :] = lane_sums(part, k)


def last_rows(frame, parts, scores, weights, beta_out, q0, q1, q2, q3, part, limits, betas):
    betas[...] = row_pass(frame, parts, scores, part, limits)
    place = lax.axis_index("x") * 4 + lax.axis_index("y")
    beta_out[...] = betas[pl.ds(place, 1), :]
    for k, out in enumerate((q0, q1, q2, q3)):
        present = frame[ROWS_AT + k : ROWS_AT + k + 1, :] > 0.0
        out[...] = jnp.where(present, weights[k : k + 1, :] * lane_sums(part, k), 0.0)


def across(value, k):
    return lax.ppermute(value, ROW_AXES, [(d, d ^ k) for d in range(4)])


def back(value, k):
    moves = [(z * 4 + g, (z ^ k) * 4 + (g - 1) % 4) for z in range(2) for g in range(4)]
    return lax.ppermute(value, ("z", "g"), moves)


def exchanged(copies):
    return lax.all_to_all(copies, COLUMN_AXES, split_axis=0, concat_axis=0, tiled=True)


def local(features, last_features, growth, cell_counts):
    part = pltpu.VMEM((ROWS, CELLS), F32)
    limits = pltpu.VMEM((COLUMN_BLOCKS, CELLS), F32)
    some_cells = shape(CELLS, WIDTH, dtype=BF16)
    row_parts = shape(8, CELLS)
    column_parts = shape(COLUMN_BLOCKS, COLUMN_BLOCKS, CELLS)

    with jax.named_scope("moments"):
        shifted = back(features, 0)
        message, own, last, frame = call(
            local_sums,
            (row_parts, some_cells, some_cells, shape(FRAME, CELLS)),
            4,
            (
                pltpu.VMEM((1, CELLS, WIDTH), BF16),
                pltpu.VMEM((CELLS, WIDTH), BF16),
                pltpu.VMEM((1, CELLS), F32),
                pltpu.SMEM((5,), jnp.int32),
                pltpu.SemaphoreType.DMA((4,)),
            ),
            space=pltpu.HBM,
            name="local_sums",
        )(features, last_features, growth, cell_counts)
        other = lax.ppermute(message, "c", [(0, 1), (1, 0)])
        mine = call(core_sums, row_parts, 2, name="core_sums")(message, other)
        beside = lax.ppermute(mine, "z", [(0, 1), (1, 0)])
    with jax.named_scope("gather"):
        copies = call(
            parcel, shape(COLUMN_BLOCKS, CELLS + EXTRA, WIDTH, dtype=BF16), 7, name="parcel"
        )(frame, mine, beside, back(mine, 0), back(mine, 1), shifted, last)
        targets = exchanged(copies)
        sources = [own] + [across(features, k) for k in range(1, ROW_BLOCKS)]

    def row_exchange(sums):
        return [sums] + [across(sums, k) for k in range(1, ROW_BLOCKS)]

    with jax.named_scope("first_rows"):
        scores, sums = call(
            first_pass,
            (shape(COLUMN_BLOCKS, ROWS, CELLS), row_parts),
            6,
            (pltpu.VMEM((ROWS, WIDTH), BF16), part, part, limits, limits),
            name="first_pass",
        )(frame, targets, *sources)
    with jax.named_scope("first_columns"):
        log_p, copies = call(
            first_columns,
            (shape(ROW_BLOCKS, CELLS), column_parts),
            6,
            (part, limits),
            name="first_columns",
        )(frame, *row_exchange(sums), scores)
        parts = exchanged(copies)
    with jax.named_scope("second_rows"):
        sums = call(second_rows, shape(ROW_BLOCKS, CELLS), 3, (part, limits), name="second_rows")(
            frame, parts, scores
        )
    with jax.named_scope("last_columns"):
        weights, source_pot, copies = call(
            last_columns,
            (shape(ROW_BLOCKS, CELLS), shape(1, CELLS), column_parts),
            7,
            (part, limits),
            name="last_columns",
        )(frame, log_p, *row_exchange(sums), scores)
        parts = exchanged(copies)
    with jax.named_scope("mass"):
        target_pot, *masses = call(
            last_rows, (shape(1, CELLS),) * 5, 4, (part, limits, limits), name="last_rows"
        )(frame, parts, scores, weights)
        masses = [masses[0]] + [across(masses[k], k) for k in range(1, ROW_BLOCKS)]
        row_mass = (masses[0] + masses[1]) + (masses[2] + masses[3])
    return source_pot, target_pot, row_mass


def solution(mesh):
    fine = Mesh(mesh.devices.reshape(SIZES), AXES)
    blk = ("x", "z", "y", "c")
    return jax.shard_map(
        local,
        mesh=fine,
        in_specs=(P("g", blk, None), P(blk, None), P("g", blk), P()),
        out_specs=(P("g", blk),) * 3,
        check_vma=False,
    )
```

time: 117 us -> 87.6 us (0.75)
  starting transfers between devices: 54 us -> 32.3 us
  blocking collectives: 12.5 us -> 19.6 us
  local copies, waits for them, and re-layouts: 8.61 us -> 2.99 us
  waiting for transfers between devices: 26.9 us -> 22 us
  Pallas kernels: 12.5 us -> 9.06 us
    ppermute x14 -> x5, starting transfers between devices: 30.6 us -> 10.3 us  [the longest x3 8.1 us: back(): return lax.ppermute(value, ('z', 'g'), moves)]
    ppermute x14 -> x5, waiting for transfers between devices: 14.3 us -> 2.73 us  [the longest x3 1.9 us: back(): return lax.ppermute(value, ('z', 'g'), moves)]
    all_to_all x3 -> x1, starting transfers between devices: 14 us -> 6.89 us  [exchanged(): lax.all_to_all(copies, COLUMN_AXES, split_axis=0, concat_axis=0, tiled=True)]
    all_to_all x1 -> x2, blocking collectives: 12.5 us -> 19.6 us  [exchanged(): lax.all_to_all(copies, COLUMN_AXES, split_axis=0, concat_axis=0, tiled=True)]
    ppermute x9 -> x12, waiting for transfers between devices: 2.83 us -> 9.86 us  [across(): return lax.ppermute(value, ROW_AXES, [(d, d ^ k) for d in range(4)])]
    ppermute x9 -> x12, starting transfers between devices: 9.3 us -> 15.1 us  [across(): return lax.ppermute(value, ROW_AXES, [(d, d ^ k) for d in range(4)])]
    unnamed x20 -> x10, local copies, waits for them, and re-layouts: 7.51 us -> 2.99 us
    pallas_call x7 -> x8, Pallas kernels: 12.5 us -> 9.06 us  [the longest x1 2.71 us: local(): call(first_pass, (shape(COLUMN_BLOCKS, ROWS, CELLS), row_parts), 6, (pltp...]
  transfers between devices with their start and end apart: 26 -> 18, of which waited for: 12 -> 11; matrix products, arithmetic and copies ran while one was open for 1% -> 0% of each run, Pallas kernels for 1% -> 1%
where the time goes in v2:
time: 87.6 us; the launch traced here: 87.2 us
  starting transfers between devices  32.3 us (37%)
  waiting for transfers between devices  22 us (25%)
  blocking collectives  19.6 us (22%)
  Pallas kernels  9.06 us (10%)
  local copies, waits for them, and re-layouts  2.99 us (3%)
    all_to_all x2, blocking collectives, exchanged(): lax.all_to_all(copies, COLUMN_AXES, split_axis=0, concat_axis=0, tiled=True)  19.6 us
    ppermute x12, starting transfers between devices, across(): return lax.ppermute(value, ROW_AXES, [(d, d ^ k) for d in range(4)])  15.1 us
    ppermute x12, waiting for transfers between devices, across(): return lax.ppermute(value, ROW_AXES, [(d, d ^ k) for d in range(4)])  9.86 us
    all_to_all x1, waiting for transfers between devices, exchanged(): lax.all_to_all(copies, COLUMN_AXES, split_axis=0, concat_axis=0, tiled=True)  9.43 us
    ppermute x3, starting transfers between devices, back(): return lax.ppermute(value, ('z', 'g'), moves)  8.1 us
    all_to_all x1, starting transfers between devices, exchanged(): lax.all_to_all(copies, COLUMN_AXES, split_axis=0, concat_axis=0, tiled=True)  6.89 us
    unnamed x10, local copies, waits for them, and re-layouts  2.99 us
    pallas_call x1, Pallas kernels, local(): call(first_pass, (shape(COLUMN_BLOCKS, ROWS, CELLS), row_parts), 6, (pltp...  2.71 us
  transfers between devices with their start and end apart: 18, of which 11 were waited for; matrix products, arithmetic and copies ran while one was open for 0% of the time, Pallas kernels for 1%

profile of v2, /device:TPU:1, one launch (start us, length us, event | category | flops | bytes accessed | tf_op | source)
XLA Modules:
  0.0 87.2 jit_solution(4345711743581703737)
XLA Ops:
  0.6 6.9 %collective-permute-start.4 = (bf16[1,128,256]{2,1,0:T(8,128)(2,1)}, bf16[1,128,256]{2,1,0:T(8,128)(2,1)S(1)}, u32[]{:S(2)}, u32[]{:S(2)}) collective-permute-start(bf16[1,128,256]{2,1,0:T(8,128)(2,1)} %features.1), channel_id=1, source_target_pairs={{0,3},{1,0},{2,1},{3,2},{32,35},{33,32},{34,33},{35,34},{4,7},{5,4... | collective-permute-start | bytes 196616 | tf_op jit(solution)/shard_map/moments/ppermute | solution.py:289
  7.6 0.8 copy-done
  8.4 0.8 copy-done.1
  9.2 0.7 copy-done.3
  9.9 0.7 copy-done.4
  10.5 0.8 local_sums.1
  11.4 1.0 %collective-permute-start = (f32[8,128]{1,0:T(8,128)S(1)}, f32[8,128]{1,0:T(8,128)S(1)}, u32[]{:S(2)}, u32[]{:S(2)}) collective-permute-start(f32[8,128]{1,0:T(8,128)S(1)} %get-tuple-element.20.mine), channel_id=1, source_target_pairs={{0,4},{4,0},{1,5},{5,1},{2,6},{6,2},{3,7},{7,3},{8,12},{12,8},{9,1... | collective-permute-start | bytes 12296 | tf_op jit(solution)/shard_map/moments/ppermute | solution.py:319
  12.4 0.8 collective-permute-done.other
  13.3 0.7 collective-permute-start.3
  14.0 0.4 collective-permute-start.2
  14.4 1.2 %collective-permute-start.1 = (f32[8,128]{1,0:T(8,128)S(1)}, f32[8,128]{1,0:T(8,128)S(1)}, u32[]{:S(2)}, u32[]{:S(2)}) collective-permute-start(f32[8,128]{1,0:T(8,128)S(1)} %core_sums.1.mine), channel_id=1, source_target_pairs={{0,32},{32,0},{1,33},{33,1},{2,34},{34,2},{3,35},{35,3},{4,36},{36... | collective-permute-start | bytes 12296 | tf_op jit(solution)/shard_map/moments/ppermute | solution.py:321
  15.6 1.9 %collective-permute-done.3.back_across = f32[8,128]{1,0:T(8,128)S(1)} collective-permute-done((f32[8,128]{1,0:T(8,128)S(1)}, f32[8,128]{1,0:T(8,128)S(1)}, u32[]{:S(2)}, u32[]{:S(2)}) %collective-permute-start.3) | collective-permute-done | bytes 4128 | tf_op jit(solution)/shard_map/gather/ppermute | solution.py:289
  17.5 0.0 collective-permute-done.2.back
  17.5 0.0 collective-permute-done.1.across
  17.5 0.0 collective-permute-done.4.shifted
  17.5 1.2 %parcel.1 = bf16[16,144,256]{2,1,0:T(8,128)(2,1)} custom-call(f32[24,128]{1,0:T(8,128)S(1)} %get-tuple-element.19.frame, f32[8,128]{1,0:T(8,128)S(1)} %core_sums.1.mine, f32[8,128]{1,0:T(8,128)S(1)} %collective-permute-done.1.across, f32[8,128]{1,0:T(8,128)S(1)} %collective-permute-done.2.back, f32[8,128]{1,0:T(8,128)S(1)} %collective-permute-done.3.back_across, ...), custom_call_target="tpu_custom_call" | custom-call | tf_op jit(solution)/shard_map/gather/parcel/pallas_call | solution.py:323
  18.7 6.9 %all-to-all-start = ((bf16[16,144,256]{2,1,0:T(8,128)(2,1)}), bf16[16,144,256]{2,1,0:T(8,128)(2,1)S(1)}, u32[]{:S(2)}, u32[]{:S(2)}) async-start(bf16[16,144,256]{2,1,0:T(8,128)(2,1)} %parcel.1), calls=%async_computation | async-start | bytes 2359296 | tf_op jit(solution)/shard_map/gather/all_to_all | solution.py:293
  25.6 2.0 %collective-permute-start.5 = (bf16[1,128,256]{2,1,0:T(8,128)(2,1)S(1)}, bf16[1,128,256]{2,1,0:T(8,128)(2,1)S(1)}, u32[]{:S(2)}, u32[]{:S(2)}) collective-permute-start(bf16[1,128,256]{2,1,0:T(8,128)(2,1)S(1)} %copy-done.2), channel_id=1, source_target_pairs={{0,4},{4,0},{32,36},{36,32},{1,5},{5,1},{33,37},{37,33},{2,6},{6,2... | collective-permute-start | bytes 196616 | tf_op jit(solution)/shard_map/gather/ppermute | solution.py:284
  27.6 1.6 %collective-permute-start.7 = (bf16[1,128,256]{2,1,0:T(8,128)(2,1)S(1)}, bf16[1,128,256]{2,1,0:T(8,128)(2,1)S(1)}, u32[]{:S(2)}, u32[]{:S(2)}) collective-permute-start(bf16[1,128,256]{2,1,0:T(8,128)(2,1)S(1)} %copy-done.2), channel_id=1, source_target_pairs={{0,36},{4,32},{32,4},{36,0},{1,37},{5,33},{33,5},{37,1},{2,38},{6,... | collective-permute-start | bytes 196616 | tf_op jit(solution)/shard_map/gather/ppermute | solution.py:284
  29.2 0.1 collective-permute-start.6
  29.3 0.0 collective-permute-done.5.x1
  29.3 2.6 %collective-permute-done.7.x3 = bf16[1,128,256]{2,1,0:T(8,128)(2,1)S(1)} collective-permute-done((bf16[1,128,256]{2,1,0:T(8,128)(2,1)S(1)}, bf16[1,128,256]{2,1,0:T(8,128)(2,1)S(1)}, u32[]{:S(2)}, u32[]{:S(2)}) %collective-permute-start.7) | collective-permute-done | bytes 65568 | tf_op jit(solution)/shard_map/gather/ppermute | solution.py:284
  31.9 0.7 collective-permute-done.6.x2
  32.6 9.4 %all-to-all-done.targets = bf16[16,144,256]{2,1,0:T(8,128)(2,1)S(1)} async-done(((bf16[16,144,256]{2,1,0:T(8,128)(2,1)}), bf16[16,144,256]{2,1,0:T(8,128)(2,1)S(1)}, u32[]{:S(2)}, u32[]{:S(2)}) %all-to-all-start) | async-done | bytes 1179680 | tf_op jit(solution)/shard_map/gather/all_to_all | solution.py:293
  42.1 2.7 %first_pass.1 = (f32[16,512,128]{2,1,0:T(8,128)S(1)}, f32[8,128]{1,0:T(8,128)S(1)}) custom-call(f32[24,128]{1,0:T(8,128)S(1)} %get-tuple-element.19.frame, bf16[16,144,256]{2,1,0:T(8,128)(2,1)S(1)} %all-to-all-done.targets, bf16[128,256]{1,0:T(8,128)(2,1)S(1)} %get-tuple-element.22.x0, bf16[1,128,256]{2,1,0:T(8,128)(2,1)S(1)} %collective-permute-done.5.x1, ...), custom_call_target="tpu_custom_call" | custom-call | tf_op jit(solution)/shard_map/first_rows/first_pass/pallas_call | solution.py:333
  44.8 4.7 %collective-permute-start.10 = (f32[8,128]{1,0:T(8,128)S(1)}, f32[8,128]{1,0:T(8,128)S(1)}, u32[]{:S(2)}, u32[]{:S(2)}) collective-permute-start(f32[8,128]{1,0:T(8,128)S(1)} %get-tuple-element.23.p0), channel_id=1, source_target_pairs={{0,36},{4,32},{32,4},{36,0},{1,37},{5,33},{33,5},{37,1},{2,38},{6,... | collective-permute-start | bytes 12296 | tf_op jit(solution)/shard_map/first_columns/ppermute | solution.py:284
  49.5 0.2 collective-permute-start.9
  49.6 0.3 collective-permute-start.8
  50.0 1.0 %collective-permute-done.10.p3 = f32[8,128]{1,0:T(8,128)S(1)} collective-permute-done((f32[8,128]{1,0:T(8,128)S(1)}, f32[8,128]{1,0:T(8,128)S(1)}, u32[]{:S(2)}, u32[]{:S(2)}) %collective-permute-start.10) | collective-permute-done | bytes 4128 | tf_op jit(solution)/shard_map/first_columns/ppermute | solution.py:284
  50.9 1.0 %collective-permute-done.9.p2 = f32[8,128]{1,0:T(8,128)S(1)} collective-permute-done((f32[8,128]{1,0:T(8,128)S(1)}, f32[8,128]{1,0:T(8,128)S(1)}, u32[]{:S(2)}, u32[]{:S(2)}) %collective-permute-start.9) | collective-permute-done | bytes 4128 | tf_op jit(solution)/shard_map/first_columns/ppermute | solution.py:284
  51.9 0.8 first_columns.1
  52.8 9.7 %all_to_all.15.parts = f32[16,16,128]{2,1,0:T(8,128)S(1)} all-to-all(f32[16,16,128]{2,1,0:T(8,128)S(1)} %get-tuple-element.26), channel_id=1, replica_groups=mesh['x'=4,'z'=2,'y'=4,'c'=2,'g'=4] {'x','y'}, dimensions={0} | all-to-all | bytes 262144 | tf_op jit(solution)/shard_map/first_columns/all_to_all | solution.py:293
  62.5 0.9 %second_rows.1.p0 = f32[4,128]{1,0:T(4,128)S(1)} custom-call(f32[24,128]{1,0:T(8,128)S(1)} %get-tuple-element.19.frame, f32[16,16,128]{2,1,0:T(8,128)S(1)} %all_to_all.15.parts, f32[16,512,128]{2,1,0:T(8,128)S(1)} %get-tuple-element.24.scores), custom_call_target="tpu_custom_call" | custom-call | tf_op jit(solution)/shard_map/second_rows/second_rows/pallas_call | solution.py:350
  63.4 2.7 %collective-permute-start.13 = (f32[4,128]{1,0:T(4,128)S(1)}, f32[4,128]{1,0:T(4,128)S(1)}, u32[]{:S(2)}, u32[]{:S(2)}) collective-permute-start(f32[4,128]{1,0:T(4,128)S(1)} %second_rows.1.p0), channel_id=1, source_target_pairs={{0,36},{4,32},{32,4},{36,0},{1,37},{5,33},{33,5},{37,1},{2,38},{6,... | collective-permute-start | bytes 6152 | tf_op jit(solution)/shard_map/last_columns/ppermute | solution.py:284
  66.1 0.1 collective-permute-start.12
  66.3 0.3 collective-permute-start.11
  66.6 0.9 %collective-permute-done.13.p3 = f32[4,128]{1,0:T(4,128)S(1)} collective-permute-done((f32[4,128]{1,0:T(4,128)S(1)}, f32[4,128]{1,0:T(4,128)S(1)}, u32[]{:S(2)}, u32[]{:S(2)}) %collective-permute-start.13) | collective-permute-done | bytes 2080 | tf_op jit(solution)/shard_map/last_columns/ppermute | solution.py:284
  67.5 1.0 %collective-permute-done.12.p2 = f32[4,128]{1,0:T(4,128)S(1)} collective-permute-done((f32[4,128]{1,0:T(4,128)S(1)}, f32[4,128]{1,0:T(4,128)S(1)}, u32[]{:S(2)}, u32[]{:S(2)}) %collective-permute-start.12) | collective-permute-done | bytes 2080 | tf_op jit(solution)/shard_map/last_columns/ppermute | solution.py:284
  68.5 0.0 collective-permute-done.11.p1
  68.5 1.2 %last_columns.1 = (f32[4,128]{1,0:T(4,128)S(1)}, f32[1,128]{1,0:T(1,128)}, f32[16,16,128]{2,1,0:T(8,128)S(1)}) custom-call(f32[24,128]{1,0:T(8,128)S(1)} %get-tuple-element.19.frame, f32[4,128]{1,0:T(4,128)S(1)} %get-tuple-element.25.log_p, f32[4,128]{1,0:T(4,128)S(1)} %second_rows.1.p0, f32[4,128]{1,0:T(4,128)S(1)} %collective-permute-done.11.p1, ...), custom_call_target="tpu_custom_call" | custom-call | tf_op jit(solution)/shard_map/last_columns/last_columns/pallas_call | solution.py:354
  69.8 9.9 %all_to_all.16.parts = f32[16,16,128]{2,1,0:T(8,128)S(1)} all-to-all(f32[16,16,128]{2,1,0:T(8,128)S(1)} %get-tuple-element.28), channel_id=1, replica_groups=mesh['x'=4,'z'=2,'y'=4,'c'=2,'g'=4] {'x','y'}, dimensions={0} | all-to-all | bytes 262144 | tf_op jit(solution)/shard_map/last_columns/all_to_all | solution.py:293
  79.7 1.3 %last_rows.1 = (f32[1,128]{1,0:T(1,128)}, f32[1,128]{1,0:T(1,128)S(1)}, f32[1,128]{1,0:T(1,128)S(1)}, f32[1,128]{1,0:T(1,128)S(1)}, f32[1,128]{1,0:T(1,128)S(1)}) custom-call(f32[24,128]{1,0:T(8,128)S(1)} %get-tuple-element.19.frame, f32[16,16,128]{2,1,0:T(8,128)S(1)} %all_to_all.16.parts, f32[16,512,128]{2,1,0:T(8,128)S(1)} %get-tuple-element.24.scores, ...), custom_call_target="tpu_custom_call" | custom-call | tf_op jit(solution)/shard_map/mass/last_rows/pallas_call | solution.py:363
  81.0 1.5 %collective-permute-start.14 = (f32[1,128]{1,0:T(1,128)S(1)}, f32[1,128]{1,0:T(1,128)S(1)}, u32[]{:S(2)}, u32[]{:S(2)}) collective-permute-start(f32[1,128]{1,0:T(1,128)S(1)} %get-tuple-element.32), channel_id=1, source_target_pairs={{0,4},{4,0},{32,36},{36,32},{1,5},{5,1},{33,37},{37,33},{2,6},{6,2... | collective-permute-start | bytes 1544 | tf_op jit(solution)/shard_map/mass/ppermute | solution.py:284
  82.4 1.3 %collective-permute-start.15 = (f32[1,128]{1,0:T(1,128)S(1)}, f32[1,128]{1,0:T(1,128)S(1)}, u32[]{:S(2)}, u32[]{:S(2)}) collective-permute-start(f32[1,128]{1,0:T(1,128)S(1)} %get-tuple-element.33), channel_id=1, source_target_pairs={{0,32},{4,36},{32,0},{36,4},{1,33},{5,37},{33,1},{37,5},{2,34},{6,... | collective-permute-start | bytes 1544 | tf_op jit(solution)/shard_map/mass/ppermute | solution.py:284
  83.7 0.4 collective-permute-start.16
  84.1 0.8 collective-permute-done.15
  84.8 1.8 %collective-permute-done.16 = f32[1,128]{1,0:T(1,128)S(1)} collective-permute-done((f32[1,128]{1,0:T(1,128)S(1)}, f32[1,128]{1,0:T(1,128)S(1)}, u32[]{:S(2)}, u32[]{:S(2)}) %collective-permute-start.16) | collective-permute-done | bytes 544 | tf_op jit(solution)/shard_map/mass/ppermute | solution.py:284
  86.7 0.5 add_add_fusion
  (9 shorter events, 0.0 us)
Async XLA Ops:
  0.6 16.9 %collective-permute-start.4 = (bf16[1,128,256]{2,1,0:T(8,128)(2,1)}, bf16[1,128,256]{2,1,0:T(8,128)(2,1)S(1)}, u32[]{:S(2)}, u32[]{:S(2)}) collective-permute-start(bf16[1,128,256]{2,1,0:T(8,128)(2,1)} %features.1), channel_id=1, source_target_pairs={{0,3},{1,0},{2,1},{3,2},{32,35},{33,32},{34,33},{35,34},{4,7},{5,4... | collective-permute-start | bytes 196616 | tf_op jit(solution)/shard_map/moments/ppermute | solution.py:289
  7.6 0.8 copy-start
  8.4 0.8 copy-start.1
  9.2 0.7 copy-start.3
  9.9 0.7 copy-start.4
  11.4 1.9 %collective-permute-start = (f32[8,128]{1,0:T(8,128)S(1)}, f32[8,128]{1,0:T(8,128)S(1)}, u32[]{:S(2)}, u32[]{:S(2)}) collective-permute-start(f32[8,128]{1,0:T(8,128)S(1)} %get-tuple-element.20.mine), channel_id=1, source_target_pairs={{0,4},{4,0},{1,5},{5,1},{2,6},{6,2},{3,7},{7,3},{8,12},{12,8},{9,1... | collective-permute-start | bytes 12296 | tf_op jit(solution)/shard_map/moments/ppermute | solution.py:319
  13.3 4.3 %collective-permute-start.3 = (f32[8,128]{1,0:T(8,128)S(1)}, f32[8,128]{1,0:T(8,128)S(1)}, u32[]{:S(2)}, u32[]{:S(2)}) collective-permute-start(f32[8,128]{1,0:T(8,128)S(1)} %core_sums.1.mine), channel_id=1, source_target_pairs={{0,35},{1,32},{2,33},{3,34},{32,3},{33,0},{34,1},{35,2},{4,39},{5,... | collective-permute-start | bytes 12296 | tf_op jit(solution)/shard_map/gather/ppermute | solution.py:289
  14.0 3.5 %collective-permute-start.2 = (f32[8,128]{1,0:T(8,128)S(1)}, f32[8,128]{1,0:T(8,128)S(1)}, u32[]{:S(2)}, u32[]{:S(2)}) collective-permute-start(f32[8,128]{1,0:T(8,128)S(1)} %core_sums.1.mine), channel_id=1, source_target_pairs={{0,3},{1,0},{2,1},{3,2},{32,35},{33,32},{34,33},{35,34},{4,7},{5,4... | collective-permute-start | bytes 12296 | tf_op jit(solution)/shard_map/gather/ppermute | solution.py:289
  14.4 3.1 %collective-permute-start.1 = (f32[8,128]{1,0:T(8,128)S(1)}, f32[8,128]{1,0:T(8,128)S(1)}, u32[]{:S(2)}, u32[]{:S(2)}) collective-permute-start(f32[8,128]{1,0:T(8,128)S(1)} %core_sums.1.mine), channel_id=1, source_target_pairs={{0,32},{32,0},{1,33},{33,1},{2,34},{34,2},{3,35},{35,3},{4,36},{36... | collective-permute-start | bytes 12296 | tf_op jit(solution)/shard_map/moments/ppermute | solution.py:321
  18.7 6.9 %copy-start.2 = (bf16[1,128,256]{2,1,0:T(8,128)(2,1)S(1)}, bf16[1,128,256]{2,1,0:T(8,128)(2,1)}, u32[]{:S(2)}) copy-start(bf16[1,128,256]{2,1,0:T(8,128)(2,1)} %features.1) | copy-start | bytes 196612
  18.7 23.3 %all-to-all-start = ((bf16[16,144,256]{2,1,0:T(8,128)(2,1)}), bf16[16,144,256]{2,1,0:T(8,128)(2,1)S(1)}, u32[]{:S(2)}, u32[]{:S(2)}) async-start(bf16[16,144,256]{2,1,0:T(8,128)(2,1)} %parcel.1), calls=%async_computation | async-start | bytes 2359296 | tf_op jit(solution)/shard_map/gather/all_to_all | solution.py:293
  25.6 3.6 %collective-permute-start.5 = (bf16[1,128,256]{2,1,0:T(8,128)(2,1)S(1)}, bf16[1,128,256]{2,1,0:T(8,128)(2,1)S(1)}, u32[]{:S(2)}, u32[]{:S(2)}) collective-permute-start(bf16[1,128,256]{2,1,0:T(8,128)(2,1)S(1)} %copy-done.2), channel_id=1, source_target_pairs={{0,4},{4,0},{32,36},{36,32},{1,5},{5,1},{33,37},{37,33},{2,6},{6,2... | collective-permute-start | bytes 196616 | tf_op jit(solution)/shard_map/gather/ppermute | solution.py:284
  27.6 4.3 %collective-permute-start.7 = (bf16[1,128,256]{2,1,0:T(8,128)(2,1)S(1)}, bf16[1,128,256]{2,1,0:T(8,128)(2,1)S(1)}, u32[]{:S(2)}, u32[]{:S(2)}) collective-permute-start(bf16[1,128,256]{2,1,0:T(8,128)(2,1)S(1)} %copy-done.2), channel_id=1, source_target_pairs={{0,36},{4,32},{32,4},{36,0},{1,37},{5,33},{33,5},{37,1},{2,38},{6,... | collective-permute-start | bytes 196616 | tf_op jit(solution)/shard_map/gather/ppermute | solution.py:284
  29.2 3.4 %collective-permute-start.6 = (bf16[1,128,256]{2,1,0:T(8,128)(2,1)S(1)}, bf16[1,128,256]{2,1,0:T(8,128)(2,1)S(1)}, u32[]{:S(2)}, u32[]{:S(2)}) collective-permute-start(bf16[1,128,256]{2,1,0:T(8,128)(2,1)S(1)} %copy-done.2), channel_id=1, source_target_pairs={{0,32},{4,36},{32,0},{36,4},{1,33},{5,37},{33,1},{37,5},{2,34},{6,... | collective-permute-start | bytes 196616 | tf_op jit(solution)/shard_map/gather/ppermute | solution.py:284
  44.8 6.1 %collective-permute-start.10 = (f32[8,128]{1,0:T(8,128)S(1)}, f32[8,128]{1,0:T(8,128)S(1)}, u32[]{:S(2)}, u32[]{:S(2)}) collective-permute-start(f32[8,128]{1,0:T(8,128)S(1)} %get-tuple-element.23.p0), channel_id=1, source_target_pairs={{0,36},{4,32},{32,4},{36,0},{1,37},{5,33},{33,5},{37,1},{2,38},{6,... | collective-permute-start | bytes 12296 | tf_op jit(solution)/shard_map/first_columns/ppermute | solution.py:284
  49.5 2.5 %collective-permute-start.9 = (f32[8,128]{1,0:T(8,128)S(1)}, f32[8,128]{1,0:T(8,128)S(1)}, u32[]{:S(2)}, u32[]{:S(2)}) collective-permute-start(f32[8,128]{1,0:T(8,128)S(1)} %get-tuple-element.23.p0), channel_id=1, source_target_pairs={{0,32},{4,36},{32,0},{36,4},{1,33},{5,37},{33,1},{37,5},{2,34},{6,... | collective-permute-start | bytes 12296 | tf_op jit(solution)/shard_map/first_columns/ppermute | solution.py:284
  49.6 2.3 %collective-permute-start.8 = (f32[8,128]{1,0:T(8,128)S(1)}, f32[8,128]{1,0:T(8,128)S(1)}, u32[]{:S(2)}, u32[]{:S(2)}) collective-permute-start(f32[8,128]{1,0:T(8,128)S(1)} %get-tuple-element.23.p0), channel_id=1, source_target_pairs={{0,4},{4,0},{32,36},{36,32},{1,5},{5,1},{33,37},{37,33},{2,6},{6,2... | collective-permute-start | bytes 12296 | tf_op jit(solution)/shard_map/first_columns/ppermute | solution.py:284
  63.4 4.1 %collective-permute-start.13 = (f32[4,128]{1,0:T(4,128)S(1)}, f32[4,128]{1,0:T(4,128)S(1)}, u32[]{:S(2)}, u32[]{:S(2)}) collective-permute-start(f32[4,128]{1,0:T(4,128)S(1)} %second_rows.1.p0), channel_id=1, source_target_pairs={{0,36},{4,32},{32,4},{36,0},{1,37},{5,33},{33,5},{37,1},{2,38},{6,... | collective-permute-start | bytes 6152 | tf_op jit(solution)/shard_map/last_columns/ppermute | solution.py:284
  66.1 2.4 %collective-permute-start.12 = (f32[4,128]{1,0:T(4,128)S(1)}, f32[4,128]{1,0:T(4,128)S(1)}, u32[]{:S(2)}, u32[]{:S(2)}) collective-permute-start(f32[4,128]{1,0:T(4,128)S(1)} %second_rows.1.p0), channel_id=1, source_target_pairs={{0,32},{4,36},{32,0},{36,4},{1,33},{5,37},{33,1},{37,5},{2,34},{6,... | collective-permute-start | bytes 6152 | tf_op jit(solution)/shard_map/last_columns/ppermute | solution.py:284
  66.3 2.3 %collective-permute-start.11 = (f32[4,128]{1,0:T(4,128)S(1)}, f32[4,128]{1,0:T(4,128)S(1)}, u32[]{:S(2)}, u32[]{:S(2)}) collective-permute-start(f32[4,128]{1,0:T(4,128)S(1)} %second_rows.1.p0), channel_id=1, source_target_pairs={{0,4},{4,0},{32,36},{36,32},{1,5},{5,1},{33,37},{37,33},{2,6},{6,2... | collective-permute-start | bytes 6152 | tf_op jit(solution)/shard_map/last_columns/ppermute | solution.py:284
  81.0 3.1 %collective-permute-start.14 = (f32[1,128]{1,0:T(1,128)S(1)}, f32[1,128]{1,0:T(1,128)S(1)}, u32[]{:S(2)}, u32[]{:S(2)}) collective-permute-start(f32[1,128]{1,0:T(1,128)S(1)} %get-tuple-element.32), channel_id=1, source_target_pairs={{0,4},{4,0},{32,36},{36,32},{1,5},{5,1},{33,37},{37,33},{2,6},{6,2... | collective-permute-start | bytes 1544 | tf_op jit(solution)/shard_map/mass/ppermute | solution.py:284
  82.4 2.4 %collective-permute-start.15 = (f32[1,128]{1,0:T(1,128)S(1)}, f32[1,128]{1,0:T(1,128)S(1)}, u32[]{:S(2)}, u32[]{:S(2)}) collective-permute-start(f32[1,128]{1,0:T(1,128)S(1)} %get-tuple-element.33), channel_id=1, source_target_pairs={{0,32},{4,36},{32,0},{36,4},{1,33},{5,37},{33,1},{37,5},{2,34},{6,... | collective-permute-start | bytes 1544 | tf_op jit(solution)/shard_map/mass/ppermute | solution.py:284
  83.7 3.0 %collective-permute-start.16 = (f32[1,128]{1,0:T(1,128)S(1)}, f32[1,128]{1,0:T(1,128)S(1)}, u32[]{:S(2)}, u32[]{:S(2)}) collective-permute-start(f32[1,128]{1,0:T(1,128)S(1)} %get-tuple-element.34), channel_id=1, source_target_pairs={{0,36},{4,32},{32,4},{36,0},{1,37},{5,33},{33,5},{37,1},{2,38},{6,... | collective-permute-start | bytes 1544 | tf_op jit(solution)/shard_map/mass/ppermute | solution.py:284

commit v3 on v2

--- a/solution.py
+++ b/solution.py
@@ -43,11 +43,12 @@
     return jax.ShapeDtypeStruct(dims, dtype)
 
 
-def call(kernel, out_shape, n_inputs, scratch=(), space=pltpu.VMEM, name=None):
+def call(kernel, out_shape, n_inputs, scratch=(), space=pltpu.VMEM, awaited=0, name=None):
     return pl.pallas_call(
         kernel,
         out_shape=out_shape,
-        in_specs=[pl.BlockSpec(memory_space=space)] * n_inputs,
+        in_specs=[pl.BlockSpec(memory_space=space)] * n_inputs
+        + [pl.BlockSpec(memory_space=pl.ANY)] * awaited,
         out_specs=jax.tree.map(lambda _: pl.BlockSpec(memory_space=pltpu.VMEM), out_shape),
         scratch_shapes=list(scratch),
         compiler_params=pltpu.CompilerParams(vmem_limit_bytes=16 * 1024 * 1024),
@@ -110,8 +111,10 @@
     frame[LAST_GROUP : LAST_GROUP + 1, :] = ones * (g == 3).astype(F32)
 
 
-def core_sums(mine, other, out):
+def core_sums(mine, other, cells, other_cells, out, both):
     out[...] = mine[...] + other[...]
+    both[:CELLS, :] = cells[...]
+    both[CELLS:, :] = other_cells[...]
 
 
 def three_terms(value):
@@ -121,12 +124,12 @@
     return high, middle, rest - middle
 
 
-def parcel(frame, mine, across, back, back_across, shifted, last, out):
+def parcel(frame, mine, across, back, back_across, shifted, last, sources, out):
     is_last = frame[LAST_GROUP : LAST_GROUP + 1, :] > 0.0
     here = mine[...] + across[...]
     there = back[...] + back_across[...]
     wide_last = jnp.concatenate([is_last, is_last], axis=1)
-    targets = jnp.where(wide_last, last[...].astype(F32), shifted[0].astype(F32))
+    targets = jnp.where(wide_last, last[...].astype(F32), shifted[...].astype(F32))
     squares = targets * targets
     norms = jnp.sum((squares[:, :CELLS] + squares[:, CELLS:]).T, axis=0, keepdims=True)
     target_sums = jnp.where(is_last, here[4:8], there[0:4])
@@ -149,7 +152,7 @@
     return jnp.sum(part[k * CELLS : (k + 1) * CELLS, :].T, axis=0, keepdims=True)
 
 
-def first_pass(frame, targets, x0, x1, x2, x3, scores, sums, rows, weights, part, limits, norms):
+def first_pass(frame, targets, near, far, scores, sums, rows, weights, part, limits, norms):
     extra = targets[:, CELLS:, :].astype(F32)
     extra = extra[:, 0:4] + extra[:, 4:8] + extra[:, 8:12]
     total = jnp.sum(extra, axis=0)
@@ -159,8 +162,8 @@
     dot = jnp.sum(means, axis=1, keepdims=True) / n_s / n_t
     spread = total[2:3, :CELLS] / n_s + total[2:3, CELLS:] / n_t - 2.0 * dot
     scale = LOG2E / (EPSILON * spread)
-    for k, block in enumerate((x0[...], x1[0], x2[0], x3[0])):
-        at = slice(k * CELLS, (k + 1) * CELLS)
+    for k, block in enumerate((near[...], far[...])):
+        at = slice(k * 2 * CELLS, (k + 1) * 2 * CELLS)
         rows[at, :] = block
         wide = block.astype(F32)
         weights[at, :] = jnp.sum(wide * wide, axis=1, keepdims=True) * scale
@@ -280,6 +283,20 @@
         out[...] = jnp.where(present, weights[k : k + 1, :] * lane_sums(part, k), 0.0)
 
 
+def outputs(alpha, beta, q0, q1, q2, q3, alpha_out, beta_out, mass_out):
+    alpha_out[...] = alpha[...]
+    beta_out[...] = beta[...]
+    mass_out[...] = (q0[...] + q1[...]) + (q2[...] + q3[...])
+
+
+def in_hbm(array):
+    return pltpu.with_memory_space_constraint(array, pltpu.HBM)
+
+
+def swapped(value, axis):
+    return lax.ppermute(value, axis, [(0, 1), (1, 0)])
+
+
 def across(value, k):
     return lax.ppermute(value, ROW_AXES, [(d, d ^ k) for d in range(4)])
 
@@ -301,7 +318,6 @@
     column_parts = shape(COLUMN_BLOCKS, COLUMN_BLOCKS, CELLS)
 
     with jax.named_scope("moments"):
-        shifted = back(features, 0)
         message, own, last, frame = call(
             local_sums,
             (row_parts, some_cells, some_cells, shape(FRAME, CELLS)),
@@ -315,16 +331,19 @@
             ),
             space=pltpu.HBM,
             name="local_sums",
-        )(features, last_features, growth, cell_counts)
-        other = lax.ppermute(message, "c", [(0, 1), (1, 0)])
-        mine = call(core_sums, row_parts, 2, name="core_sums")(message, other)
-        beside = lax.ppermute(mine, "z", [(0, 1), (1, 0)])
+        )(*(in_hbm(a) for a in (features, last_features, growth, cell_counts)))
+        shifted = back(own, 0)
+        other = swapped(message, "c")
+        mine, near = call(
+            core_sums, (row_parts, shape(2 * CELLS, WIDTH, dtype=BF16)), 4, name="core_sums"
+        )(message, other, own, swapped(own, "c"))
     with jax.named_scope("gather"):
+        sums = (swapped(mine, "z"), back(mine, 0), back(mine, 1))
+        far = swapped(near, "z")
         copies = call(
-            parcel, shape(COLUMN_BLOCKS, CELLS + EXTRA, WIDTH, dtype=BF16), 7, name="parcel"
-        )(frame, mine, beside, back(mine, 0), back(mine, 1), shifted, last)
+            parcel, shape(COLUMN_BLOCKS, CELLS + EXTRA, WIDTH, dtype=BF16), 7, awaited=1, name="parcel"
+        )(frame, mine, *sums, shifted, last, far)
         targets = exchanged(copies)
-        sources = [own] + [across(features, k) for k in range(1, ROW_BLOCKS)]
 
     def row_exchange(sums):
         return [sums] + [across(sums, k) for k in range(1, ROW_BLOCKS)]
@@ -333,10 +352,10 @@
         scores, sums = call(
             first_pass,
             (shape(COLUMN_BLOCKS, ROWS, CELLS), row_parts),
-            6,
+            4,
             (pltpu.VMEM((ROWS, WIDTH), BF16), part, part, limits, limits),
             name="first_pass",
-        )(frame, targets, *sources)
+        )(frame, targets, near, far)
     with jax.named_scope("first_columns"):
         log_p, copies = call(
             first_columns,
@@ -364,8 +383,9 @@
             last_rows, (shape(1, CELLS),) * 5, 4, (part, limits, limits), name="last_rows"
         )(frame, parts, scores, weights)
         masses = [masses[0]] + [across(masses[k], k) for k in range(1, ROW_BLOCKS)]
-        row_mass = (masses[0] + masses[1]) + (masses[2] + masses[3])
-    return source_pot, target_pot, row_mass
+        return call(outputs, (shape(1, CELLS),) * 3, 6, name="outputs")(
+            source_pot, target_pot, *masses
+        )
 
 
 def solution(mesh):

time: 87.6 us -> 83.3 us (0.951)
  blocking collectives: 19.6 us -> 42.4 us
  waiting for transfers between devices: 22 us -> 9.16 us
  starting transfers between devices: 32.3 us -> 22.9 us
  local copies, waits for them, and re-layouts: 2.99 us -> 0 us
  Pallas kernels: 9.06 us -> 7.9 us
    all_to_all x2 -> x3, blocking collectives: 19.6 us -> 42.4 us  [exchanged(): lax.all_to_all(copies, COLUMN_AXES, split_axis=0, concat_axis=0, tiled=True)]
    all_to_all x1 -> x0, waiting for transfers between devices: 9.43 us -> none  [exchanged(): lax.all_to_all(copies, COLUMN_AXES, split_axis=0, concat_axis=0, tiled=True)]
    all_to_all x1 -> x0, starting transfers between devices: 6.89 us -> none  [exchanged(): lax.all_to_all(copies, COLUMN_AXES, split_axis=0, concat_axis=0, tiled=True)]
    ppermute x12 -> x9, waiting for transfers between devices: 9.86 us -> 6.43 us  [across(): return lax.ppermute(value, ROW_AXES, [(d, d ^ k) for d in range(4)])]
    ppermute x12 -> x9, starting transfers between devices: 15.1 us -> 11.8 us  [across(): return lax.ppermute(value, ROW_AXES, [(d, d ^ k) for d in range(4)])]
    unnamed x10 -> x0, local copies, waits for them, and re-layouts: 2.99 us -> none
    ppermute x2 -> x4, starting transfers between devices: 2.22 us -> 4.97 us  [swapped(): return lax.ppermute(value, axis, [(0, 1), (1, 0)])]
    ppermute x3, starting transfers between devices: 8.1 us -> 6.18 us  [back(): return lax.ppermute(value, ('z', 'g'), moves)]
  transfers between devices with their start and end apart: 18 -> 16, of which waited for: 11 -> 8; matrix products, arithmetic and copies ran while one was open for 0% -> 0% of each run, Pallas kernels for 1% -> 0%
where the time goes in v3:
time: 83.3 us; the launch traced here: 83.1 us
  blocking collectives  42.4 us (51%)
  starting transfers between devices  22.9 us (27%)
  waiting for transfers between devices  9.16 us (11%)
  Pallas kernels  7.9 us (9%)
    all_to_all x3, blocking collectives, exchanged(): lax.all_to_all(copies, COLUMN_AXES, split_axis=0, concat_axis=0, tiled=True)  42.4 us
    ppermute x9, starting transfers between devices, across(): return lax.ppermute(value, ROW_AXES, [(d, d ^ k) for d in range(4)])  11.8 us
    ppermute x9, waiting for transfers between devices, across(): return lax.ppermute(value, ROW_AXES, [(d, d ^ k) for d in range(4)])  6.43 us
    ppermute x3, starting transfers between devices, back(): return lax.ppermute(value, ('z', 'g'), moves)  6.18 us
    ppermute x4, starting transfers between devices, swapped(): return lax.ppermute(value, axis, [(0, 1), (1, 0)])  4.97 us
    pallas_call x1, Pallas kernels, local(): call(first_pass, (shape(COLUMN_BLOCKS, ROWS, CELLS), row_parts), 4, (pltp...  2.68 us
  transfers between devices with their start and end apart: 16, of which 8 were waited for; matrix products, arithmetic and copies ran while one was open for 0% of the time, Pallas kernels for 0%

profile of v3, /device:TPU:1, one launch (start us, length us, event | category | flops | bytes accessed | tf_op | source)
XLA Modules:
  0.0 83.1 jit_solution(14354719956823887314)
XLA Ops:
  0.6 1.0 %local_sums.1 = (f32[8,128]{1,0:T(8,128)S(1)}, bf16[128,256]{1,0:T(8,128)(2,1)S(1)}, bf16[128,256]{1,0:T(8,128)(2,1)S(1)}, f32[24,128]{1,0:T(8,128)S(1)}) custom-call(bf16[1,128,256]{2,1,0:T(8,128)(2,1)} %features.1, bf16[128,256]{1,0:T(8,128)(2,1)} %last.1, f32[1,128]{1,0:T(1,128)} %growth.1, s32[5]{0:T(128)} %counts.1), custom_call_target="tpu_custom_call" | custom-call | tf_op jit(solution)/shard_map/moments/local_sums/pallas_call | solution.py:321
  1.7 3.3 %collective-permute-start.1 = (bf16[128,256]{1,0:T(8,128)(2,1)S(1)}, bf16[128,256]{1,0:T(8,128)(2,1)S(1)}, u32[]{:S(2)}, u32[]{:S(2)}) collective-permute-start(bf16[128,256]{1,0:T(8,128)(2,1)S(1)} %get-tuple-element.23.cells), channel_id=1, source_target_pairs={{0,4},{4,0},{1,5},{5,1},{2,6},{6,2},{3,7},{7,3},{8,12},{12,8},{9,1... | collective-permute-start | bytes 196616 | tf_op jit(solution)/shard_map/moments/ppermute | solution.py:297
  5.0 0.1 collective-permute-start
  5.1 1.1 %collective-permute-done.other = f32[8,128]{1,0:T(8,128)S(1)} collective-permute-done((f32[8,128]{1,0:T(8,128)S(1)}, f32[8,128]{1,0:T(8,128)S(1)}, u32[]{:S(2)}, u32[]{:S(2)}) %collective-permute-start) | collective-permute-done | bytes 4128 | tf_op jit(solution)/shard_map/moments/ppermute | solution.py:297
  6.2 0.0 collective-permute-done.1.other_cells
  6.2 0.1 collective-permute-start.6
  6.3 5.0 %collective-permute-start.5 = (bf16[128,256]{1,0:T(8,128)(2,1)S(1)}, bf16[128,256]{1,0:T(8,128)(2,1)S(1)}, u32[]{:S(2)}, u32[]{:S(2)}) collective-permute-start(bf16[128,256]{1,0:T(8,128)(2,1)S(1)} %get-tuple-element.23.cells), channel_id=1, source_target_pairs={{0,3},{1,0},{2,1},{3,2},{32,35},{33,32},{34,33},{35,34},{4,7},{5,4... | collective-permute-start | bytes 196616 | tf_op jit(solution)/shard_map/moments/ppermute | solution.py:306
  11.3 0.7 collective-permute-start.4
  12.0 0.5 collective-permute-start.3
  12.5 1.5 %collective-permute-start.2 = (f32[8,128]{1,0:T(8,128)S(1)}, f32[8,128]{1,0:T(8,128)S(1)}, u32[]{:S(2)}, u32[]{:S(2)}) collective-permute-start(f32[8,128]{1,0:T(8,128)S(1)} %get-tuple-element.24.mine), channel_id=1, source_target_pairs={{0,32},{32,0},{1,33},{33,1},{2,34},{34,2},{3,35},{35,3},{4,36},{36... | collective-permute-start | bytes 12296 | tf_op jit(solution)/shard_map/gather/ppermute | solution.py:297
  13.9 0.0 collective-permute-done.5.shifted
  13.9 1.6 %collective-permute-done.4.back_across = f32[8,128]{1,0:T(8,128)S(1)} collective-permute-done((f32[8,128]{1,0:T(8,128)S(1)}, f32[8,128]{1,0:T(8,128)S(1)}, u32[]{:S(2)}, u32[]{:S(2)}) %collective-permute-start.4) | collective-permute-done | bytes 4128 | tf_op jit(solution)/shard_map/gather/ppermute | solution.py:306
  15.6 0.0 collective-permute-done.3.back
  15.6 0.0 collective-permute-done.2.across
  15.6 0.0 collective-permute-done.6.sources.far
  15.6 0.2 parcel.1
  15.8 22.6 %all_to_all.15.targets = bf16[16,144,256]{2,1,0:T(8,128)(2,1)S(1)} all-to-all(bf16[16,144,256]{2,1,0:T(8,128)(2,1)S(1)} %parcel.1), channel_id=1, replica_groups=mesh['x'=4,'z'=2,'y'=4,'c'=2,'g'=4] {'x','y'}, dimensions={0} | all-to-all | bytes 2359296 | tf_op jit(solution)/shard_map/gather/all_to_all | solution.py:310
  38.3 2.7 %first_pass.1 = (f32[16,512,128]{2,1,0:T(8,128)S(1)}, f32[8,128]{1,0:T(8,128)S(1)}) custom-call(f32[24,128]{1,0:T(8,128)S(1)} %get-tuple-element.21.frame, bf16[16,144,256]{2,1,0:T(8,128)(2,1)S(1)} %all_to_all.15.targets, bf16[256,256]{1,0:T(8,128)(2,1)S(1)} %get-tuple-element.26.near, bf16[256,256]{1,0:T(8,128)(2,1)S(1)} %collective-permute-done.6.sources.far), custom_call_target="tpu_custom_call" | custom-call | tf_op jit(solution)/shard_map/first_rows/first_pass/pallas_call | solution.py:352
  41.0 4.8 %collective-permute-start.9 = (f32[8,128]{1,0:T(8,128)S(1)}, f32[8,128]{1,0:T(8,128)S(1)}, u32[]{:S(2)}, u32[]{:S(2)}) collective-permute-start(f32[8,128]{1,0:T(8,128)S(1)} %get-tuple-element.27.p0), channel_id=1, source_target_pairs={{0,36},{4,32},{32,4},{36,0},{1,37},{5,33},{33,5},{37,1},{2,38},{6,... | collective-permute-start | bytes 12296 | tf_op jit(solution)/shard_map/first_columns/ppermute | solution.py:301
  45.8 0.0 collective-permute-start.8
  45.9 0.5 collective-permute-start.7
  46.3 0.8 collective-permute-done.9.p3
  47.1 1.1 %collective-permute-done.8.p2 = f32[8,128]{1,0:T(8,128)S(1)} collective-permute-done((f32[8,128]{1,0:T(8,128)S(1)}, f32[8,128]{1,0:T(8,128)S(1)}, u32[]{:S(2)}, u32[]{:S(2)}) %collective-permute-start.8) | collective-permute-done | bytes 4128 | tf_op jit(solution)/shard_map/first_columns/ppermute | solution.py:301
  48.3 0.0 collective-permute-done.7.p1
  48.3 0.8 %first_columns.1 = (f32[4,128]{1,0:T(4,128)S(1)}, f32[16,16,128]{2,1,0:T(8,128)S(1)}) custom-call(f32[24,128]{1,0:T(8,128)S(1)} %get-tuple-element.21.frame, f32[8,128]{1,0:T(8,128)S(1)} %get-tuple-element.27.p0, f32[8,128]{1,0:T(8,128)S(1)} %collective-permute-done.7.p1, f32[8,128]{1,0:T(8,128)S(1)} %collective-permute-done.8.p2, ...), custom_call_target="tpu_custom_call" | custom-call | tf_op jit(solution)/shard_map/first_columns/first_columns/pallas_call | solution.py:360
  49.1 9.9 %all_to_all.16.parts = f32[16,16,128]{2,1,0:T(8,128)S(1)} all-to-all(f32[16,16,128]{2,1,0:T(8,128)S(1)} %get-tuple-element.30), channel_id=1, replica_groups=mesh['x'=4,'z'=2,'y'=4,'c'=2,'g'=4] {'x','y'}, dimensions={0} | all-to-all | bytes 262144 | tf_op jit(solution)/shard_map/first_columns/all_to_all | solution.py:310
  59.1 0.9 %second_rows.1.p0 = f32[4,128]{1,0:T(4,128)S(1)} custom-call(f32[24,128]{1,0:T(8,128)S(1)} %get-tuple-element.21.frame, f32[16,16,128]{2,1,0:T(8,128)S(1)} %all_to_all.16.parts, f32[16,512,128]{2,1,0:T(8,128)S(1)} %get-tuple-element.28.scores), custom_call_target="tpu_custom_call" | custom-call | tf_op jit(solution)/shard_map/second_rows/second_rows/pallas_call | solution.py:369
  60.0 2.7 %collective-permute-start.12 = (f32[4,128]{1,0:T(4,128)S(1)}, f32[4,128]{1,0:T(4,128)S(1)}, u32[]{:S(2)}, u32[]{:S(2)}) collective-permute-start(f32[4,128]{1,0:T(4,128)S(1)} %second_rows.1.p0), channel_id=1, source_target_pairs={{0,36},{4,32},{32,4},{36,0},{1,37},{5,33},{33,5},{37,1},{2,38},{6,... | collective-permute-start | bytes 6152 | tf_op jit(solution)/shard_map/last_columns/ppermute | solution.py:301
  62.7 0.2 collective-permute-start.11
  62.8 0.3 collective-permute-start.10
  63.2 0.9 %collective-permute-done.12.p3 = f32[4,128]{1,0:T(4,128)S(1)} collective-permute-done((f32[4,128]{1,0:T(4,128)S(1)}, f32[4,128]{1,0:T(4,128)S(1)}, u32[]{:S(2)}, u32[]{:S(2)}) %collective-permute-start.12) | collective-permute-done | bytes 2080 | tf_op jit(solution)/shard_map/last_columns/ppermute | solution.py:301
  64.1 1.0 %collective-permute-done.11.p2 = f32[4,128]{1,0:T(4,128)S(1)} collective-permute-done((f32[4,128]{1,0:T(4,128)S(1)}, f32[4,128]{1,0:T(4,128)S(1)}, u32[]{:S(2)}, u32[]{:S(2)}) %collective-permute-start.11) | collective-permute-done | bytes 2080 | tf_op jit(solution)/shard_map/last_columns/ppermute | solution.py:301
  65.1 0.0 collective-permute-done.10.p1
  65.1 0.8 %last_columns.1 = (f32[4,128]{1,0:T(4,128)S(1)}, f32[1,128]{1,0:T(1,128)S(1)}, f32[16,16,128]{2,1,0:T(8,128)S(1)}) custom-call(f32[24,128]{1,0:T(8,128)S(1)} %get-tuple-element.21.frame, f32[4,128]{1,0:T(4,128)S(1)} %get-tuple-element.29.log_p, f32[4,128]{1,0:T(4,128)S(1)} %second_rows.1.p0, f32[4,128]{1,0:T(4,128)S(1)} %collective-permute-done.10.p1, ...), custom_call_target="tpu_custom_call" | custom-call | tf_op jit(solution)/shard_map/last_columns/last_columns/pallas_call | solution.py:373
  66.0 9.9 %all_to_all.17.parts = f32[16,16,128]{2,1,0:T(8,128)S(1)} all-to-all(f32[16,16,128]{2,1,0:T(8,128)S(1)} %get-tuple-element.32), channel_id=1, replica_groups=mesh['x'=4,'z'=2,'y'=4,'c'=2,'g'=4] {'x','y'}, dimensions={0} | all-to-all | bytes 262144 | tf_op jit(solution)/shard_map/last_columns/all_to_all | solution.py:310
  75.8 0.9 %last_rows.1 = (f32[1,128]{1,0:T(1,128)S(1)}, f32[1,128]{1,0:T(1,128)S(1)}, f32[1,128]{1,0:T(1,128)S(1)}, f32[1,128]{1,0:T(1,128)S(1)}, f32[1,128]{1,0:T(1,128)S(1)}) custom-call(f32[24,128]{1,0:T(8,128)S(1)} %get-tuple-element.21.frame, f32[16,16,128]{2,1,0:T(8,128)S(1)} %all_to_all.17.parts, f32[16,512,128]{2,1,0:T(8,128)S(1)} %get-tuple-element.28.scores, ...), custom_call_target="tpu_custom_call" | custom-call | tf_op jit(solution)/shard_map/mass/last_rows/pallas_call | solution.py:382
  76.8 1.6 %collective-permute-start.13 = (f32[1,128]{1,0:T(1,128)S(1)}, f32[1,128]{1,0:T(1,128)S(1)}, u32[]{:S(2)}, u32[]{:S(2)}) collective-permute-start(f32[1,128]{1,0:T(1,128)S(1)} %get-tuple-element.36), channel_id=1, source_target_pairs={{0,4},{4,0},{32,36},{36,32},{1,5},{5,1},{33,37},{37,33},{2,6},{6,2... | collective-permute-start | bytes 1544 | tf_op jit(solution)/shard_map/mass/ppermute | solution.py:301
  78.3 1.3 %collective-permute-start.14 = (f32[1,128]{1,0:T(1,128)S(1)}, f32[1,128]{1,0:T(1,128)S(1)}, u32[]{:S(2)}, u32[]{:S(2)}) collective-permute-start(f32[1,128]{1,0:T(1,128)S(1)} %get-tuple-element.37), channel_id=1, source_target_pairs={{0,32},{4,36},{32,0},{36,4},{1,33},{5,37},{33,1},{37,5},{2,34},{6,... | collective-permute-start | bytes 1544 | tf_op jit(solution)/shard_map/mass/ppermute | solution.py:301
  79.6 0.4 collective-permute-start.15
  80.1 0.0 collective-permute-done.13.q1
  80.1 0.7 collective-permute-done.14.q2
  80.7 1.8 %collective-permute-done.15.q3 = f32[1,128]{1,0:T(1,128)S(1)} collective-permute-done((f32[1,128]{1,0:T(1,128)S(1)}, f32[1,128]{1,0:T(1,128)S(1)}, u32[]{:S(2)}, u32[]{:S(2)}) %collective-permute-start.15) | collective-permute-done | bytes 544 | tf_op jit(solution)/shard_map/mass/ppermute | solution.py:301
  82.6 0.5 outputs.1
  (1 shorter events, 0.0 us)
Async XLA Ops:
  1.7 4.5 %collective-permute-start.1 = (bf16[128,256]{1,0:T(8,128)(2,1)S(1)}, bf16[128,256]{1,0:T(8,128)(2,1)S(1)}, u32[]{:S(2)}, u32[]{:S(2)}) collective-permute-start(bf16[128,256]{1,0:T(8,128)(2,1)S(1)} %get-tuple-element.23.cells), channel_id=1, source_target_pairs={{0,4},{4,0},{1,5},{5,1},{2,6},{6,2},{3,7},{7,3},{8,12},{12,8},{9,1... | collective-permute-start | bytes 196616 | tf_op jit(solution)/shard_map/moments/ppermute | solution.py:297
  5.0 1.2 %collective-permute-start = (f32[8,128]{1,0:T(8,128)S(1)}, f32[8,128]{1,0:T(8,128)S(1)}, u32[]{:S(2)}, u32[]{:S(2)}) collective-permute-start(f32[8,128]{1,0:T(8,128)S(1)} %get-tuple-element.22.mine), channel_id=1, source_target_pairs={{0,4},{4,0},{1,5},{5,1},{2,6},{6,2},{3,7},{7,3},{8,12},{12,8},{9,1... | collective-permute-start | bytes 12296 | tf_op jit(solution)/shard_map/moments/ppermute | solution.py:297
  6.2 9.4 %collective-permute-start.6 = (bf16[256,256]{1,0:T(8,128)(2,1)S(1)}, bf16[256,256]{1,0:T(8,128)(2,1)S(1)}, u32[]{:S(2)}, u32[]{:S(2)}) collective-permute-start(bf16[256,256]{1,0:T(8,128)(2,1)S(1)} %get-tuple-element.26.near), channel_id=1, source_target_pairs={{0,32},{32,0},{1,33},{33,1},{2,34},{34,2},{3,35},{35,3},{4,36},{36... | collective-permute-start | bytes 393224 | tf_op jit(solution)/shard_map/gather/ppermute | solution.py:297
  6.3 7.6 %collective-permute-start.5 = (bf16[128,256]{1,0:T(8,128)(2,1)S(1)}, bf16[128,256]{1,0:T(8,128)(2,1)S(1)}, u32[]{:S(2)}, u32[]{:S(2)}) collective-permute-start(bf16[128,256]{1,0:T(8,128)(2,1)S(1)} %get-tuple-element.23.cells), channel_id=1, source_target_pairs={{0,3},{1,0},{2,1},{3,2},{32,35},{33,32},{34,33},{35,34},{4,7},{5,4... | collective-permute-start | bytes 196616 | tf_op jit(solution)/shard_map/moments/ppermute | solution.py:306
  11.3 4.3 %collective-permute-start.4 = (f32[8,128]{1,0:T(8,128)S(1)}, f32[8,128]{1,0:T(8,128)S(1)}, u32[]{:S(2)}, u32[]{:S(2)}) collective-permute-start(f32[8,128]{1,0:T(8,128)S(1)} %get-tuple-element.24.mine), channel_id=1, source_target_pairs={{0,35},{1,32},{2,33},{3,34},{32,3},{33,0},{34,1},{35,2},{4,39},{5,... | collective-permute-start | bytes 12296 | tf_op jit(solution)/shard_map/gather/ppermute | solution.py:306
  12.0 3.6 %collective-permute-start.3 = (f32[8,128]{1,0:T(8,128)S(1)}, f32[8,128]{1,0:T(8,128)S(1)}, u32[]{:S(2)}, u32[]{:S(2)}) collective-permute-start(f32[8,128]{1,0:T(8,128)S(1)} %get-tuple-element.24.mine), channel_id=1, source_target_pairs={{0,3},{1,0},{2,1},{3,2},{32,35},{33,32},{34,33},{35,34},{4,7},{5,4... | collective-permute-start | bytes 12296 | tf_op jit(solution)/shard_map/gather/ppermute | solution.py:306
  12.5 3.1 %collective-permute-start.2 = (f32[8,128]{1,0:T(8,128)S(1)}, f32[8,128]{1,0:T(8,128)S(1)}, u32[]{:S(2)}, u32[]{:S(2)}) collective-permute-start(f32[8,128]{1,0:T(8,128)S(1)} %get-tuple-element.24.mine), channel_id=1, source_target_pairs={{0,32},{32,0},{1,33},{33,1},{2,34},{34,2},{3,35},{35,3},{4,36},{36... | collective-permute-start | bytes 12296 | tf_op jit(solution)/shard_map/gather/ppermute | solution.py:297
  41.0 6.1 %collective-permute-start.9 = (f32[8,128]{1,0:T(8,128)S(1)}, f32[8,128]{1,0:T(8,128)S(1)}, u32[]{:S(2)}, u32[]{:S(2)}) collective-permute-start(f32[8,128]{1,0:T(8,128)S(1)} %get-tuple-element.27.p0), channel_id=1, source_target_pairs={{0,36},{4,32},{32,4},{36,0},{1,37},{5,33},{33,5},{37,1},{2,38},{6,... | collective-permute-start | bytes 12296 | tf_op jit(solution)/shard_map/first_columns/ppermute | solution.py:301
  45.8 2.5 %collective-permute-start.8 = (f32[8,128]{1,0:T(8,128)S(1)}, f32[8,128]{1,0:T(8,128)S(1)}, u32[]{:S(2)}, u32[]{:S(2)}) collective-permute-start(f32[8,128]{1,0:T(8,128)S(1)} %get-tuple-element.27.p0), channel_id=1, source_target_pairs={{0,32},{4,36},{32,0},{36,4},{1,33},{5,37},{33,1},{37,5},{2,34},{6,... | collective-permute-start | bytes 12296 | tf_op jit(solution)/shard_map/first_columns/ppermute | solution.py:301
  45.9 2.4 %collective-permute-start.7 = (f32[8,128]{1,0:T(8,128)S(1)}, f32[8,128]{1,0:T(8,128)S(1)}, u32[]{:S(2)}, u32[]{:S(2)}) collective-permute-start(f32[8,128]{1,0:T(8,128)S(1)} %get-tuple-element.27.p0), channel_id=1, source_target_pairs={{0,4},{4,0},{32,36},{36,32},{1,5},{5,1},{33,37},{37,33},{2,6},{6,2... | collective-permute-start | bytes 12296 | tf_op jit(solution)/shard_map/first_columns/ppermute | solution.py:301
  60.0 4.1 %collective-permute-start.12 = (f32[4,128]{1,0:T(4,128)S(1)}, f32[4,128]{1,0:T(4,128)S(1)}, u32[]{:S(2)}, u32[]{:S(2)}) collective-permute-start(f32[4,128]{1,0:T(4,128)S(1)} %second_rows.1.p0), channel_id=1, source_target_pairs={{0,36},{4,32},{32,4},{36,0},{1,37},{5,33},{33,5},{37,1},{2,38},{6,... | collective-permute-start | bytes 6152 | tf_op jit(solution)/shard_map/last_columns/ppermute | solution.py:301
  62.7 2.4 %collective-permute-start.11 = (f32[4,128]{1,0:T(4,128)S(1)}, f32[4,128]{1,0:T(4,128)S(1)}, u32[]{:S(2)}, u32[]{:S(2)}) collective-permute-start(f32[4,128]{1,0:T(4,128)S(1)} %second_rows.1.p0), channel_id=1, source_target_pairs={{0,32},{4,36},{32,0},{36,4},{1,33},{5,37},{33,1},{37,5},{2,34},{6,... | collective-permute-start | bytes 6152 | tf_op jit(solution)/shard_map/last_columns/ppermute | solution.py:301
  62.8 2.3 %collective-permute-start.10 = (f32[4,128]{1,0:T(4,128)S(1)}, f32[4,128]{1,0:T(4,128)S(1)}, u32[]{:S(2)}, u32[]{:S(2)}) collective-permute-start(f32[4,128]{1,0:T(4,128)S(1)} %second_rows.1.p0), channel_id=1, source_target_pairs={{0,4},{4,0},{32,36},{36,32},{1,5},{5,1},{33,37},{37,33},{2,6},{6,2... | collective-permute-start | bytes 6152 | tf_op jit(solution)/shard_map/last_columns/ppermute | solution.py:301
  76.8 3.3 %collective-permute-start.13 = (f32[1,128]{1,0:T(1,128)S(1)}, f32[1,128]{1,0:T(1,128)S(1)}, u32[]{:S(2)}, u32[]{:S(2)}) collective-permute-start(f32[1,128]{1,0:T(1,128)S(1)} %get-tuple-element.36), channel_id=1, source_target_pairs={{0,4},{4,0},{32,36},{36,32},{1,5},{5,1},{33,37},{37,33},{2,6},{6,2... | collective-permute-start | bytes 1544 | tf_op jit(solution)/shard_map/mass/ppermute | solution.py:301
  78.3 2.4 %collective-permute-start.14 = (f32[1,128]{1,0:T(1,128)S(1)}, f32[1,128]{1,0:T(1,128)S(1)}, u32[]{:S(2)}, u32[]{:S(2)}) collective-permute-start(f32[1,128]{1,0:T(1,128)S(1)} %get-tuple-element.37), channel_id=1, source_target_pairs={{0,32},{4,36},{32,0},{36,4},{1,33},{5,37},{33,1},{37,5},{2,34},{6,... | collective-permute-start | bytes 1544 | tf_op jit(solution)/shard_map/mass/ppermute | solution.py:301
  79.6 3.0 %collective-permute-start.15 = (f32[1,128]{1,0:T(1,128)S(1)}, f32[1,128]{1,0:T(1,128)S(1)}, u32[]{:S(2)}, u32[]{:S(2)}) collective-permute-start(f32[1,128]{1,0:T(1,128)S(1)} %get-tuple-element.38), channel_id=1, source_target_pairs={{0,36},{4,32},{32,4},{36,0},{1,37},{5,33},{33,5},{37,1},{2,38},{6,... | collective-permute-start | bytes 1544 | tf_op jit(solution)/shard_map/mass/ppermute | solution.py:301

commit v4 on v3

--- a/solution.py
+++ b/solution.py
@@ -24,7 +24,6 @@
 ROW_BLOCKS = 4
 COLUMN_BLOCKS = 16
 ROWS = ROW_BLOCKS * CELLS
-EXTRA = 16
 STRIP = 64
 
 COLUMNS_AT = 0
@@ -43,12 +42,11 @@
     return jax.ShapeDtypeStruct(dims, dtype)
 
 
-def call(kernel, out_shape, n_inputs, scratch=(), space=pltpu.VMEM, awaited=0, name=None):
+def call(kernel, out_shape, n_inputs, scratch=(), space=pltpu.VMEM, name=None):
     return pl.pallas_call(
         kernel,
         out_shape=out_shape,
-        in_specs=[pl.BlockSpec(memory_space=space)] * n_inputs
-        + [pl.BlockSpec(memory_space=pl.ANY)] * awaited,
+        in_specs=[pl.BlockSpec(memory_space=space)] * n_inputs,
         out_specs=jax.tree.map(lambda _: pl.BlockSpec(memory_space=pltpu.VMEM), out_shape),
         scratch_shapes=list(scratch),
         compiler_params=pltpu.CompilerParams(vmem_limit_bytes=16 * 1024 * 1024),
@@ -60,40 +58,37 @@
     return (((x * 2 + z) * 4 + y) * 2 + c) * CELLS
 
 
-def across_sums(cells, present):
+def own_sums(cells, present):
     kept = jnp.where(present, cells, 0.0)
     total = jnp.sum(kept, axis=0, keepdims=True)
-    squares = jnp.sum(kept * kept, axis=0, keepdims=True)
-    norm = jnp.sum(squares, axis=1, keepdims=True)
-    return total[:, :CELLS], total[:, CELLS:], jnp.broadcast_to(norm, (1, CELLS))
+    squares = kept * kept
+    norm = jnp.sum(jnp.sum(squares, axis=0, keepdims=True), axis=1, keepdims=True)
+    squares = cells * cells
+    norms = jnp.sum((squares[:, :CELLS] + squares[:, CELLS:]).T, axis=0, keepdims=True)
+    return total[:, :CELLS], total[:, CELLS:], jnp.broadcast_to(norm, (1, CELLS)), norms
 
 
 def local_sums(
-    features, last, growth, counts, message, own_out, last_out, frame, own, final, rates, numbers, sems
+    features, last, growth, counts, copies, own_out, last_out, frame, own, final, rates, numbers, sems
 ):
-    copies = [
+    loads = [
         pltpu.make_async_copy(source, target, sems.at[i])
         for i, (source, target) in enumerate(
             ((features, own), (last, final), (growth, rates), (counts, numbers))
         )
     ]
-    for copy in copies:
-        copy.start()
+    for load in loads:
+        load.start()
     x, z, y, c, g = (lax.axis_index(a) for a in AXES)
     start = block_start(x, z, y, c)
-    for copy in reversed(copies):
-        copy.wait()
+    for load in reversed(loads):
+        load.wait()
     count_source = numbers[g]
     count_target = numbers[g + 1]
     row = start + lax.broadcasted_iota(jnp.int32, (CELLS, 1), 0)
-    pieces = [
-        *across_sums(own[0].astype(F32), row < count_source),
-        jnp.zeros((1, CELLS), F32),
-        *across_sums(final[...].astype(F32), row < numbers[4]),
-        jnp.zeros((1, CELLS), F32),
-    ]
-    for i, piece in enumerate(pieces):
-        message[i : i + 1, :] = piece
+    rows = own_sums(own[0].astype(F32), row < count_source)
+    rows += own_sums(final[...].astype(F32), row < numbers[4])
+    copies[...] = jnp.broadcast_to(jnp.concatenate(rows, axis=0)[None], copies.shape)
     own_out[...] = own[0]
     last_out[...] = final[...]
     block = lax.broadcasted_iota(jnp.int32, (COLUMN_BLOCKS, CELLS), 0)
@@ -111,79 +106,67 @@
     frame[LAST_GROUP : LAST_GROUP + 1, :] = ones * (g == 3).astype(F32)
 
 
-def core_sums(mine, other, cells, other_cells, out, both):
+def group_sums(frame, messages, shifted, last, own, sums, norms, last_norms, own_out, copies):
+    is_last = frame[LAST_GROUP : LAST_GROUP + 1, :] > 0.0
+    wide_last = jnp.concatenate([is_last, is_last], axis=1)
+    targets = jnp.where(wide_last, last[...].astype(F32), shifted[...].astype(F32)).astype(BF16)
+    for i in range(COLUMN_BLOCKS):
+        copies[i] = targets
+    sums[...] = jnp.sum(messages[...], axis=0)
+    for i in range(COLUMN_BLOCKS):
+        norms[i : i + 1, :] = messages[i, 3:4, :]
+        last_norms[i : i + 1, :] = messages[i, 7:8, :]
+    own_out[...] = own[...]
+
+
+def core_sums(mine, other, out):
     out[...] = mine[...] + other[...]
-    both[:CELLS, :] = cells[...]
-    both[CELLS:, :] = other_cells[...]
-
-
-def three_terms(value):
-    high = value.astype(BF16).astype(F32)
-    rest = value - high
-    middle = rest.astype(BF16).astype(F32)
-    return high, middle, rest - middle
-
-
-def parcel(frame, mine, across, back, back_across, shifted, last, sources, out):
+
+
+def prepared(
+    frame, mine, across, back, back_across, norms, last_norms, x0, x1, x2, x3,
+    rows, weights, column_weights, twice,
+):
     is_last = frame[LAST_GROUP : LAST_GROUP + 1, :] > 0.0
-    here = mine[...] + across[...]
-    there = back[...] + back_across[...]
-    wide_last = jnp.concatenate([is_last, is_last], axis=1)
-    targets = jnp.where(wide_last, last[...].astype(F32), shifted[...].astype(F32))
-    squares = targets * targets
-    norms = jnp.sum((squares[:, :CELLS] + squares[:, CELLS:]).T, axis=0, keepdims=True)
-    target_sums = jnp.where(is_last, here[4:8], there[0:4])
-    extra = jnp.concatenate(
-        [
-            jnp.concatenate([here[0:1], here[1:2]], axis=1),
-            jnp.concatenate([target_sums[0:1], target_sums[1:2]], axis=1),
-            jnp.concatenate([here[2:3], target_sums[2:3]], axis=1),
-            jnp.concatenate([norms, norms], axis=1),
-        ],
-        axis=0,
-    )
-    rows = jnp.concatenate([*three_terms(extra), jnp.zeros((4, WIDTH), F32)], axis=0)
-    whole = jnp.concatenate([targets.astype(BF16), rows.astype(BF16)], axis=0)
-    for i in range(COLUMN_BLOCKS):
-        out[i] = whole
-
-
-def lane_sums(part, k):
-    return jnp.sum(part[k * CELLS : (k + 1) * CELLS, :].T, axis=0, keepdims=True)
-
-
-def first_pass(frame, targets, near, far, scores, sums, rows, weights, part, limits, norms):
-    extra = targets[:, CELLS:, :].astype(F32)
-    extra = extra[:, 0:4] + extra[:, 4:8] + extra[:, 8:12]
-    total = jnp.sum(extra, axis=0)
+    sources = mine[...] + across[...]
+    targets = jnp.where(is_last, sources[4:8], (back[...] + back_across[...])[0:4])
     n_s = frame[N_S : N_S + 1, :]
     n_t = frame[N_T : N_T + 1, :]
-    means = total[0:1] * total[1:2]
-    dot = jnp.sum(means, axis=1, keepdims=True) / n_s / n_t
-    spread = total[2:3, :CELLS] / n_s + total[2:3, CELLS:] / n_t - 2.0 * dot
+    products = (sources[0:2] / n_s) * (targets[0:2] / n_t)
+    dot = jnp.sum(jnp.sum(products, axis=0, keepdims=True), axis=1, keepdims=True)
+    spread = sources[2:3] / n_s + targets[2:3] / n_t - 2.0 * dot
     scale = LOG2E / (EPSILON * spread)
-    for k, block in enumerate((near[...], far[...])):
-        at = slice(k * 2 * CELLS, (k + 1) * 2 * CELLS)
+    twice[...] = jnp.broadcast_to(2.0 * scale, twice.shape)
+    column_weights[...] = jnp.where(is_last, last_norms[...], norms[...]) * scale
+    for k, block in enumerate((x0[...], x1[...], x2[...], x3[...])):
+        at = slice(k * CELLS, (k + 1) * CELLS)
         rows[at, :] = block
         wide = block.astype(F32)
         weights[at, :] = jnp.sum(wide * wide, axis=1, keepdims=True) * scale
-    for i in range(COLUMN_BLOCKS):
-        norms[i : i + 1, :] = extra[i, 3:4, :CELLS] * scale
+
+
+def lane_sums(part, k):
+    return jnp.sum(part[k * CELLS : (k + 1) * CELLS, :].T, axis=0, keepdims=True)
+
+
+def first_pass(
+    frame, targets, rows, weights, column_weights, twice, scores, sums, part, limits
+):
     part[...] = jnp.zeros_like(part)
     limits[...] = jnp.where(frame[COLUMNS_AT : COLUMNS_AT + COLUMN_BLOCKS, :] > 0.0, 0.0, ABSENT)
-    twice = 2.0 * scale
+    factor = twice[0:1, :]
 
     @pl.loop(0, COLUMN_BLOCKS // 2)
     def _(pair):
         first = pair * 2
-        block = targets[pl.ds(first, 2), :CELLS, :].reshape(2 * CELLS, WIDTH)
+        block = targets[pl.ds(first, 2)].reshape(2 * CELLS, WIDTH)
         products = lax.dot_general(
             rows[...], block, (((1,), (1,)), ((), ())), preferred_element_type=F32
         )
         running = part[...]
         for half in range(2):
             at = pl.ds(first + half, 1)
-            tile = (weights[...] + norms[at, :]) - twice * products[
+            tile = (weights[...] + column_weights[at, :]) - factor * products[
                 :, half * CELLS : (half + 1) * CELLS
             ]
             scores[first + half] = tile
@@ -318,9 +301,9 @@
     column_parts = shape(COLUMN_BLOCKS, COLUMN_BLOCKS, CELLS)
 
     with jax.named_scope("moments"):
-        message, own, last, frame = call(
+        copies, own, last, frame = call(
             local_sums,
-            (row_parts, some_cells, some_cells, shape(FRAME, CELLS)),
+            (shape(COLUMN_BLOCKS, 8, CELLS), some_cells, some_cells, shape(FRAME, CELLS)),
             4,
             (
                 pltpu.VMEM((1, CELLS, WIDTH), BF16),
@@ -333,17 +316,24 @@
             name="local_sums",
         )(*(in_hbm(a) for a in (features, last_features, growth, cell_counts)))
         shifted = back(own, 0)
-        other = swapped(message, "c")
-        mine, near = call(
-            core_sums, (row_parts, shape(2 * CELLS, WIDTH, dtype=BF16)), 4, name="core_sums"
-        )(message, other, own, swapped(own, "c"))
+        every_norm = shape(COLUMN_BLOCKS, CELLS)
+        sums, norms, last_norms, own, copies = call(
+            group_sums,
+            (row_parts, every_norm, every_norm, some_cells, shape(COLUMN_BLOCKS, CELLS, WIDTH, dtype=BF16)),
+            5,
+            name="group_sums",
+        )(frame, exchanged(copies), shifted, last, own)
     with jax.named_scope("gather"):
-        sums = (swapped(mine, "z"), back(mine, 0), back(mine, 1))
-        far = swapped(near, "z")
-        copies = call(
-            parcel, shape(COLUMN_BLOCKS, CELLS + EXTRA, WIDTH, dtype=BF16), 7, awaited=1, name="parcel"
-        )(frame, mine, *sums, shifted, last, far)
         targets = exchanged(copies)
+        sources = [own] + [across(own, k) for k in range(1, ROW_BLOCKS)]
+        mine = call(core_sums, row_parts, 2, name="core_sums")(sums, swapped(sums, "c"))
+        sums = (mine, swapped(mine, "z"), back(mine, 0), back(mine, 1))
+        ready = call(
+            prepared,
+            (shape(ROWS, WIDTH, dtype=BF16), shape(ROWS, CELLS), every_norm, shape(8, CELLS)),
+            11,
+            name="prepared",
+        )(frame, *sums, back(norms, 0), last_norms, *sources)
 
     def row_exchange(sums):
         return [sums] + [across(sums, k) for k in range(1, ROW_BLOCKS)]
@@ -352,10 +342,10 @@
         scores, sums = call(
             first_pass,
             (shape(COLUMN_BLOCKS, ROWS, CELLS), row_parts),
-            4,
-            (pltpu.VMEM((ROWS, WIDTH), BF16), part, part, limits, limits),
+            6,
+            (part, limits),
             name="first_pass",
-        )(frame, targets, near, far)
+        )(frame, targets, *ready)
     with jax.named_scope("first_columns"):
         log_p, copies = call(
             first_columns,

time: 83.3 us -> 86.3 us (1.036)
  blocking collectives: 42.4 us -> 33.5 us
  starting transfers between devices: 22.9 us -> 31.2 us
  waiting for transfers between devices: 9.16 us -> 11.5 us
  Pallas kernels: 7.9 us -> 9.08 us
    all_to_all x3, blocking collectives: 42.4 us -> 33.5 us  [exchanged(): lax.all_to_all(copies, COLUMN_AXES, split_axis=0, concat_axis=0, tiled=True)]
    ppermute x3 -> x4, starting transfers between devices: 6.18 us -> 10.7 us  [back(): return lax.ppermute(value, ('z', 'g'), moves)]
    ppermute x9 -> x12, starting transfers between devices: 11.8 us -> 15.6 us  [across(): return lax.ppermute(value, ROW_AXES, [(d, d ^ k) for d in range(4)])]
    ppermute x4 -> x2, starting transfers between devices: 4.97 us -> 1.25 us  [swapped(): return lax.ppermute(value, axis, [(0, 1), (1, 0)])]
    all_to_all x0 -> x1, starting transfers between devices: none -> 3.65 us  [exchanged(): lax.all_to_all(copies, COLUMN_AXES, split_axis=0, concat_axis=0, tiled=True)]
    all_to_all x0 -> x1, waiting for transfers between devices: none -> 1.44 us  [exchanged(): lax.all_to_all(copies, COLUMN_AXES, split_axis=0, concat_axis=0, tiled=True)]
    ppermute x3 -> x4, waiting for transfers between devices: 1.66 us -> 2.82 us  [back(): return lax.ppermute(value, ('z', 'g'), moves)]
    pallas_call x4 -> x5, Pallas kernels: 3.88 us -> 4.95 us  [the longest x1 2.54 us: local(): call(first_pass, (shape(COLUMN_BLOCKS, ROWS, CELLS), row_parts), 6, (part...]
  transfers between devices with their start and end apart: 16 -> 19, of which waited for: 8 -> 10; matrix products, arithmetic and copies ran while one was open for 0% -> 0% of each run, Pallas kernels for 0% -> 0%
where the time goes in v4:
time: 86.3 us; the launch traced here: 86 us
  blocking collectives  33.5 us (39%)
  starting transfers between devices  31.2 us (36%)
  waiting for transfers between devices  11.5 us (13%)
  Pallas kernels  9.08 us (11%)
    all_to_all x3, blocking collectives, exchanged(): lax.all_to_all(copies, COLUMN_AXES, split_axis=0, concat_axis=0, tiled=True)  33.5 us
    ppermute x12, starting transfers between devices, across(): return lax.ppermute(value, ROW_AXES, [(d, d ^ k) for d in range(4)])  15.6 us
    ppermute x4, starting transfers between devices, back(): return lax.ppermute(value, ('z', 'g'), moves)  10.7 us
    ppermute x12, waiting for transfers between devices, across(): return lax.ppermute(value, ROW_AXES, [(d, d ^ k) for d in range(4)])  5.89 us
    all_to_all x1, starting transfers between devices, exchanged(): lax.all_to_all(copies, COLUMN_AXES, split_axis=0, concat_axis=0, tiled=True)  3.65 us
    ppermute x4, waiting for transfers between devices, back(): return lax.ppermute(value, ('z', 'g'), moves)  2.82 us
    pallas_call x1, Pallas kernels, local(): call(first_pass, (shape(COLUMN_BLOCKS, ROWS, CELLS), row_parts), 6, (part...  2.54 us
  transfers between devices with their start and end apart: 19, of which 10 were waited for; matrix products, arithmetic and copies ran while one was open for 0% of the time, Pallas kernels for 0%

profile of v4, /device:TPU:1, one launch (start us, length us, event | category | flops | bytes accessed | tf_op | source)
XLA Modules:
  0.0 86.0 jit_solution(12025100558708835586)
XLA Ops:
  0.6 1.1 %local_sums.1 = (f32[16,8,128]{2,1,0:T(8,128)S(1)}, bf16[128,256]{1,0:T(8,128)(2,1)S(1)}, bf16[128,256]{1,0:T(8,128)(2,1)S(1)}, f32[24,128]{1,0:T(8,128)S(1)}) custom-call(bf16[1,128,256]{2,1,0:T(8,128)(2,1)} %features.1, bf16[128,256]{1,0:T(8,128)(2,1)} %last.1, f32[1,128]{1,0:T(1,128)} %growth.1, s32[5]{0:T(128)} %counts.1), custom_call_target="tpu_custom_call" | custom-call | tf_op jit(solution)/shard_map/moments/local_sums/pallas_call | solution.py:304
  1.7 6.9 %collective-permute-start = (bf16[128,256]{1,0:T(8,128)(2,1)S(1)}, bf16[128,256]{1,0:T(8,128)(2,1)S(1)}, u32[]{:S(2)}, u32[]{:S(2)}) collective-permute-start(bf16[128,256]{1,0:T(8,128)(2,1)S(1)} %get-tuple-element.30.own), channel_id=1, source_target_pairs={{0,3},{1,0},{2,1},{3,2},{32,35},{33,32},{34,33},{35,34},{4,7},{5,4... | collective-permute-start | bytes 196616 | tf_op jit(solution)/shard_map/moments/ppermute | solution.py:289
  8.7 13.1 %all_to_all.20.messages = f32[16,8,128]{2,1,0:T(8,128)S(1)} all-to-all(f32[16,8,128]{2,1,0:T(8,128)S(1)} %get-tuple-element.29), channel_id=1, replica_groups=mesh['x'=4,'z'=2,'y'=4,'c'=2,'g'=4] {'x','y'}, dimensions={0} | all-to-all | bytes 131072 | tf_op jit(solution)/shard_map/moments/all_to_all | solution.py:293
  21.7 0.0 collective-permute-done.shifted
  21.7 1.1 %group_sums.1 = (f32[8,128]{1,0:T(8,128)S(1)}, f32[16,128]{1,0:T(8,128)S(1)}, f32[16,128]{1,0:T(8,128)S(1)}, bf16[128,256]{1,0:T(8,128)(2,1)S(1)}, bf16[16,128,256]{2,1,0:T(8,128)(2,1)}) custom-call(f32[24,128]{1,0:T(8,128)S(1)} %get-tuple-element.28.frame, f32[16,8,128]{2,1,0:T(8,128)S(1)} %all_to_all.20.messages, ...), custom_call_target="tpu_custom_call" | custom-call | tf_op jit(solution)/shard_map/moments/group_sums/pallas_call | solution.py:320
  22.9 3.7 %all-to-all-start.1 = ((bf16[16,128,256]{2,1,0:T(8,128)(2,1)}), bf16[16,128,256]{2,1,0:T(8,128)(2,1)S(1)}, u32[]{:S(2)}, u32[]{:S(2)}) async-start(bf16[16,128,256]{2,1,0:T(8,128)(2,1)} %get-tuple-element.32), calls=%async_computation.1 | async-start | bytes 2097152 | tf_op jit(solution)/shard_map/gather/all_to_all | solution.py:293
  26.5 3.1 %collective-permute-start.8 = (bf16[128,256]{1,0:T(8,128)(2,1)S(1)}, bf16[128,256]{1,0:T(8,128)(2,1)S(1)}, u32[]{:S(2)}, u32[]{:S(2)}) collective-permute-start(bf16[128,256]{1,0:T(8,128)(2,1)S(1)} %get-tuple-element.36.x0), channel_id=1, source_target_pairs={{0,36},{4,32},{32,4},{36,0},{1,37},{5,33},{33,5},{37,1},{2,38},{6,... | collective-permute-start | bytes 196616 | tf_op jit(solution)/shard_map/gather/ppermute | solution.py:284
  29.6 0.7 collective-permute-start.7
  30.4 0.0 collective-permute-start.6
  30.4 0.5 collective-permute-start.1
  30.9 1.2 %collective-permute-start.5 = (f32[16,128]{1,0:T(8,128)S(1)}, f32[16,128]{1,0:T(8,128)S(1)}, u32[]{:S(2)}, u32[]{:S(2)}) collective-permute-start(f32[16,128]{1,0:T(8,128)S(1)} %get-tuple-element.34), channel_id=1, source_target_pairs={{0,3},{1,0},{2,1},{3,2},{32,35},{33,32},{34,33},{35,34},{4,7},{5,4... | collective-permute-start | bytes 24584 | tf_op jit(solution)/shard_map/gather/ppermute | solution.py:289
  32.0 0.0 collective-permute-done.1.other
  32.0 0.4 collective-permute-start.4
  32.4 2.1 %collective-permute-done.5.norms = f32[16,128]{1,0:T(8,128)S(1)} collective-permute-done((f32[16,128]{1,0:T(8,128)S(1)}, f32[16,128]{1,0:T(8,128)S(1)}, u32[]{:S(2)}, u32[]{:S(2)}) %collective-permute-start.5) | collective-permute-done | bytes 8224 | tf_op jit(solution)/shard_map/gather/ppermute | solution.py:289
  34.6 2.2 %collective-permute-start.3 = (f32[8,128]{1,0:T(8,128)S(1)}, f32[8,128]{1,0:T(8,128)S(1)}, u32[]{:S(2)}, u32[]{:S(2)}) collective-permute-start(f32[8,128]{1,0:T(8,128)S(1)} %core_sums.1.mine), channel_id=1, source_target_pairs={{0,3},{1,0},{2,1},{3,2},{32,35},{33,32},{34,33},{35,34},{4,7},{5,4... | collective-permute-start | bytes 12296 | tf_op jit(solution)/shard_map/gather/ppermute | solution.py:289
  36.8 0.0 collective-permute-done.4.back_across
  36.8 0.7 collective-permute-start.2
  37.5 0.7 collective-permute-done.3.back
  38.2 1.3 %collective-permute-done.2.across = f32[8,128]{1,0:T(8,128)S(1)} collective-permute-done((f32[8,128]{1,0:T(8,128)S(1)}, f32[8,128]{1,0:T(8,128)S(1)}, u32[]{:S(2)}, u32[]{:S(2)}) %collective-permute-start.2) | collective-permute-done | bytes 4128 | tf_op jit(solution)/shard_map/gather/ppermute | solution.py:280
  39.6 0.0 collective-permute-done.8.x3
  39.6 0.0 collective-permute-done.7.x2
  39.6 0.0 collective-permute-done.6.x1
  39.6 0.2 prepared.1
  39.7 1.4 %all-to-all-done.1.targets = bf16[16,128,256]{2,1,0:T(8,128)(2,1)S(1)} async-done(((bf16[16,128,256]{2,1,0:T(8,128)(2,1)}), bf16[16,128,256]{2,1,0:T(8,128)(2,1)S(1)}, u32[]{:S(2)}, u32[]{:S(2)}) %all-to-all-start.1) | async-done | bytes 1048608 | tf_op jit(solution)/shard_map/gather/all_to_all | solution.py:293
  41.2 2.5 %first_pass.1 = (f32[16,512,128]{2,1,0:T(8,128)S(1)}, f32[8,128]{1,0:T(8,128)S(1)}) custom-call(f32[24,128]{1,0:T(8,128)S(1)} %get-tuple-element.28.frame, bf16[16,128,256]{2,1,0:T(8,128)(2,1)S(1)} %all-to-all-done.1.targets, bf16[512,256]{1,0:T(8,128)(2,1)S(1)} %get-tuple-element.37.rows, f32[512,128]{1,0:T(8,128)S(1)} %get-tuple-element.38.weights, ...), custom_call_target="tpu_custom_call" | custom-call | tf_op jit(solution)/shard_map/first_rows/first_pass/pallas_call | solution.py:342
  43.7 4.1 %collective-permute-start.11 = (f32[8,128]{1,0:T(8,128)S(1)}, f32[8,128]{1,0:T(8,128)S(1)}, u32[]{:S(2)}, u32[]{:S(2)}) collective-permute-start(f32[8,128]{1,0:T(8,128)S(1)} %get-tuple-element.41.p0), channel_id=1, source_target_pairs={{0,36},{4,32},{32,4},{36,0},{1,37},{5,33},{33,5},{37,1},{2,38},{6,... | collective-permute-start | bytes 12296 | tf_op jit(solution)/shard_map/first_columns/ppermute | solution.py:284
  47.8 0.7 collective-permute-start.10
  48.5 0.0 collective-permute-start.9
  48.6 0.5 collective-permute-done.11.p3
  49.1 1.4 %collective-permute-done.10.p2 = f32[8,128]{1,0:T(8,128)S(1)} collective-permute-done((f32[8,128]{1,0:T(8,128)S(1)}, f32[8,128]{1,0:T(8,128)S(1)}, u32[]{:S(2)}, u32[]{:S(2)}) %collective-permute-start.10) | collective-permute-done | bytes 4128 | tf_op jit(solution)/shard_map/first_columns/ppermute | solution.py:284
  50.5 0.0 collective-permute-done.9.p1
  50.5 0.8 first_columns.1
  51.4 10.7 %all_to_all.21.parts = f32[16,16,128]{2,1,0:T(8,128)S(1)} all-to-all(f32[16,16,128]{2,1,0:T(8,128)S(1)} %get-tuple-element.44), channel_id=1, replica_groups=mesh['x'=4,'z'=2,'y'=4,'c'=2,'g'=4] {'x','y'}, dimensions={0} | all-to-all | bytes 262144 | tf_op jit(solution)/shard_map/first_columns/all_to_all | solution.py:293
  62.0 1.0 %second_rows.1.p0 = f32[4,128]{1,0:T(4,128)S(1)} custom-call(f32[24,128]{1,0:T(8,128)S(1)} %get-tuple-element.28.frame, f32[16,16,128]{2,1,0:T(8,128)S(1)} %all_to_all.21.parts, f32[16,512,128]{2,1,0:T(8,128)S(1)} %get-tuple-element.42.scores), custom_call_target="tpu_custom_call" | custom-call | tf_op jit(solution)/shard_map/second_rows/second_rows/pallas_call | solution.py:359
  63.0 2.5 %collective-permute-start.14 = (f32[4,128]{1,0:T(4,128)S(1)}, f32[4,128]{1,0:T(4,128)S(1)}, u32[]{:S(2)}, u32[]{:S(2)}) collective-permute-start(f32[4,128]{1,0:T(4,128)S(1)} %second_rows.1.p0), channel_id=1, source_target_pairs={{0,36},{4,32},{32,4},{36,0},{1,37},{5,33},{33,5},{37,1},{2,38},{6,... | collective-permute-start | bytes 6152 | tf_op jit(solution)/shard_map/last_columns/ppermute | solution.py:284
  65.5 0.7 collective-permute-start.13
  66.3 0.5 collective-permute-done.14.p3
  66.8 1.4 %collective-permute-done.13.p2 = f32[4,128]{1,0:T(4,128)S(1)} collective-permute-done((f32[4,128]{1,0:T(4,128)S(1)}, f32[4,128]{1,0:T(4,128)S(1)}, u32[]{:S(2)}, u32[]{:S(2)}) %collective-permute-start.13) | collective-permute-done | bytes 2080 | tf_op jit(solution)/shard_map/last_columns/ppermute | solution.py:284
  68.2 0.8 last_columns.1
  69.0 9.8 %all_to_all.22.parts = f32[16,16,128]{2,1,0:T(8,128)S(1)} all-to-all(f32[16,16,128]{2,1,0:T(8,128)S(1)} %get-tuple-element.46), channel_id=1, replica_groups=mesh['x'=4,'z'=2,'y'=4,'c'=2,'g'=4] {'x','y'}, dimensions={0} | all-to-all | bytes 262144 | tf_op jit(solution)/shard_map/last_columns/all_to_all | solution.py:293
  78.9 1.0 %last_rows.1 = (f32[1,128]{1,0:T(1,128)S(1)}, f32[1,128]{1,0:T(1,128)S(1)}, f32[1,128]{1,0:T(1,128)S(1)}, f32[1,128]{1,0:T(1,128)S(1)}, f32[1,128]{1,0:T(1,128)S(1)}) custom-call(f32[24,128]{1,0:T(8,128)S(1)} %get-tuple-element.28.frame, f32[16,16,128]{2,1,0:T(8,128)S(1)} %all_to_all.22.parts, f32[16,512,128]{2,1,0:T(8,128)S(1)} %get-tuple-element.42.scores, ...), custom_call_target="tpu_custom_call" | custom-call | tf_op jit(solution)/shard_map/mass/last_rows/pallas_call | solution.py:372
  79.8 1.9 %collective-permute-start.15 = (f32[1,128]{1,0:T(1,128)S(1)}, f32[1,128]{1,0:T(1,128)S(1)}, u32[]{:S(2)}, u32[]{:S(2)}) collective-permute-start(f32[1,128]{1,0:T(1,128)S(1)} %get-tuple-element.50), channel_id=1, source_target_pairs={{0,4},{4,0},{32,36},{36,32},{1,5},{5,1},{33,37},{37,33},{2,6},{6,2... | collective-permute-start | bytes 1544 | tf_op jit(solution)/shard_map/mass/ppermute | solution.py:284
  81.8 0.7 collective-permute-start.16
  82.5 1.0 %collective-permute-start.17 = (f32[1,128]{1,0:T(1,128)S(1)}, f32[1,128]{1,0:T(1,128)S(1)}, u32[]{:S(2)}, u32[]{:S(2)}) collective-permute-start(f32[1,128]{1,0:T(1,128)S(1)} %get-tuple-element.52), channel_id=1, source_target_pairs={{0,36},{4,32},{32,4},{36,0},{1,37},{5,33},{33,5},{37,1},{2,38},{6,... | collective-permute-start | bytes 1544 | tf_op jit(solution)/shard_map/mass/ppermute | solution.py:284
  83.5 0.0 collective-permute-done.15.q1
  83.5 0.7 collective-permute-done.16.q2
  84.2 1.3 %collective-permute-done.17.q3 = f32[1,128]{1,0:T(1,128)S(1)} collective-permute-done((f32[1,128]{1,0:T(1,128)S(1)}, f32[1,128]{1,0:T(1,128)S(1)}, u32[]{:S(2)}, u32[]{:S(2)}) %collective-permute-start.17) | collective-permute-done | bytes 544 | tf_op jit(solution)/shard_map/mass/ppermute | solution.py:284
  85.5 0.5 outputs.1
  (3 shorter events, 0.0 us)
Async XLA Ops:
  1.7 20.0 %collective-permute-start = (bf16[128,256]{1,0:T(8,128)(2,1)S(1)}, bf16[128,256]{1,0:T(8,128)(2,1)S(1)}, u32[]{:S(2)}, u32[]{:S(2)}) collective-permute-start(bf16[128,256]{1,0:T(8,128)(2,1)S(1)} %get-tuple-element.30.own), channel_id=1, source_target_pairs={{0,3},{1,0},{2,1},{3,2},{32,35},{33,32},{34,33},{35,34},{4,7},{5,4... | collective-permute-start | bytes 196616 | tf_op jit(solution)/shard_map/moments/ppermute | solution.py:289
  22.9 18.3 %all-to-all-start.1 = ((bf16[16,128,256]{2,1,0:T(8,128)(2,1)}), bf16[16,128,256]{2,1,0:T(8,128)(2,1)S(1)}, u32[]{:S(2)}, u32[]{:S(2)}) async-start(bf16[16,128,256]{2,1,0:T(8,128)(2,1)} %get-tuple-element.32), calls=%async_computation.1 | async-start | bytes 2097152 | tf_op jit(solution)/shard_map/gather/all_to_all | solution.py:293
  26.5 13.0 %collective-permute-start.8 = (bf16[128,256]{1,0:T(8,128)(2,1)S(1)}, bf16[128,256]{1,0:T(8,128)(2,1)S(1)}, u32[]{:S(2)}, u32[]{:S(2)}) collective-permute-start(bf16[128,256]{1,0:T(8,128)(2,1)S(1)} %get-tuple-element.36.x0), channel_id=1, source_target_pairs={{0,36},{4,32},{32,4},{36,0},{1,37},{5,33},{33,5},{37,1},{2,38},{6,... | collective-permute-start | bytes 196616 | tf_op jit(solution)/shard_map/gather/ppermute | solution.py:284
  29.6 9.9 %collective-permute-start.7 = (bf16[128,256]{1,0:T(8,128)(2,1)S(1)}, bf16[128,256]{1,0:T(8,128)(2,1)S(1)}, u32[]{:S(2)}, u32[]{:S(2)}) collective-permute-start(bf16[128,256]{1,0:T(8,128)(2,1)S(1)} %get-tuple-element.36.x0), channel_id=1, source_target_pairs={{0,32},{4,36},{32,0},{36,4},{1,33},{5,37},{33,1},{37,5},{2,34},{6,... | collective-permute-start | bytes 196616 | tf_op jit(solution)/shard_map/gather/ppermute | solution.py:284
  30.4 9.2 %collective-permute-start.6 = (bf16[128,256]{1,0:T(8,128)(2,1)S(1)}, bf16[128,256]{1,0:T(8,128)(2,1)S(1)}, u32[]{:S(2)}, u32[]{:S(2)}) collective-permute-start(bf16[128,256]{1,0:T(8,128)(2,1)S(1)} %get-tuple-element.36.x0), channel_id=1, source_target_pairs={{0,4},{4,0},{32,36},{36,32},{1,5},{5,1},{33,37},{37,33},{2,6},{6,2... | collective-permute-start | bytes 196616 | tf_op jit(solution)/shard_map/gather/ppermute | solution.py:284
  30.4 1.7 %collective-permute-start.1 = (f32[8,128]{1,0:T(8,128)S(1)}, f32[8,128]{1,0:T(8,128)S(1)}, u32[]{:S(2)}, u32[]{:S(2)}) collective-permute-start(f32[8,128]{1,0:T(8,128)S(1)} %get-tuple-element.33.mine), channel_id=1, source_target_pairs={{0,4},{4,0},{1,5},{5,1},{2,6},{6,2},{3,7},{7,3},{8,12},{12,8},{9,1... | collective-permute-start | bytes 12296 | tf_op jit(solution)/shard_map/gather/ppermute | solution.py:280
  30.9 3.7 %collective-permute-start.5 = (f32[16,128]{1,0:T(8,128)S(1)}, f32[16,128]{1,0:T(8,128)S(1)}, u32[]{:S(2)}, u32[]{:S(2)}) collective-permute-start(f32[16,128]{1,0:T(8,128)S(1)} %get-tuple-element.34), channel_id=1, source_target_pairs={{0,3},{1,0},{2,1},{3,2},{32,35},{33,32},{34,33},{35,34},{4,7},{5,4... | collective-permute-start | bytes 24584 | tf_op jit(solution)/shard_map/gather/ppermute | solution.py:289
  32.0 4.8 %collective-permute-start.4 = (f32[8,128]{1,0:T(8,128)S(1)}, f32[8,128]{1,0:T(8,128)S(1)}, u32[]{:S(2)}, u32[]{:S(2)}) collective-permute-start(f32[8,128]{1,0:T(8,128)S(1)} %core_sums.1.mine), channel_id=1, source_target_pairs={{0,35},{1,32},{2,33},{3,34},{32,3},{33,0},{34,1},{35,2},{4,39},{5,... | collective-permute-start | bytes 12296 | tf_op jit(solution)/shard_map/gather/ppermute | solution.py:289
  34.6 3.7 %collective-permute-start.3 = (f32[8,128]{1,0:T(8,128)S(1)}, f32[8,128]{1,0:T(8,128)S(1)}, u32[]{:S(2)}, u32[]{:S(2)}) collective-permute-start(f32[8,128]{1,0:T(8,128)S(1)} %core_sums.1.mine), channel_id=1, source_target_pairs={{0,3},{1,0},{2,1},{3,2},{32,35},{33,32},{34,33},{35,34},{4,7},{5,4... | collective-permute-start | bytes 12296 | tf_op jit(solution)/shard_map/gather/ppermute | solution.py:289
  36.8 2.8 %collective-permute-start.2 = (f32[8,128]{1,0:T(8,128)S(1)}, f32[8,128]{1,0:T(8,128)S(1)}, u32[]{:S(2)}, u32[]{:S(2)}) collective-permute-start(f32[8,128]{1,0:T(8,128)S(1)} %core_sums.1.mine), channel_id=1, source_target_pairs={{0,32},{32,0},{1,33},{33,1},{2,34},{34,2},{3,35},{35,3},{4,36},{36... | collective-permute-start | bytes 12296 | tf_op jit(solution)/shard_map/gather/ppermute | solution.py:280
  43.7 5.4 %collective-permute-start.11 = (f32[8,128]{1,0:T(8,128)S(1)}, f32[8,128]{1,0:T(8,128)S(1)}, u32[]{:S(2)}, u32[]{:S(2)}) collective-permute-start(f32[8,128]{1,0:T(8,128)S(1)} %get-tuple-element.41.p0), channel_id=1, source_target_pairs={{0,36},{4,32},{32,4},{36,0},{1,37},{5,33},{33,5},{37,1},{2,38},{6,... | collective-permute-start | bytes 12296 | tf_op jit(solution)/shard_map/first_columns/ppermute | solution.py:284
  47.8 2.7 %collective-permute-start.10 = (f32[8,128]{1,0:T(8,128)S(1)}, f32[8,128]{1,0:T(8,128)S(1)}, u32[]{:S(2)}, u32[]{:S(2)}) collective-permute-start(f32[8,128]{1,0:T(8,128)S(1)} %get-tuple-element.41.p0), channel_id=1, source_target_pairs={{0,32},{4,36},{32,0},{36,4},{1,33},{5,37},{33,1},{37,5},{2,34},{6,... | collective-permute-start | bytes 12296 | tf_op jit(solution)/shard_map/first_columns/ppermute | solution.py:284
  48.5 2.0 %collective-permute-start.9 = (f32[8,128]{1,0:T(8,128)S(1)}, f32[8,128]{1,0:T(8,128)S(1)}, u32[]{:S(2)}, u32[]{:S(2)}) collective-permute-start(f32[8,128]{1,0:T(8,128)S(1)} %get-tuple-element.41.p0), channel_id=1, source_target_pairs={{0,4},{4,0},{32,36},{36,32},{1,5},{5,1},{33,37},{37,33},{2,6},{6,2... | collective-permute-start | bytes 12296 | tf_op jit(solution)/shard_map/first_columns/ppermute | solution.py:284
  63.0 3.8 %collective-permute-start.14 = (f32[4,128]{1,0:T(4,128)S(1)}, f32[4,128]{1,0:T(4,128)S(1)}, u32[]{:S(2)}, u32[]{:S(2)}) collective-permute-start(f32[4,128]{1,0:T(4,128)S(1)} %second_rows.1.p0), channel_id=1, source_target_pairs={{0,36},{4,32},{32,4},{36,0},{1,37},{5,33},{33,5},{37,1},{2,38},{6,... | collective-permute-start | bytes 6152 | tf_op jit(solution)/shard_map/last_columns/ppermute | solution.py:284
  65.5 2.7 %collective-permute-start.13 = (f32[4,128]{1,0:T(4,128)S(1)}, f32[4,128]{1,0:T(4,128)S(1)}, u32[]{:S(2)}, u32[]{:S(2)}) collective-permute-start(f32[4,128]{1,0:T(4,128)S(1)} %second_rows.1.p0), channel_id=1, source_target_pairs={{0,32},{4,36},{32,0},{36,4},{1,33},{5,37},{33,1},{37,5},{2,34},{6,... | collective-permute-start | bytes 6152 | tf_op jit(solution)/shard_map/last_columns/ppermute | solution.py:284
  66.3 1.9 %collective-permute-start.12 = (f32[4,128]{1,0:T(4,128)S(1)}, f32[4,128]{1,0:T(4,128)S(1)}, u32[]{:S(2)}, u32[]{:S(2)}) collective-permute-start(f32[4,128]{1,0:T(4,128)S(1)} %second_rows.1.p0), channel_id=1, source_target_pairs={{0,4},{4,0},{32,36},{36,32},{1,5},{5,1},{33,37},{37,33},{2,6},{6,2... | collective-permute-start | bytes 6152 | tf_op jit(solution)/shard_map/last_columns/ppermute | solution.py:284
  79.8 3.6 %collective-permute-start.15 = (f32[1,128]{1,0:T(1,128)S(1)}, f32[1,128]{1,0:T(1,128)S(1)}, u32[]{:S(2)}, u32[]{:S(2)}) collective-permute-start(f32[1,128]{1,0:T(1,128)S(1)} %get-tuple-element.50), channel_id=1, source_target_pairs={{0,4},{4,0},{32,36},{36,32},{1,5},{5,1},{33,37},{37,33},{2,6},{6,2... | collective-permute-start | bytes 1544 | tf_op jit(solution)/shard_map/mass/ppermute | solution.py:284
  81.8 2.4 %collective-permute-start.16 = (f32[1,128]{1,0:T(1,128)S(1)}, f32[1,128]{1,0:T(1,128)S(1)}, u32[]{:S(2)}, u32[]{:S(2)}) collective-permute-start(f32[1,128]{1,0:T(1,128)S(1)} %get-tuple-element.51), channel_id=1, source_target_pairs={{0,32},{4,36},{32,0},{36,4},{1,33},{5,37},{33,1},{37,5},{2,34},{6,... | collective-permute-start | bytes 1544 | tf_op jit(solution)/shard_map/mass/ppermute | solution.py:284
  82.5 3.0 %collective-permute-start.17 = (f32[1,128]{1,0:T(1,128)S(1)}, f32[1,128]{1,0:T(1,128)S(1)}, u32[]{:S(2)}, u32[]{:S(2)}) collective-permute-start(f32[1,128]{1,0:T(1,128)S(1)} %get-tuple-element.52), channel_id=1, source_target_pairs={{0,36},{4,32},{32,4},{36,0},{1,37},{5,33},{33,5},{37,1},{2,38},{6,... | collective-permute-start | bytes 1544 | tf_op jit(solution)/shard_map/mass/ppermute | solution.py:284

commit v5 on v4

--- a/solution.py
+++ b/solution.py
@@ -42,11 +42,12 @@
     return jax.ShapeDtypeStruct(dims, dtype)
 
 
-def call(kernel, out_shape, n_inputs, scratch=(), space=pltpu.VMEM, name=None):
+def call(kernel, out_shape, n_inputs, scratch=(), space=pltpu.VMEM, awaited=0, name=None):
     return pl.pallas_call(
         kernel,
         out_shape=out_shape,
-        in_specs=[pl.BlockSpec(memory_space=space)] * n_inputs,
+        in_specs=[pl.BlockSpec(memory_space=space)] * n_inputs
+        + [pl.BlockSpec(memory_space=pl.ANY)] * awaited,
         out_specs=jax.tree.map(lambda _: pl.BlockSpec(memory_space=pltpu.VMEM), out_shape),
         scratch_shapes=list(scratch),
         compiler_params=pltpu.CompilerParams(vmem_limit_bytes=16 * 1024 * 1024),
@@ -106,7 +107,7 @@
     frame[LAST_GROUP : LAST_GROUP + 1, :] = ones * (g == 3).astype(F32)
 
 
-def group_sums(frame, messages, shifted, last, own, sums, norms, last_norms, own_out, copies):
+def group_sums(frame, messages, shifted, last, x1, x2, x3, sums, norms, last_norms, copies):
     is_last = frame[LAST_GROUP : LAST_GROUP + 1, :] > 0.0
     wide_last = jnp.concatenate([is_last, is_last], axis=1)
     targets = jnp.where(wide_last, last[...].astype(F32), shifted[...].astype(F32)).astype(BF16)
@@ -116,7 +117,6 @@
     for i in range(COLUMN_BLOCKS):
         norms[i : i + 1, :] = messages[i, 3:4, :]
         last_norms[i : i + 1, :] = messages[i, 7:8, :]
-    own_out[...] = own[...]
 
 
 def core_sums(mine, other, out):
@@ -317,15 +317,16 @@
         )(*(in_hbm(a) for a in (features, last_features, growth, cell_counts)))
         shifted = back(own, 0)
         every_norm = shape(COLUMN_BLOCKS, CELLS)
-        sums, norms, last_norms, own, copies = call(
+        sources = [across(own, k) for k in range(1, ROW_BLOCKS)]
+        sums, norms, last_norms, copies = call(
             group_sums,
-            (row_parts, every_norm, every_norm, some_cells, shape(COLUMN_BLOCKS, CELLS, WIDTH, dtype=BF16)),
-            5,
+            (row_parts, every_norm, every_norm, shape(COLUMN_BLOCKS, CELLS, WIDTH, dtype=BF16)),
+            4,
+            awaited=3,
             name="group_sums",
-        )(frame, exchanged(copies), shifted, last, own)
+        )(frame, exchanged(copies), shifted, last, *sources)
     with jax.named_scope("gather"):
         targets = exchanged(copies)
-        sources = [own] + [across(own, k) for k in range(1, ROW_BLOCKS)]
         mine = call(core_sums, row_parts, 2, name="core_sums")(sums, swapped(sums, "c"))
         sums = (mine, swapped(mine, "z"), back(mine, 0), back(mine, 1))
         ready = call(
@@ -333,7 +334,7 @@
             (shape(ROWS, WIDTH, dtype=BF16), shape(ROWS, CELLS), every_norm, shape(8, CELLS)),
             11,
             name="prepared",
-        )(frame, *sums, back(norms, 0), last_norms, *sources)
+        )(frame, *sums, back(norms, 0), last_norms, own, *sources)
 
     def row_exchange(sums):
         return [sums] + [across(sums, k) for k in range(1, ROW_BLOCKS)]

time: 86.3 us -> 87.6 us (1.015)
  waiting for transfers between devices: 11.5 us -> 15.2 us
  starting transfers between devices: 31.2 us -> 29.7 us
    all_to_all x1, waiting for transfers between devices: 1.44 us -> 6.69 us  [exchanged(): lax.all_to_all(copies, COLUMN_AXES, split_axis=0, concat_axis=0, tiled=True)]
    ppermute x4, starting transfers between devices: 10.7 us -> 6.39 us  [back(): return lax.ppermute(value, ('z', 'g'), moves)]
    ppermute x2, starting transfers between devices: 1.25 us -> 3.37 us  [swapped(): return lax.ppermute(value, axis, [(0, 1), (1, 0)])]
    ppermute x2, waiting for transfers between devices: 1.34 us -> 0.01 us  [swapped(): return lax.ppermute(value, axis, [(0, 1), (1, 0)])]
    all_to_all x3, blocking collectives: 33.5 us -> 32.7 us  [exchanged(): lax.all_to_all(copies, COLUMN_AXES, split_axis=0, concat_axis=0, tiled=True)]
  transfers between devices with their start and end apart: 19 -> 19, of which waited for: 10 -> 9; matrix products, arithmetic and copies ran while one was open for 0% -> 0% of each run, Pallas kernels for 0% -> 0%
where the time goes in v5:
time: 87.6 us; the launch traced here: 87.3 us
  blocking collectives  32.7 us (37%)
  starting transfers between devices  29.7 us (34%)
  waiting for transfers between devices  15.2 us (17%)
  Pallas kernels  9.07 us (10%)
    all_to_all x3, blocking collectives, exchanged(): lax.all_to_all(copies, COLUMN_AXES, split_axis=0, concat_axis=0, tiled=True)  32.7 us
    ppermute x12, starting transfers between devices, across(): return lax.ppermute(value, ROW_AXES, [(d, d ^ k) for d in range(4)])  16.3 us
    all_to_all x1, waiting for transfers between devices, exchanged(): lax.all_to_all(copies, COLUMN_AXES, split_axis=0, concat_axis=0, tiled=True)  6.69 us
    ppermute x4, starting transfers between devices, back(): return lax.ppermute(value, ('z', 'g'), moves)  6.39 us
    ppermute x12, waiting for transfers between devices, across(): return lax.ppermute(value, ROW_AXES, [(d, d ^ k) for d in range(4)])  5.9 us
    all_to_all x1, starting transfers between devices, exchanged(): lax.all_to_all(copies, COLUMN_AXES, split_axis=0, concat_axis=0, tiled=True)  3.65 us
    ppermute x2, starting transfers between devices, swapped(): return lax.ppermute(value, axis, [(0, 1), (1, 0)])  3.37 us
    ppermute x4, waiting for transfers between devices, back(): return lax.ppermute(value, ('z', 'g'), moves)  2.56 us
  transfers between devices with their start and end apart: 19, of which 9 were waited for; matrix products, arithmetic and copies ran while one was open for 0% of the time, Pallas kernels for 0%

profile of v5, /device:TPU:1, one launch (start us, length us, event | category | flops | bytes accessed | tf_op | source)
XLA Modules:
  0.0 87.3 jit_solution(5745020106229234034)
XLA Ops:
  0.6 1.1 %local_sums.1 = (f32[16,8,128]{2,1,0:T(8,128)S(1)}, bf16[128,256]{1,0:T(8,128)(2,1)S(1)}, bf16[128,256]{1,0:T(8,128)(2,1)S(1)}, f32[24,128]{1,0:T(8,128)S(1)}) custom-call(bf16[1,128,256]{2,1,0:T(8,128)(2,1)} %features.1, bf16[128,256]{1,0:T(8,128)(2,1)} %last.1, f32[1,128]{1,0:T(1,128)} %growth.1, s32[5]{0:T(128)} %counts.1), custom_call_target="tpu_custom_call" | custom-call | tf_op jit(solution)/shard_map/moments/local_sums/pallas_call | solution.py:304
  1.7 3.1 %collective-permute-start.3 = (bf16[128,256]{1,0:T(8,128)(2,1)S(1)}, bf16[128,256]{1,0:T(8,128)(2,1)S(1)}, u32[]{:S(2)}, u32[]{:S(2)}) collective-permute-start(bf16[128,256]{1,0:T(8,128)(2,1)S(1)} %get-tuple-element.29.x0), channel_id=1, source_target_pairs={{0,36},{4,32},{32,4},{36,0},{1,37},{5,33},{33,5},{37,1},{2,38},{6,... | collective-permute-start | bytes 196616 | tf_op jit(solution)/shard_map/moments/ppermute | solution.py:284
  4.9 1.6 %collective-permute-start.2 = (bf16[128,256]{1,0:T(8,128)(2,1)S(1)}, bf16[128,256]{1,0:T(8,128)(2,1)S(1)}, u32[]{:S(2)}, u32[]{:S(2)}) collective-permute-start(bf16[128,256]{1,0:T(8,128)(2,1)S(1)} %get-tuple-element.29.x0), channel_id=1, source_target_pairs={{0,32},{4,36},{32,0},{36,4},{1,33},{5,37},{33,1},{37,5},{2,34},{6,... | collective-permute-start | bytes 196616 | tf_op jit(solution)/shard_map/moments/ppermute | solution.py:284
  6.4 0.0 collective-permute-start.1
  6.4 4.4 %collective-permute-start = (bf16[128,256]{1,0:T(8,128)(2,1)S(1)}, bf16[128,256]{1,0:T(8,128)(2,1)S(1)}, u32[]{:S(2)}, u32[]{:S(2)}) collective-permute-start(bf16[128,256]{1,0:T(8,128)(2,1)S(1)} %get-tuple-element.29.x0), channel_id=1, source_target_pairs={{0,3},{1,0},{2,1},{3,2},{32,35},{33,32},{34,33},{35,34},{4,7},{5,4... | collective-permute-start | bytes 196616 | tf_op jit(solution)/shard_map/moments/ppermute | solution.py:289
  10.8 13.1 %all_to_all.20.messages = f32[16,8,128]{2,1,0:T(8,128)S(1)} all-to-all(f32[16,8,128]{2,1,0:T(8,128)S(1)} %get-tuple-element.28), channel_id=1, replica_groups=mesh['x'=4,'z'=2,'y'=4,'c'=2,'g'=4] {'x','y'}, dimensions={0} | all-to-all | bytes 131072 | tf_op jit(solution)/shard_map/moments/all_to_all | solution.py:293
  23.9 0.0 collective-permute-done.3.x3
  23.9 0.0 collective-permute-done.2.x2
  23.9 0.0 collective-permute-done.1.x1
  23.9 0.0 collective-permute-done.shifted
  23.9 1.1 %group_sums.1 = (f32[8,128]{1,0:T(8,128)S(1)}, f32[16,128]{1,0:T(8,128)S(1)}, f32[16,128]{1,0:T(8,128)S(1)}, bf16[16,128,256]{2,1,0:T(8,128)(2,1)}) custom-call(f32[24,128]{1,0:T(8,128)S(1)} %get-tuple-element.27.frame, f32[16,8,128]{2,1,0:T(8,128)S(1)} %all_to_all.20.messages, bf16[128,256]{1,0:T(8,128)(2,1)S(1)} %collective-permute-done.shifted, ...), custom_call_target="tpu_custom_call" | custom-call | tf_op jit(solution)/shard_map/moments/group_sums/pallas_call | solution.py:321
  25.0 3.7 %all-to-all-start.1 = ((bf16[16,128,256]{2,1,0:T(8,128)(2,1)}), bf16[16,128,256]{2,1,0:T(8,128)(2,1)S(1)}, u32[]{:S(2)}, u32[]{:S(2)}) async-start(bf16[16,128,256]{2,1,0:T(8,128)(2,1)} %get-tuple-element.31), calls=%async_computation.1 | async-start | bytes 2097152 | tf_op jit(solution)/shard_map/gather/all_to_all | solution.py:293
  28.7 2.2 %collective-permute-start.4 = (f32[8,128]{1,0:T(8,128)S(1)}, f32[8,128]{1,0:T(8,128)S(1)}, u32[]{:S(2)}, u32[]{:S(2)}) collective-permute-start(f32[8,128]{1,0:T(8,128)S(1)} %get-tuple-element.32.mine), channel_id=1, source_target_pairs={{0,4},{4,0},{1,5},{5,1},{2,6},{6,2},{3,7},{7,3},{8,12},{12,8},{9,1... | collective-permute-start | bytes 12296 | tf_op jit(solution)/shard_map/gather/ppermute | solution.py:280
  30.9 1.2 %collective-permute-start.8 = (f32[16,128]{1,0:T(8,128)S(1)}, f32[16,128]{1,0:T(8,128)S(1)}, u32[]{:S(2)}, u32[]{:S(2)}) collective-permute-start(f32[16,128]{1,0:T(8,128)S(1)} %get-tuple-element.33), channel_id=1, source_target_pairs={{0,3},{1,0},{2,1},{3,2},{32,35},{33,32},{34,33},{35,34},{4,7},{5,4... | collective-permute-start | bytes 24584 | tf_op jit(solution)/shard_map/gather/ppermute | solution.py:289
  32.1 0.0 collective-permute-done.4.other
  32.1 0.4 collective-permute-start.7
  32.5 0.4 collective-permute-start.6
  32.9 1.2 %collective-permute-start.5 = (f32[8,128]{1,0:T(8,128)S(1)}, f32[8,128]{1,0:T(8,128)S(1)}, u32[]{:S(2)}, u32[]{:S(2)}) collective-permute-start(f32[8,128]{1,0:T(8,128)S(1)} %core_sums.1.mine), channel_id=1, source_target_pairs={{0,32},{32,0},{1,33},{33,1},{2,34},{34,2},{3,35},{35,3},{4,36},{36... | collective-permute-start | bytes 12296 | tf_op jit(solution)/shard_map/gather/ppermute | solution.py:280
  34.1 0.2 collective-permute-done.8.norms
  34.3 2.3 %collective-permute-done.7.back_across = f32[8,128]{1,0:T(8,128)S(1)} collective-permute-done((f32[8,128]{1,0:T(8,128)S(1)}, f32[8,128]{1,0:T(8,128)S(1)}, u32[]{:S(2)}, u32[]{:S(2)}) %collective-permute-start.7) | collective-permute-done | bytes 4128 | tf_op jit(solution)/shard_map/gather/ppermute | solution.py:289
  36.6 0.0 collective-permute-done.6.back
  36.6 0.0 collective-permute-done.5.across
  36.7 0.2 prepared.1
  36.8 6.7 %all-to-all-done.1.targets = bf16[16,128,256]{2,1,0:T(8,128)(2,1)S(1)} async-done(((bf16[16,128,256]{2,1,0:T(8,128)(2,1)}), bf16[16,128,256]{2,1,0:T(8,128)(2,1)S(1)}, u32[]{:S(2)}, u32[]{:S(2)}) %all-to-all-start.1) | async-done | bytes 1048608 | tf_op jit(solution)/shard_map/gather/all_to_all | solution.py:293
  43.5 2.5 %first_pass.1 = (f32[16,512,128]{2,1,0:T(8,128)S(1)}, f32[8,128]{1,0:T(8,128)S(1)}) custom-call(f32[24,128]{1,0:T(8,128)S(1)} %get-tuple-element.27.frame, bf16[16,128,256]{2,1,0:T(8,128)(2,1)S(1)} %all-to-all-done.1.targets, bf16[512,256]{1,0:T(8,128)(2,1)S(1)} %get-tuple-element.35.rows, f32[512,128]{1,0:T(8,128)S(1)} %get-tuple-element.36.weights, ...), custom_call_target="tpu_custom_call" | custom-call | tf_op jit(solution)/shard_map/first_rows/first_pass/pallas_call | solution.py:343
  46.0 3.9 %collective-permute-start.11 = (f32[8,128]{1,0:T(8,128)S(1)}, f32[8,128]{1,0:T(8,128)S(1)}, u32[]{:S(2)}, u32[]{:S(2)}) collective-permute-start(f32[8,128]{1,0:T(8,128)S(1)} %get-tuple-element.39.p0), channel_id=1, source_target_pairs={{0,36},{4,32},{32,4},{36,0},{1,37},{5,33},{33,5},{37,1},{2,38},{6,... | collective-permute-start | bytes 12296 | tf_op jit(solution)/shard_map/first_columns/ppermute | solution.py:284
  50.0 0.7 collective-permute-start.10
  50.7 0.0 collective-permute-start.9
  50.7 0.5 collective-permute-done.11.p3
  51.3 1.4 %collective-permute-done.10.p2 = f32[8,128]{1,0:T(8,128)S(1)} collective-permute-done((f32[8,128]{1,0:T(8,128)S(1)}, f32[8,128]{1,0:T(8,128)S(1)}, u32[]{:S(2)}, u32[]{:S(2)}) %collective-permute-start.10) | collective-permute-done | bytes 4128 | tf_op jit(solution)/shard_map/first_columns/ppermute | solution.py:284
  52.7 0.8 first_columns.1
  53.5 9.8 %all_to_all.21.parts = f32[16,16,128]{2,1,0:T(8,128)S(1)} all-to-all(f32[16,16,128]{2,1,0:T(8,128)S(1)} %get-tuple-element.42), channel_id=1, replica_groups=mesh['x'=4,'z'=2,'y'=4,'c'=2,'g'=4] {'x','y'}, dimensions={0} | all-to-all | bytes 262144 | tf_op jit(solution)/shard_map/first_columns/all_to_all | solution.py:293
  63.3 1.0 %second_rows.1.p0 = f32[4,128]{1,0:T(4,128)S(1)} custom-call(f32[24,128]{1,0:T(8,128)S(1)} %get-tuple-element.27.frame, f32[16,16,128]{2,1,0:T(8,128)S(1)} %all_to_all.21.parts, f32[16,512,128]{2,1,0:T(8,128)S(1)} %get-tuple-element.40.scores), custom_call_target="tpu_custom_call" | custom-call | tf_op jit(solution)/shard_map/second_rows/second_rows/pallas_call | solution.py:360
  64.3 2.5 %collective-permute-start.14 = (f32[4,128]{1,0:T(4,128)S(1)}, f32[4,128]{1,0:T(4,128)S(1)}, u32[]{:S(2)}, u32[]{:S(2)}) collective-permute-start(f32[4,128]{1,0:T(4,128)S(1)} %second_rows.1.p0), channel_id=1, source_target_pairs={{0,36},{4,32},{32,4},{36,0},{1,37},{5,33},{33,5},{37,1},{2,38},{6,... | collective-permute-start | bytes 6152 | tf_op jit(solution)/shard_map/last_columns/ppermute | solution.py:284
  66.8 0.7 collective-permute-start.13
  67.5 0.0 collective-permute-start.12
  67.5 0.5 collective-permute-done.14.p3
  68.1 1.4 %collective-permute-done.13.p2 = f32[4,128]{1,0:T(4,128)S(1)} collective-permute-done((f32[4,128]{1,0:T(4,128)S(1)}, f32[4,128]{1,0:T(4,128)S(1)}, u32[]{:S(2)}, u32[]{:S(2)}) %collective-permute-start.13) | collective-permute-done | bytes 2080 | tf_op jit(solution)/shard_map/last_columns/ppermute | solution.py:284
  69.5 0.0 collective-permute-done.12.p1
  69.5 0.8 last_columns.1
  70.3 9.8 %all_to_all.22.parts = f32[16,16,128]{2,1,0:T(8,128)S(1)} all-to-all(f32[16,16,128]{2,1,0:T(8,128)S(1)} %get-tuple-element.44), channel_id=1, replica_groups=mesh['x'=4,'z'=2,'y'=4,'c'=2,'g'=4] {'x','y'}, dimensions={0} | all-to-all | bytes 262144 | tf_op jit(solution)/shard_map/last_columns/all_to_all | solution.py:293
  80.1 1.0 %last_rows.1 = (f32[1,128]{1,0:T(1,128)S(1)}, f32[1,128]{1,0:T(1,128)S(1)}, f32[1,128]{1,0:T(1,128)S(1)}, f32[1,128]{1,0:T(1,128)S(1)}, f32[1,128]{1,0:T(1,128)S(1)}) custom-call(f32[24,128]{1,0:T(8,128)S(1)} %get-tuple-element.27.frame, f32[16,16,128]{2,1,0:T(8,128)S(1)} %all_to_all.22.parts, f32[16,512,128]{2,1,0:T(8,128)S(1)} %get-tuple-element.40.scores, ...), custom_call_target="tpu_custom_call" | custom-call | tf_op jit(solution)/shard_map/mass/last_rows/pallas_call | solution.py:373
  81.1 1.9 %collective-permute-start.15 = (f32[1,128]{1,0:T(1,128)S(1)}, f32[1,128]{1,0:T(1,128)S(1)}, u32[]{:S(2)}, u32[]{:S(2)}) collective-permute-start(f32[1,128]{1,0:T(1,128)S(1)} %get-tuple-element.48), channel_id=1, source_target_pairs={{0,4},{4,0},{32,36},{36,32},{1,5},{5,1},{33,37},{37,33},{2,6},{6,2... | collective-permute-start | bytes 1544 | tf_op jit(solution)/shard_map/mass/ppermute | solution.py:284
  83.0 0.8 collective-permute-start.16
  83.8 1.0 %collective-permute-start.17 = (f32[1,128]{1,0:T(1,128)S(1)}, f32[1,128]{1,0:T(1,128)S(1)}, u32[]{:S(2)}, u32[]{:S(2)}) collective-permute-start(f32[1,128]{1,0:T(1,128)S(1)} %get-tuple-element.50), channel_id=1, source_target_pairs={{0,36},{4,32},{32,4},{36,0},{1,37},{5,33},{33,5},{37,1},{2,38},{6,... | collective-permute-start | bytes 1544 | tf_op jit(solution)/shard_map/mass/ppermute | solution.py:284
  84.8 0.7 collective-permute-done.16.q2
  85.4 1.3 %collective-permute-done.17.q3 = f32[1,128]{1,0:T(1,128)S(1)} collective-permute-done((f32[1,128]{1,0:T(1,128)S(1)}, f32[1,128]{1,0:T(1,128)S(1)}, u32[]{:S(2)}, u32[]{:S(2)}) %collective-permute-start.17) | collective-permute-done | bytes 544 | tf_op jit(solution)/shard_map/mass/ppermute | solution.py:284
  86.8 0.5 outputs.1
  (3 shorter events, 0.0 us)
Async XLA Ops:
  1.7 22.1 %collective-permute-start.3 = (bf16[128,256]{1,0:T(8,128)(2,1)S(1)}, bf16[128,256]{1,0:T(8,128)(2,1)S(1)}, u32[]{:S(2)}, u32[]{:S(2)}) collective-permute-start(bf16[128,256]{1,0:T(8,128)(2,1)S(1)} %get-tuple-element.29.x0), channel_id=1, source_target_pairs={{0,36},{4,32},{32,4},{36,0},{1,37},{5,33},{33,5},{37,1},{2,38},{6,... | collective-permute-start | bytes 196616 | tf_op jit(solution)/shard_map/moments/ppermute | solution.py:284
  4.9 19.0 %collective-permute-start.2 = (bf16[128,256]{1,0:T(8,128)(2,1)S(1)}, bf16[128,256]{1,0:T(8,128)(2,1)S(1)}, u32[]{:S(2)}, u32[]{:S(2)}) collective-permute-start(bf16[128,256]{1,0:T(8,128)(2,1)S(1)} %get-tuple-element.29.x0), channel_id=1, source_target_pairs={{0,32},{4,36},{32,0},{36,4},{1,33},{5,37},{33,1},{37,5},{2,34},{6,... | collective-permute-start | bytes 196616 | tf_op jit(solution)/shard_map/moments/ppermute | solution.py:284
  6.4 17.5 %collective-permute-start.1 = (bf16[128,256]{1,0:T(8,128)(2,1)S(1)}, bf16[128,256]{1,0:T(8,128)(2,1)S(1)}, u32[]{:S(2)}, u32[]{:S(2)}) collective-permute-start(bf16[128,256]{1,0:T(8,128)(2,1)S(1)} %get-tuple-element.29.x0), channel_id=1, source_target_pairs={{0,4},{4,0},{32,36},{36,32},{1,5},{5,1},{33,37},{37,33},{2,6},{6,2... | collective-permute-start | bytes 196616 | tf_op jit(solution)/shard_map/moments/ppermute | solution.py:284
  6.4 17.5 %collective-permute-start = (bf16[128,256]{1,0:T(8,128)(2,1)S(1)}, bf16[128,256]{1,0:T(8,128)(2,1)S(1)}, u32[]{:S(2)}, u32[]{:S(2)}) collective-permute-start(bf16[128,256]{1,0:T(8,128)(2,1)S(1)} %get-tuple-element.29.x0), channel_id=1, source_target_pairs={{0,3},{1,0},{2,1},{3,2},{32,35},{33,32},{34,33},{35,34},{4,7},{5,4... | collective-permute-start | bytes 196616 | tf_op jit(solution)/shard_map/moments/ppermute | solution.py:289
  25.0 18.5 %all-to-all-start.1 = ((bf16[16,128,256]{2,1,0:T(8,128)(2,1)}), bf16[16,128,256]{2,1,0:T(8,128)(2,1)S(1)}, u32[]{:S(2)}, u32[]{:S(2)}) async-start(bf16[16,128,256]{2,1,0:T(8,128)(2,1)} %get-tuple-element.31), calls=%async_computation.1 | async-start | bytes 2097152 | tf_op jit(solution)/shard_map/gather/all_to_all | solution.py:293
  28.7 3.4 %collective-permute-start.4 = (f32[8,128]{1,0:T(8,128)S(1)}, f32[8,128]{1,0:T(8,128)S(1)}, u32[]{:S(2)}, u32[]{:S(2)}) collective-permute-start(f32[8,128]{1,0:T(8,128)S(1)} %get-tuple-element.32.mine), channel_id=1, source_target_pairs={{0,4},{4,0},{1,5},{5,1},{2,6},{6,2},{3,7},{7,3},{8,12},{12,8},{9,1... | collective-permute-start | bytes 12296 | tf_op jit(solution)/shard_map/gather/ppermute | solution.py:280
  30.9 3.4 %collective-permute-start.8 = (f32[16,128]{1,0:T(8,128)S(1)}, f32[16,128]{1,0:T(8,128)S(1)}, u32[]{:S(2)}, u32[]{:S(2)}) collective-permute-start(f32[16,128]{1,0:T(8,128)S(1)} %get-tuple-element.33), channel_id=1, source_target_pairs={{0,3},{1,0},{2,1},{3,2},{32,35},{33,32},{34,33},{35,34},{4,7},{5,4... | collective-permute-start | bytes 24584 | tf_op jit(solution)/shard_map/gather/ppermute | solution.py:289
  32.1 4.6 %collective-permute-start.7 = (f32[8,128]{1,0:T(8,128)S(1)}, f32[8,128]{1,0:T(8,128)S(1)}, u32[]{:S(2)}, u32[]{:S(2)}) collective-permute-start(f32[8,128]{1,0:T(8,128)S(1)} %core_sums.1.mine), channel_id=1, source_target_pairs={{0,35},{1,32},{2,33},{3,34},{32,3},{33,0},{34,1},{35,2},{4,39},{5,... | collective-permute-start | bytes 12296 | tf_op jit(solution)/shard_map/gather/ppermute | solution.py:289
  32.5 4.2 %collective-permute-start.6 = (f32[8,128]{1,0:T(8,128)S(1)}, f32[8,128]{1,0:T(8,128)S(1)}, u32[]{:S(2)}, u32[]{:S(2)}) collective-permute-start(f32[8,128]{1,0:T(8,128)S(1)} %core_sums.1.mine), channel_id=1, source_target_pairs={{0,3},{1,0},{2,1},{3,2},{32,35},{33,32},{34,33},{35,34},{4,7},{5,4... | collective-permute-start | bytes 12296 | tf_op jit(solution)/shard_map/gather/ppermute | solution.py:289
  32.9 3.7 %collective-permute-start.5 = (f32[8,128]{1,0:T(8,128)S(1)}, f32[8,128]{1,0:T(8,128)S(1)}, u32[]{:S(2)}, u32[]{:S(2)}) collective-permute-start(f32[8,128]{1,0:T(8,128)S(1)} %core_sums.1.mine), channel_id=1, source_target_pairs={{0,32},{32,0},{1,33},{33,1},{2,34},{34,2},{3,35},{35,3},{4,36},{36... | collective-permute-start | bytes 12296 | tf_op jit(solution)/shard_map/gather/ppermute | solution.py:280
  46.0 5.2 %collective-permute-start.11 = (f32[8,128]{1,0:T(8,128)S(1)}, f32[8,128]{1,0:T(8,128)S(1)}, u32[]{:S(2)}, u32[]{:S(2)}) collective-permute-start(f32[8,128]{1,0:T(8,128)S(1)} %get-tuple-element.39.p0), channel_id=1, source_target_pairs={{0,36},{4,32},{32,4},{36,0},{1,37},{5,33},{33,5},{37,1},{2,38},{6,... | collective-permute-start | bytes 12296 | tf_op jit(solution)/shard_map/first_columns/ppermute | solution.py:284
  50.0 2.7 %collective-permute-start.10 = (f32[8,128]{1,0:T(8,128)S(1)}, f32[8,128]{1,0:T(8,128)S(1)}, u32[]{:S(2)}, u32[]{:S(2)}) collective-permute-start(f32[8,128]{1,0:T(8,128)S(1)} %get-tuple-element.39.p0), channel_id=1, source_target_pairs={{0,32},{4,36},{32,0},{36,4},{1,33},{5,37},{33,1},{37,5},{2,34},{6,... | collective-permute-start | bytes 12296 | tf_op jit(solution)/shard_map/first_columns/ppermute | solution.py:284
  50.7 2.0 %collective-permute-start.9 = (f32[8,128]{1,0:T(8,128)S(1)}, f32[8,128]{1,0:T(8,128)S(1)}, u32[]{:S(2)}, u32[]{:S(2)}) collective-permute-start(f32[8,128]{1,0:T(8,128)S(1)} %get-tuple-element.39.p0), channel_id=1, source_target_pairs={{0,4},{4,0},{32,36},{36,32},{1,5},{5,1},{33,37},{37,33},{2,6},{6,2... | collective-permute-start | bytes 12296 | tf_op jit(solution)/shard_map/first_columns/ppermute | solution.py:284
  64.3 3.8 %collective-permute-start.14 = (f32[4,128]{1,0:T(4,128)S(1)}, f32[4,128]{1,0:T(4,128)S(1)}, u32[]{:S(2)}, u32[]{:S(2)}) collective-permute-start(f32[4,128]{1,0:T(4,128)S(1)} %second_rows.1.p0), channel_id=1, source_target_pairs={{0,36},{4,32},{32,4},{36,0},{1,37},{5,33},{33,5},{37,1},{2,38},{6,... | collective-permute-start | bytes 6152 | tf_op jit(solution)/shard_map/last_columns/ppermute | solution.py:284
  66.8 2.7 %collective-permute-start.13 = (f32[4,128]{1,0:T(4,128)S(1)}, f32[4,128]{1,0:T(4,128)S(1)}, u32[]{:S(2)}, u32[]{:S(2)}) collective-permute-start(f32[4,128]{1,0:T(4,128)S(1)} %second_rows.1.p0), channel_id=1, source_target_pairs={{0,32},{4,36},{32,0},{36,4},{1,33},{5,37},{33,1},{37,5},{2,34},{6,... | collective-permute-start | bytes 6152 | tf_op jit(solution)/shard_map/last_columns/ppermute | solution.py:284
  67.5 1.9 %collective-permute-start.12 = (f32[4,128]{1,0:T(4,128)S(1)}, f32[4,128]{1,0:T(4,128)S(1)}, u32[]{:S(2)}, u32[]{:S(2)}) collective-permute-start(f32[4,128]{1,0:T(4,128)S(1)} %second_rows.1.p0), channel_id=1, source_target_pairs={{0,4},{4,0},{32,36},{36,32},{1,5},{5,1},{33,37},{37,33},{2,6},{6,2... | collective-permute-start | bytes 6152 | tf_op jit(solution)/shard_map/last_columns/ppermute | solution.py:284
  81.1 3.6 %collective-permute-start.15 = (f32[1,128]{1,0:T(1,128)S(1)}, f32[1,128]{1,0:T(1,128)S(1)}, u32[]{:S(2)}, u32[]{:S(2)}) collective-permute-start(f32[1,128]{1,0:T(1,128)S(1)} %get-tuple-element.48), channel_id=1, source_target_pairs={{0,4},{4,0},{32,36},{36,32},{1,5},{5,1},{33,37},{37,33},{2,6},{6,2... | collective-permute-start | bytes 1544 | tf_op jit(solution)/shard_map/mass/ppermute | solution.py:284
  83.0 2.4 %collective-permute-start.16 = (f32[1,128]{1,0:T(1,128)S(1)}, f32[1,128]{1,0:T(1,128)S(1)}, u32[]{:S(2)}, u32[]{:S(2)}) collective-permute-start(f32[1,128]{1,0:T(1,128)S(1)} %get-tuple-element.49), channel_id=1, source_target_pairs={{0,32},{4,36},{32,0},{36,4},{1,33},{5,37},{33,1},{37,5},{2,34},{6,... | collective-permute-start | bytes 1544 | tf_op jit(solution)/shard_map/mass/ppermute | solution.py:284
  83.8 3.0 %collective-permute-start.17 = (f32[1,128]{1,0:T(1,128)S(1)}, f32[1,128]{1,0:T(1,128)S(1)}, u32[]{:S(2)}, u32[]{:S(2)}) collective-permute-start(f32[1,128]{1,0:T(1,128)S(1)} %get-tuple-element.50), channel_id=1, source_target_pairs={{0,36},{4,32},{32,4},{36,0},{1,37},{5,33},{33,5},{37,1},{2,38},{6,... | collective-permute-start | bytes 1544 | tf_op jit(solution)/shard_map/mass/ppermute | solution.py:284

commit v6 on v5

--- a/solution.py
+++ b/solution.py
@@ -62,11 +62,10 @@
 def own_sums(cells, present):
     kept = jnp.where(present, cells, 0.0)
     total = jnp.sum(kept, axis=0, keepdims=True)
-    squares = kept * kept
-    norm = jnp.sum(jnp.sum(squares, axis=0, keepdims=True), axis=1, keepdims=True)
-    squares = cells * cells
-    norms = jnp.sum((squares[:, :CELLS] + squares[:, CELLS:]).T, axis=0, keepdims=True)
-    return total[:, :CELLS], total[:, CELLS:], jnp.broadcast_to(norm, (1, CELLS)), norms
+    squares = jnp.sum(kept * kept, axis=0, keepdims=True)
+    norm = jnp.sum(squares, axis=1, keepdims=True)
+    zeros = jnp.zeros((1, CELLS), F32)
+    return total[:, :CELLS], total[:, CELLS:], jnp.broadcast_to(norm, (1, CELLS)), zeros
 
 
 def local_sums(
@@ -107,26 +106,25 @@
     frame[LAST_GROUP : LAST_GROUP + 1, :] = ones * (g == 3).astype(F32)
 
 
-def group_sums(frame, messages, shifted, last, x1, x2, x3, sums, norms, last_norms, copies):
+def parcel(frame, shifted, last, copies):
     is_last = frame[LAST_GROUP : LAST_GROUP + 1, :] > 0.0
     wide_last = jnp.concatenate([is_last, is_last], axis=1)
     targets = jnp.where(wide_last, last[...].astype(F32), shifted[...].astype(F32)).astype(BF16)
     for i in range(COLUMN_BLOCKS):
         copies[i] = targets
+
+
+def group_sums(messages, own, other, copies, sums, near, copies_out):
     sums[...] = jnp.sum(messages[...], axis=0)
-    for i in range(COLUMN_BLOCKS):
-        norms[i : i + 1, :] = messages[i, 3:4, :]
-        last_norms[i : i + 1, :] = messages[i, 7:8, :]
+    near[:CELLS, :] = own[...]
+    near[CELLS:, :] = other[...]
 
 
 def core_sums(mine, other, out):
     out[...] = mine[...] + other[...]
 
 
-def prepared(
-    frame, mine, across, back, back_across, norms, last_norms, x0, x1, x2, x3,
-    rows, weights, column_weights, twice,
-):
+def prepared(frame, mine, across, back, back_across, near, far, rows, weights, scales):
     is_last = frame[LAST_GROUP : LAST_GROUP + 1, :] > 0.0
     sources = mine[...] + across[...]
     targets = jnp.where(is_last, sources[4:8], (back[...] + back_across[...])[0:4])
@@ -136,10 +134,9 @@
     dot = jnp.sum(jnp.sum(products, axis=0, keepdims=True), axis=1, keepdims=True)
     spread = sources[2:3] / n_s + targets[2:3] / n_t - 2.0 * dot
     scale = LOG2E / (EPSILON * spread)
-    twice[...] = jnp.broadcast_to(2.0 * scale, twice.shape)
-    column_weights[...] = jnp.where(is_last, last_norms[...], norms[...]) * scale
-    for k, block in enumerate((x0[...], x1[...], x2[...], x3[...])):
-        at = slice(k * CELLS, (k + 1) * CELLS)
+    scales[...] = jnp.broadcast_to(scale, scales.shape)
+    for k, block in enumerate((near[...], far[...])):
+        at = slice(k * 2 * CELLS, (k + 1) * 2 * CELLS)
         rows[at, :] = block
         wide = block.astype(F32)
         weights[at, :] = jnp.sum(wide * wide, axis=1, keepdims=True) * scale
@@ -149,12 +146,11 @@
     return jnp.sum(part[k * CELLS : (k + 1) * CELLS, :].T, axis=0, keepdims=True)
 
 
-def first_pass(
-    frame, targets, rows, weights, column_weights, twice, scores, sums, part, limits
-):
+def first_pass(frame, targets, rows, weights, scales, scores, sums, part, limits):
     part[...] = jnp.zeros_like(part)
     limits[...] = jnp.where(frame[COLUMNS_AT : COLUMNS_AT + COLUMN_BLOCKS, :] > 0.0, 0.0, ABSENT)
-    factor = twice[0:1, :]
+    scale = scales[0:1, :]
+    twice = 2.0 * scale
 
     @pl.loop(0, COLUMN_BLOCKS // 2)
     def _(pair):
@@ -165,12 +161,14 @@
         )
         running = part[...]
         for half in range(2):
-            at = pl.ds(first + half, 1)
-            tile = (weights[...] + column_weights[at, :]) - factor * products[
+            wide = targets[first + half].astype(F32)
+            squares = wide * wide
+            norms = jnp.sum((squares[:, :CELLS] + squares[:, CELLS:]).T, axis=0, keepdims=True)
+            tile = (weights[...] + norms * scale) - twice * products[
                 :, half * CELLS : (half + 1) * CELLS
             ]
             scores[first + half] = tile
-            running = running + jnp.exp2(limits[at, :] - tile)
+            running = running + jnp.exp2(limits[pl.ds(first + half, 1), :] - tile)
         part[...] = running
 
     for k in range(ROW_BLOCKS):
@@ -285,7 +283,7 @@
 
 
 def back(value, k):
-    moves = [(z * 4 + g, (z ^ k) * 4 + (g - 1) % 4) for z in range(2) for g in range(4)]
+    moves = [(z * 4 + g, (z ^ k) * 4 + g - 1) for z in range(2) for g in range(1, 4)]
     return lax.ppermute(value, ("z", "g"), moves)
 
 
@@ -315,26 +313,36 @@
             space=pltpu.HBM,
             name="local_sums",
         )(*(in_hbm(a) for a in (features, last_features, growth, cell_counts)))
-        shifted = back(own, 0)
-        every_norm = shape(COLUMN_BLOCKS, CELLS)
-        sources = [across(own, k) for k in range(1, ROW_BLOCKS)]
-        sums, norms, last_norms, copies = call(
+        other = swapped(own, "c")
+        messages = exchanged(copies)
+    with jax.named_scope("gather"):
+        targets = call(parcel, shape(COLUMN_BLOCKS, CELLS, WIDTH, dtype=BF16), 3, name="parcel")(
+            frame, back(own, 0), last
+        )
+        anywhere = pl.BlockSpec(memory_space=pl.ANY)
+        vmem = pl.BlockSpec(memory_space=pltpu.VMEM)
+        sums, near, targets = pl.pallas_call(
             group_sums,
-            (row_parts, every_norm, every_norm, shape(COLUMN_BLOCKS, CELLS, WIDTH, dtype=BF16)),
-            4,
-            awaited=3,
+            out_shape=(
+                row_parts,
+                shape(2 * CELLS, WIDTH, dtype=BF16),
+                shape(COLUMN_BLOCKS, CELLS, WIDTH, dtype=BF16),
+            ),
+            in_specs=[vmem] * 3 + [anywhere],
+            out_specs=(vmem, vmem, anywhere),
+            input_output_aliases={3: 2},
+            compiler_params=pltpu.CompilerParams(vmem_limit_bytes=16 * 1024 * 1024),
             name="group_sums",
-        )(frame, exchanged(copies), shifted, last, *sources)
-    with jax.named_scope("gather"):
-        targets = exchanged(copies)
+        )(messages, own, other, targets)
+        targets = exchanged(targets)
         mine = call(core_sums, row_parts, 2, name="core_sums")(sums, swapped(sums, "c"))
         sums = (mine, swapped(mine, "z"), back(mine, 0), back(mine, 1))
         ready = call(
             prepared,
-            (shape(ROWS, WIDTH, dtype=BF16), shape(ROWS, CELLS), every_norm, shape(8, CELLS)),
-            11,
+            (shape(ROWS, WIDTH, dtype=BF16), shape(ROWS, CELLS), row_parts),
+            7,
             name="prepared",
-        )(frame, *sums, back(norms, 0), last_norms, own, *sources)
+        )(frame, *sums, near, swapped(near, "z"))
 
     def row_exchange(sums):
         return [sums] + [across(sums, k) for k in range(1, ROW_BLOCKS)]
@@ -343,7 +351,7 @@
         scores, sums = call(
             first_pass,
             (shape(COLUMN_BLOCKS, ROWS, CELLS), row_parts),
-            6,
+            5,
             (part, limits),
             name="first_pass",
         )(frame, targets, *ready)

time: 87.6 us -> 82.4 us (0.941)
  blocking collectives: 32.7 us -> 19.4 us
  waiting for transfers between devices: 15.2 us -> 20.7 us
  starting transfers between devices: 29.7 us -> 31.1 us
    all_to_all x3 -> x2, blocking collectives: 32.7 us -> 19.4 us  [exchanged(): lax.all_to_all(copies, COLUMN_AXES, split_axis=0, concat_axis=0, tiled=True)]
    all_to_all x1 -> x2, starting transfers between devices: 3.65 us -> 8.68 us  [exchanged(): lax.all_to_all(copies, COLUMN_AXES, split_axis=0, concat_axis=0, tiled=True)]
    ppermute x12 -> x9, starting transfers between devices: 16.3 us -> 11.7 us  [across(): return lax.ppermute(value, ROW_AXES, [(d, d ^ k) for d in range(4)])]
    ppermute x2 -> x4, starting transfers between devices: 3.37 us -> 6.88 us  [swapped(): return lax.ppermute(value, axis, [(0, 1), (1, 0)])]
    ppermute x4 -> x3, waiting for transfers between devices: 2.56 us -> 6.04 us  [back(): return lax.ppermute(value, ('z', 'g'), moves)]
    ppermute x4 -> x3, starting transfers between devices: 6.39 us -> 3.86 us  [back(): return lax.ppermute(value, ('z', 'g'), moves)]
    all_to_all x1 -> x2, waiting for transfers between devices: 6.69 us -> 7.43 us  [exchanged(): lax.all_to_all(copies, COLUMN_AXES, split_axis=0, concat_axis=0, tiled=True)]
    ppermute x12 -> x9, waiting for transfers between devices: 5.9 us -> 6.4 us  [across(): return lax.ppermute(value, ROW_AXES, [(d, d ^ k) for d in range(4)])]
  transfers between devices with their start and end apart: 19 -> 18, of which waited for: 9 -> 11; matrix products, arithmetic and copies ran while one was open for 0% -> 0% of each run, Pallas kernels for 0% -> 2%
where the time goes in v6:
time: 82.4 us; the launch traced here: 81.6 us
  starting transfers between devices  31.1 us (38%)
  waiting for transfers between devices  20.7 us (25%)
  blocking collectives  19.4 us (24%)
  Pallas kernels  9.68 us (12%)
    all_to_all x2, blocking collectives, exchanged(): lax.all_to_all(copies, COLUMN_AXES, split_axis=0, concat_axis=0, tiled=True)  19.4 us
    ppermute x9, starting transfers between devices, across(): return lax.ppermute(value, ROW_AXES, [(d, d ^ k) for d in range(4)])  11.7 us
    all_to_all x2, starting transfers between devices, exchanged(): lax.all_to_all(copies, COLUMN_AXES, split_axis=0, concat_axis=0, tiled=True)  8.68 us
    all_to_all x2, waiting for transfers between devices, exchanged(): lax.all_to_all(copies, COLUMN_AXES, split_axis=0, concat_axis=0, tiled=True)  7.43 us
    ppermute x4, starting transfers between devices, swapped(): return lax.ppermute(value, axis, [(0, 1), (1, 0)])  6.88 us
    ppermute x9, waiting for transfers between devices, across(): return lax.ppermute(value, ROW_AXES, [(d, d ^ k) for d in range(4)])  6.4 us
    ppermute x3, waiting for transfers between devices, back(): return lax.ppermute(value, ('z', 'g'), moves)  6.04 us
    ppermute x3, starting transfers between devices, back(): return lax.ppermute(value, ('z', 'g'), moves)  3.86 us
  transfers between devices with their start and end apart: 18, of which 11 were waited for; matrix products, arithmetic and copies ran while one was open for 0% of the time, Pallas kernels for 2%

profile of v6, /device:TPU:1, one launch (start us, length us, event | category | flops | bytes accessed | tf_op | source)
XLA Modules:
  0.0 81.6 jit_solution(16372094563105954331)
XLA Ops:
  0.6 1.7 %local_sums.1 = (f32[16,8,128]{2,1,0:T(8,128)}, bf16[128,256]{1,0:T(8,128)(2,1)S(1)}, bf16[128,256]{1,0:T(8,128)(2,1)S(1)}, f32[24,128]{1,0:T(8,128)S(1)}) custom-call(bf16[1,128,256]{2,1,0:T(8,128)(2,1)} %features.1, bf16[128,256]{1,0:T(8,128)(2,1)} %last.1, f32[1,128]{1,0:T(1,128)} %growth.1, s32[5]{0:T(128)} %counts.1), custom_call_target="tpu_custom_call" | custom-call | tf_op jit(solution)/shard_map/moments/local_sums/pallas_call | solution.py:302
  2.3 1.3 %collective-permute-start.1 = (bf16[128,256]{1,0:T(8,128)(2,1)S(1)}, bf16[128,256]{1,0:T(8,128)(2,1)S(1)}, u32[]{:S(2)}, u32[]{:S(2)}) collective-permute-start(bf16[128,256]{1,0:T(8,128)(2,1)S(1)} %get-tuple-element.27.own), channel_id=1, source_target_pairs={{1,0},{2,1},{3,2},{33,32},{34,33},{35,34},{5,4},{6,5},{7,6},{37,36... | collective-permute-start | bytes 196616 | tf_op jit(solution)/shard_map/gather/ppermute | solution.py:287
  3.6 3.3 %collective-permute-start = (bf16[128,256]{1,0:T(8,128)(2,1)S(1)}, bf16[128,256]{1,0:T(8,128)(2,1)S(1)}, u32[]{:S(2)}, u32[]{:S(2)}) collective-permute-start(bf16[128,256]{1,0:T(8,128)(2,1)S(1)} %get-tuple-element.27.own), channel_id=1, source_target_pairs={{0,4},{4,0},{1,5},{5,1},{2,6},{6,2},{3,7},{7,3},{8,12},{12,8},{9,1... | collective-permute-start | bytes 196616 | tf_op jit(solution)/shard_map/moments/ppermute | solution.py:278
  6.9 5.0 %all-to-all-start = ((f32[16,8,128]{2,1,0:T(8,128)}), f32[16,8,128]{2,1,0:T(8,128)S(1)}, u32[]{:S(2)}, u32[]{:S(2)}) async-start(f32[16,8,128]{2,1,0:T(8,128)} %get-tuple-element.26), calls=%async_computation | async-start | bytes 131072 | tf_op jit(solution)/shard_map/moments/all_to_all | solution.py:291
  12.0 0.0 collective-permute-done.1.shifted
  12.0 1.1 %parcel.1.copies = bf16[16,128,256]{2,1,0:T(8,128)(2,1)} custom-call(f32[24,128]{1,0:T(8,128)S(1)} %get-tuple-element.25.frame, bf16[128,256]{1,0:T(8,128)(2,1)S(1)} %collective-permute-done.1.shifted, bf16[128,256]{1,0:T(8,128)(2,1)S(1)} %get-tuple-element.28.last), custom_call_target="tpu_custom_call" | custom-call | tf_op jit(solution)/shard_map/gather/parcel/pallas_call | solution.py:319
  13.1 5.4 %all-to-all-done.messages = f32[16,8,128]{2,1,0:T(8,128)S(1)} async-done(((f32[16,8,128]{2,1,0:T(8,128)}), f32[16,8,128]{2,1,0:T(8,128)S(1)}, u32[]{:S(2)}, u32[]{:S(2)}) %all-to-all-start) | async-done | bytes 65568 | tf_op jit(solution)/shard_map/moments/all_to_all | solution.py:291
  18.5 0.0 collective-permute-done.other
  18.5 3.7 %all-to-all-start.1 = ((bf16[16,128,256]{2,1,0:T(8,128)(2,1)}), bf16[16,128,256]{2,1,0:T(8,128)(2,1)S(1)}, u32[]{:S(2)}, u32[]{:S(2)}) async-start(bf16[16,128,256]{2,1,0:T(8,128)(2,1)} %get-tuple-element.29), calls=%async_computation.1 | async-start | bytes 2097152 | tf_op jit(solution)/shard_map/gather/all_to_all | solution.py:291
  22.2 1.7 %collective-permute-start.6 = (bf16[256,256]{1,0:T(8,128)(2,1)S(1)}, bf16[256,256]{1,0:T(8,128)(2,1)S(1)}, u32[]{:S(2)}, u32[]{:S(2)}) collective-permute-start(bf16[256,256]{1,0:T(8,128)(2,1)S(1)} %get-tuple-element.31.near), channel_id=1, source_target_pairs={{0,32},{32,0},{1,33},{33,1},{2,34},{34,2},{3,35},{35,3},{4,36},{36... | collective-permute-start | bytes 393224 | tf_op jit(solution)/shard_map/gather/ppermute | solution.py:278
  23.9 1.7 %collective-permute-start.2 = (f32[8,128]{1,0:T(8,128)S(1)}, f32[8,128]{1,0:T(8,128)S(1)}, u32[]{:S(2)}, u32[]{:S(2)}) collective-permute-start(f32[8,128]{1,0:T(8,128)S(1)} %get-tuple-element.30.mine), channel_id=1, source_target_pairs={{0,4},{4,0},{1,5},{5,1},{2,6},{6,2},{3,7},{7,3},{8,12},{12,8},{9,1... | collective-permute-start | bytes 12296 | tf_op jit(solution)/shard_map/gather/ppermute | solution.py:278
  25.6 0.8 %collective-permute-done.2.other = f32[8,128]{1,0:T(8,128)S(1)} collective-permute-done((f32[8,128]{1,0:T(8,128)S(1)}, f32[8,128]{1,0:T(8,128)S(1)}, u32[]{:S(2)}, u32[]{:S(2)}) %collective-permute-start.2) | collective-permute-done | bytes 4128 | tf_op jit(solution)/shard_map/gather/ppermute | solution.py:278
  26.5 1.3 %collective-permute-start.5 = (f32[8,128]{1,0:T(8,128)S(1)}, f32[8,128]{1,0:T(8,128)S(1)}, u32[]{:S(2)}, u32[]{:S(2)}) collective-permute-start(f32[8,128]{1,0:T(8,128)S(1)} %core_sums.1.mine), channel_id=1, source_target_pairs={{1,32},{2,33},{3,34},{33,0},{34,1},{35,2},{5,36},{6,37},{7,38},{37... | collective-permute-start | bytes 12296 | tf_op jit(solution)/shard_map/gather/ppermute | solution.py:287
  27.8 1.3 %collective-permute-start.4 = (f32[8,128]{1,0:T(8,128)S(1)}, f32[8,128]{1,0:T(8,128)S(1)}, u32[]{:S(2)}, u32[]{:S(2)}) collective-permute-start(f32[8,128]{1,0:T(8,128)S(1)} %core_sums.1.mine), channel_id=1, source_target_pairs={{1,0},{2,1},{3,2},{33,32},{34,33},{35,34},{5,4},{6,5},{7,6},{37,36... | collective-permute-start | bytes 12296 | tf_op jit(solution)/shard_map/gather/ppermute | solution.py:287
  29.1 0.1 collective-permute-start.3
  29.2 3.7 %collective-permute-done.5.back_across = f32[8,128]{1,0:T(8,128)S(1)} collective-permute-done((f32[8,128]{1,0:T(8,128)S(1)}, f32[8,128]{1,0:T(8,128)S(1)}, u32[]{:S(2)}, u32[]{:S(2)}) %collective-permute-start.5) | collective-permute-done | bytes 4128 | tf_op jit(solution)/shard_map/gather/ppermute | solution.py:287
  32.9 2.3 %collective-permute-done.4.back = f32[8,128]{1,0:T(8,128)S(1)} collective-permute-done((f32[8,128]{1,0:T(8,128)S(1)}, f32[8,128]{1,0:T(8,128)S(1)}, u32[]{:S(2)}, u32[]{:S(2)}) %collective-permute-start.4) | collective-permute-done | bytes 4128 | tf_op jit(solution)/shard_map/gather/ppermute | solution.py:287
  35.2 0.0 collective-permute-done.3.across
  35.2 0.0 collective-permute-done.6.far
  35.2 0.2 prepared.1
  35.4 2.0 %all-to-all-done.1.targets = bf16[16,128,256]{2,1,0:T(8,128)(2,1)S(1)} async-done(((bf16[16,128,256]{2,1,0:T(8,128)(2,1)}), bf16[16,128,256]{2,1,0:T(8,128)(2,1)S(1)}, u32[]{:S(2)}, u32[]{:S(2)}) %all-to-all-start.1) | async-done | bytes 1048608 | tf_op jit(solution)/shard_map/gather/all_to_all | solution.py:291
  37.4 2.5 %first_pass.1 = (f32[16,512,128]{2,1,0:T(8,128)S(1)}, f32[8,128]{1,0:T(8,128)S(1)}) custom-call(f32[24,128]{1,0:T(8,128)S(1)} %get-tuple-element.25.frame, bf16[16,128,256]{2,1,0:T(8,128)(2,1)S(1)} %all-to-all-done.1.targets, bf16[512,256]{1,0:T(8,128)(2,1)S(1)} %get-tuple-element.32.rows, f32[512,128]{1,0:T(8,128)S(1)} %get-tuple-element.33.weights, ...), custom_call_target="tpu_custom_call" | custom-call | tf_op jit(solution)/shard_map/first_rows/first_pass/pallas_call | solution.py:351
  40.0 4.7 %collective-permute-start.9 = (f32[8,128]{1,0:T(8,128)S(1)}, f32[8,128]{1,0:T(8,128)S(1)}, u32[]{:S(2)}, u32[]{:S(2)}) collective-permute-start(f32[8,128]{1,0:T(8,128)S(1)} %get-tuple-element.35.p0), channel_id=1, source_target_pairs={{0,36},{4,32},{32,4},{36,0},{1,37},{5,33},{33,5},{37,1},{2,38},{6,... | collective-permute-start | bytes 12296 | tf_op jit(solution)/shard_map/first_columns/ppermute | solution.py:282
  44.7 0.0 collective-permute-start.8
  44.7 0.5 collective-permute-start.7
  45.2 0.8 collective-permute-done.9.p3
  46.0 1.2 %collective-permute-done.8.p2 = f32[8,128]{1,0:T(8,128)S(1)} collective-permute-done((f32[8,128]{1,0:T(8,128)S(1)}, f32[8,128]{1,0:T(8,128)S(1)}, u32[]{:S(2)}, u32[]{:S(2)}) %collective-permute-start.8) | collective-permute-done | bytes 4128 | tf_op jit(solution)/shard_map/first_columns/ppermute | solution.py:282
  47.1 0.0 collective-permute-done.7.p1
  47.1 0.8 %first_columns.1 = (f32[4,128]{1,0:T(4,128)S(1)}, f32[16,16,128]{2,1,0:T(8,128)S(1)}) custom-call(f32[24,128]{1,0:T(8,128)S(1)} %get-tuple-element.25.frame, f32[8,128]{1,0:T(8,128)S(1)} %get-tuple-element.35.p0, f32[8,128]{1,0:T(8,128)S(1)} %collective-permute-done.7.p1, f32[8,128]{1,0:T(8,128)S(1)} %collective-permute-done.8.p2, ...), custom_call_target="tpu_custom_call" | custom-call | tf_op jit(solution)/shard_map/first_columns/first_columns/pallas_call | solution.py:359
  48.0 9.5 %all_to_all.20.parts = f32[16,16,128]{2,1,0:T(8,128)S(1)} all-to-all(f32[16,16,128]{2,1,0:T(8,128)S(1)} %get-tuple-element.38), channel_id=1, replica_groups=mesh['x'=4,'z'=2,'y'=4,'c'=2,'g'=4] {'x','y'}, dimensions={0} | all-to-all | bytes 262144 | tf_op jit(solution)/shard_map/first_columns/all_to_all | solution.py:291
  57.5 1.0 %second_rows.1.p0 = f32[4,128]{1,0:T(4,128)S(1)} custom-call(f32[24,128]{1,0:T(8,128)S(1)} %get-tuple-element.25.frame, f32[16,16,128]{2,1,0:T(8,128)S(1)} %all_to_all.20.parts, f32[16,512,128]{2,1,0:T(8,128)S(1)} %get-tuple-element.36.scores), custom_call_target="tpu_custom_call" | custom-call | tf_op jit(solution)/shard_map/second_rows/second_rows/pallas_call | solution.py:368
  58.5 2.7 %collective-permute-start.12 = (f32[4,128]{1,0:T(4,128)S(1)}, f32[4,128]{1,0:T(4,128)S(1)}, u32[]{:S(2)}, u32[]{:S(2)}) collective-permute-start(f32[4,128]{1,0:T(4,128)S(1)} %second_rows.1.p0), channel_id=1, source_target_pairs={{0,36},{4,32},{32,4},{36,0},{1,37},{5,33},{33,5},{37,1},{2,38},{6,... | collective-permute-start | bytes 6152 | tf_op jit(solution)/shard_map/last_columns/ppermute | solution.py:282
  61.1 0.1 collective-permute-start.11
  61.2 0.4 collective-permute-start.10
  61.7 0.8 %collective-permute-done.12.p3 = f32[4,128]{1,0:T(4,128)S(1)} collective-permute-done((f32[4,128]{1,0:T(4,128)S(1)}, f32[4,128]{1,0:T(4,128)S(1)}, u32[]{:S(2)}, u32[]{:S(2)}) %collective-permute-start.12) | collective-permute-done | bytes 2080 | tf_op jit(solution)/shard_map/last_columns/ppermute | solution.py:282
  62.5 1.1 %collective-permute-done.11.p2 = f32[4,128]{1,0:T(4,128)S(1)} collective-permute-done((f32[4,128]{1,0:T(4,128)S(1)}, f32[4,128]{1,0:T(4,128)S(1)}, u32[]{:S(2)}, u32[]{:S(2)}) %collective-permute-start.11) | collective-permute-done | bytes 2080 | tf_op jit(solution)/shard_map/last_columns/ppermute | solution.py:282
  63.6 0.0 collective-permute-done.10.p1
  63.6 0.8 %last_columns.1 = (f32[4,128]{1,0:T(4,128)S(1)}, f32[1,128]{1,0:T(1,128)S(1)}, f32[16,16,128]{2,1,0:T(8,128)S(1)}) custom-call(f32[24,128]{1,0:T(8,128)S(1)} %get-tuple-element.25.frame, f32[4,128]{1,0:T(4,128)S(1)} %get-tuple-element.37.log_p, f32[4,128]{1,0:T(4,128)S(1)} %second_rows.1.p0, f32[4,128]{1,0:T(4,128)S(1)} %collective-permute-done.10.p1, ...), custom_call_target="tpu_custom_call" | custom-call | tf_op jit(solution)/shard_map/last_columns/last_columns/pallas_call | solution.py:372
  64.4 9.9 %all_to_all.21.parts = f32[16,16,128]{2,1,0:T(8,128)S(1)} all-to-all(f32[16,16,128]{2,1,0:T(8,128)S(1)} %get-tuple-element.40), channel_id=1, replica_groups=mesh['x'=4,'z'=2,'y'=4,'c'=2,'g'=4] {'x','y'}, dimensions={0} | all-to-all | bytes 262144 | tf_op jit(solution)/shard_map/last_columns/all_to_all | solution.py:291
  74.3 1.0 %last_rows.1 = (f32[1,128]{1,0:T(1,128)S(1)}, f32[1,128]{1,0:T(1,128)S(1)}, f32[1,128]{1,0:T(1,128)S(1)}, f32[1,128]{1,0:T(1,128)S(1)}, f32[1,128]{1,0:T(1,128)S(1)}) custom-call(f32[24,128]{1,0:T(8,128)S(1)} %get-tuple-element.25.frame, f32[16,16,128]{2,1,0:T(8,128)S(1)} %all_to_all.21.parts, f32[16,512,128]{2,1,0:T(8,128)S(1)} %get-tuple-element.36.scores, ...), custom_call_target="tpu_custom_call" | custom-call | tf_op jit(solution)/shard_map/mass/last_rows/pallas_call | solution.py:381
  75.3 1.6 %collective-permute-start.13 = (f32[1,128]{1,0:T(1,128)S(1)}, f32[1,128]{1,0:T(1,128)S(1)}, u32[]{:S(2)}, u32[]{:S(2)}) collective-permute-start(f32[1,128]{1,0:T(1,128)S(1)} %get-tuple-element.44), channel_id=1, source_target_pairs={{0,4},{4,0},{32,36},{36,32},{1,5},{5,1},{33,37},{37,33},{2,6},{6,2... | collective-permute-start | bytes 1544 | tf_op jit(solution)/shard_map/mass/ppermute | solution.py:282
  76.9 1.3 %collective-permute-start.14 = (f32[1,128]{1,0:T(1,128)S(1)}, f32[1,128]{1,0:T(1,128)S(1)}, u32[]{:S(2)}, u32[]{:S(2)}) collective-permute-start(f32[1,128]{1,0:T(1,128)S(1)} %get-tuple-element.45), channel_id=1, source_target_pairs={{0,32},{4,36},{32,0},{36,4},{1,33},{5,37},{33,1},{37,5},{2,34},{6,... | collective-permute-start | bytes 1544 | tf_op jit(solution)/shard_map/mass/ppermute | solution.py:282
  78.1 0.4 collective-permute-start.15
  78.6 0.0 collective-permute-done.13.q1
  78.6 0.7 collective-permute-done.14.q2
  79.3 1.8 %collective-permute-done.15.q3 = f32[1,128]{1,0:T(1,128)S(1)} collective-permute-done((f32[1,128]{1,0:T(1,128)S(1)}, f32[1,128]{1,0:T(1,128)S(1)}, u32[]{:S(2)}, u32[]{:S(2)}) %collective-permute-start.15) | collective-permute-done | bytes 544 | tf_op jit(solution)/shard_map/mass/ppermute | solution.py:282
  81.1 0.5 outputs.1
  (2 shorter events, 0.0 us)
Async XLA Ops:
  2.3 9.7 %collective-permute-start.1 = (bf16[128,256]{1,0:T(8,128)(2,1)S(1)}, bf16[128,256]{1,0:T(8,128)(2,1)S(1)}, u32[]{:S(2)}, u32[]{:S(2)}) collective-permute-start(bf16[128,256]{1,0:T(8,128)(2,1)S(1)} %get-tuple-element.27.own), channel_id=1, source_target_pairs={{1,0},{2,1},{3,2},{33,32},{34,33},{35,34},{5,4},{6,5},{7,6},{37,36... | collective-permute-start | bytes 196616 | tf_op jit(solution)/shard_map/gather/ppermute | solution.py:287
  3.6 14.9 %collective-permute-start = (bf16[128,256]{1,0:T(8,128)(2,1)S(1)}, bf16[128,256]{1,0:T(8,128)(2,1)S(1)}, u32[]{:S(2)}, u32[]{:S(2)}) collective-permute-start(bf16[128,256]{1,0:T(8,128)(2,1)S(1)} %get-tuple-element.27.own), channel_id=1, source_target_pairs={{0,4},{4,0},{1,5},{5,1},{2,6},{6,2},{3,7},{7,3},{8,12},{12,8},{9,1... | collective-permute-start | bytes 196616 | tf_op jit(solution)/shard_map/moments/ppermute | solution.py:278
  6.9 11.5 %all-to-all-start = ((f32[16,8,128]{2,1,0:T(8,128)}), f32[16,8,128]{2,1,0:T(8,128)S(1)}, u32[]{:S(2)}, u32[]{:S(2)}) async-start(f32[16,8,128]{2,1,0:T(8,128)} %get-tuple-element.26), calls=%async_computation | async-start | bytes 131072 | tf_op jit(solution)/shard_map/moments/all_to_all | solution.py:291
  18.5 18.9 %all-to-all-start.1 = ((bf16[16,128,256]{2,1,0:T(8,128)(2,1)}), bf16[16,128,256]{2,1,0:T(8,128)(2,1)S(1)}, u32[]{:S(2)}, u32[]{:S(2)}) async-start(bf16[16,128,256]{2,1,0:T(8,128)(2,1)} %get-tuple-element.29), calls=%async_computation.1 | async-start | bytes 2097152 | tf_op jit(solution)/shard_map/gather/all_to_all | solution.py:291
  22.2 13.0 %collective-permute-start.6 = (bf16[256,256]{1,0:T(8,128)(2,1)S(1)}, bf16[256,256]{1,0:T(8,128)(2,1)S(1)}, u32[]{:S(2)}, u32[]{:S(2)}) collective-permute-start(bf16[256,256]{1,0:T(8,128)(2,1)S(1)} %get-tuple-element.31.near), channel_id=1, source_target_pairs={{0,32},{32,0},{1,33},{33,1},{2,34},{34,2},{3,35},{35,3},{4,36},{36... | collective-permute-start | bytes 393224 | tf_op jit(solution)/shard_map/gather/ppermute | solution.py:278
  23.9 2.6 %collective-permute-start.2 = (f32[8,128]{1,0:T(8,128)S(1)}, f32[8,128]{1,0:T(8,128)S(1)}, u32[]{:S(2)}, u32[]{:S(2)}) collective-permute-start(f32[8,128]{1,0:T(8,128)S(1)} %get-tuple-element.30.mine), channel_id=1, source_target_pairs={{0,4},{4,0},{1,5},{5,1},{2,6},{6,2},{3,7},{7,3},{8,12},{12,8},{9,1... | collective-permute-start | bytes 12296 | tf_op jit(solution)/shard_map/gather/ppermute | solution.py:278
  26.5 6.4 %collective-permute-start.5 = (f32[8,128]{1,0:T(8,128)S(1)}, f32[8,128]{1,0:T(8,128)S(1)}, u32[]{:S(2)}, u32[]{:S(2)}) collective-permute-start(f32[8,128]{1,0:T(8,128)S(1)} %core_sums.1.mine), channel_id=1, source_target_pairs={{1,32},{2,33},{3,34},{33,0},{34,1},{35,2},{5,36},{6,37},{7,38},{37... | collective-permute-start | bytes 12296 | tf_op jit(solution)/shard_map/gather/ppermute | solution.py:287
  27.8 7.4 %collective-permute-start.4 = (f32[8,128]{1,0:T(8,128)S(1)}, f32[8,128]{1,0:T(8,128)S(1)}, u32[]{:S(2)}, u32[]{:S(2)}) collective-permute-start(f32[8,128]{1,0:T(8,128)S(1)} %core_sums.1.mine), channel_id=1, source_target_pairs={{1,0},{2,1},{3,2},{33,32},{34,33},{35,34},{5,4},{6,5},{7,6},{37,36... | collective-permute-start | bytes 12296 | tf_op jit(solution)/shard_map/gather/ppermute | solution.py:287
  29.1 6.1 %collective-permute-start.3 = (f32[8,128]{1,0:T(8,128)S(1)}, f32[8,128]{1,0:T(8,128)S(1)}, u32[]{:S(2)}, u32[]{:S(2)}) collective-permute-start(f32[8,128]{1,0:T(8,128)S(1)} %core_sums.1.mine), channel_id=1, source_target_pairs={{0,32},{32,0},{1,33},{33,1},{2,34},{34,2},{3,35},{35,3},{4,36},{36... | collective-permute-start | bytes 12296 | tf_op jit(solution)/shard_map/gather/ppermute | solution.py:278
  40.0 6.0 %collective-permute-start.9 = (f32[8,128]{1,0:T(8,128)S(1)}, f32[8,128]{1,0:T(8,128)S(1)}, u32[]{:S(2)}, u32[]{:S(2)}) collective-permute-start(f32[8,128]{1,0:T(8,128)S(1)} %get-tuple-element.35.p0), channel_id=1, source_target_pairs={{0,36},{4,32},{32,4},{36,0},{1,37},{5,33},{33,5},{37,1},{2,38},{6,... | collective-permute-start | bytes 12296 | tf_op jit(solution)/shard_map/first_columns/ppermute | solution.py:282
  44.7 2.5 %collective-permute-start.8 = (f32[8,128]{1,0:T(8,128)S(1)}, f32[8,128]{1,0:T(8,128)S(1)}, u32[]{:S(2)}, u32[]{:S(2)}) collective-permute-start(f32[8,128]{1,0:T(8,128)S(1)} %get-tuple-element.35.p0), channel_id=1, source_target_pairs={{0,32},{4,36},{32,0},{36,4},{1,33},{5,37},{33,1},{37,5},{2,34},{6,... | collective-permute-start | bytes 12296 | tf_op jit(solution)/shard_map/first_columns/ppermute | solution.py:282
  44.7 2.5 %collective-permute-start.7 = (f32[8,128]{1,0:T(8,128)S(1)}, f32[8,128]{1,0:T(8,128)S(1)}, u32[]{:S(2)}, u32[]{:S(2)}) collective-permute-start(f32[8,128]{1,0:T(8,128)S(1)} %get-tuple-element.35.p0), channel_id=1, source_target_pairs={{0,4},{4,0},{32,36},{36,32},{1,5},{5,1},{33,37},{37,33},{2,6},{6,2... | collective-permute-start | bytes 12296 | tf_op jit(solution)/shard_map/first_columns/ppermute | solution.py:282
  58.5 4.0 %collective-permute-start.12 = (f32[4,128]{1,0:T(4,128)S(1)}, f32[4,128]{1,0:T(4,128)S(1)}, u32[]{:S(2)}, u32[]{:S(2)}) collective-permute-start(f32[4,128]{1,0:T(4,128)S(1)} %second_rows.1.p0), channel_id=1, source_target_pairs={{0,36},{4,32},{32,4},{36,0},{1,37},{5,33},{33,5},{37,1},{2,38},{6,... | collective-permute-start | bytes 6152 | tf_op jit(solution)/shard_map/last_columns/ppermute | solution.py:282
  61.1 2.4 %collective-permute-start.11 = (f32[4,128]{1,0:T(4,128)S(1)}, f32[4,128]{1,0:T(4,128)S(1)}, u32[]{:S(2)}, u32[]{:S(2)}) collective-permute-start(f32[4,128]{1,0:T(4,128)S(1)} %second_rows.1.p0), channel_id=1, source_target_pairs={{0,32},{4,36},{32,0},{36,4},{1,33},{5,37},{33,1},{37,5},{2,34},{6,... | collective-permute-start | bytes 6152 | tf_op jit(solution)/shard_map/last_columns/ppermute | solution.py:282
  61.2 2.3 %collective-permute-start.10 = (f32[4,128]{1,0:T(4,128)S(1)}, f32[4,128]{1,0:T(4,128)S(1)}, u32[]{:S(2)}, u32[]{:S(2)}) collective-permute-start(f32[4,128]{1,0:T(4,128)S(1)} %second_rows.1.p0), channel_id=1, source_target_pairs={{0,4},{4,0},{32,36},{36,32},{1,5},{5,1},{33,37},{37,33},{2,6},{6,2... | collective-permute-start | bytes 6152 | tf_op jit(solution)/shard_map/last_columns/ppermute | solution.py:282
  75.3 3.3 %collective-permute-start.13 = (f32[1,128]{1,0:T(1,128)S(1)}, f32[1,128]{1,0:T(1,128)S(1)}, u32[]{:S(2)}, u32[]{:S(2)}) collective-permute-start(f32[1,128]{1,0:T(1,128)S(1)} %get-tuple-element.44), channel_id=1, source_target_pairs={{0,4},{4,0},{32,36},{36,32},{1,5},{5,1},{33,37},{37,33},{2,6},{6,2... | collective-permute-start | bytes 1544 | tf_op jit(solution)/shard_map/mass/ppermute | solution.py:282
  76.9 2.4 %collective-permute-start.14 = (f32[1,128]{1,0:T(1,128)S(1)}, f32[1,128]{1,0:T(1,128)S(1)}, u32[]{:S(2)}, u32[]{:S(2)}) collective-permute-start(f32[1,128]{1,0:T(1,128)S(1)} %get-tuple-element.45), channel_id=1, source_target_pairs={{0,32},{4,36},{32,0},{36,4},{1,33},{5,37},{33,1},{37,5},{2,34},{6,... | collective-permute-start | bytes 1544 | tf_op jit(solution)/shard_map/mass/ppermute | solution.py:282
  78.1 3.0 %collective-permute-start.15 = (f32[1,128]{1,0:T(1,128)S(1)}, f32[1,128]{1,0:T(1,128)S(1)}, u32[]{:S(2)}, u32[]{:S(2)}) collective-permute-start(f32[1,128]{1,0:T(1,128)S(1)} %get-tuple-element.46), channel_id=1, source_target_pairs={{0,36},{4,32},{32,4},{36,0},{1,37},{5,33},{33,5},{37,1},{2,38},{6,... | collective-permute-start | bytes 1544 | tf_op jit(solution)/shard_map/mass/ppermute | solution.py:282

commit v7 on v6

--- a/solution.py
+++ b/solution.py
@@ -114,14 +114,15 @@
         copies[i] = targets
 
 
-def group_sums(messages, own, other, copies, sums, near, copies_out):
+def group_sums(messages, own, copies, sums, own_out, copies_out):
     sums[...] = jnp.sum(messages[...], axis=0)
+    own_out[...] = own[...]
+
+
+def core_sums(mine, other, own, other_own, out, near):
+    out[...] = mine[...] + other[...]
     near[:CELLS, :] = own[...]
-    near[CELLS:, :] = other[...]
-
-
-def core_sums(mine, other, out):
-    out[...] = mine[...] + other[...]
+    near[CELLS:, :] = other_own[...]
 
 
 def prepared(frame, mine, across, back, back_across, near, far, rows, weights, scales):
@@ -313,7 +314,6 @@
             space=pltpu.HBM,
             name="local_sums",
         )(*(in_hbm(a) for a in (features, last_features, growth, cell_counts)))
-        other = swapped(own, "c")
         messages = exchanged(copies)
     with jax.named_scope("gather"):
         targets = call(parcel, shape(COLUMN_BLOCKS, CELLS, WIDTH, dtype=BF16), 3, name="parcel")(
@@ -321,22 +321,24 @@
         )
         anywhere = pl.BlockSpec(memory_space=pl.ANY)
         vmem = pl.BlockSpec(memory_space=pltpu.VMEM)
-        sums, near, targets = pl.pallas_call(
+        sums, own, targets = pl.pallas_call(
             group_sums,
             out_shape=(
                 row_parts,
-                shape(2 * CELLS, WIDTH, dtype=BF16),
+                some_cells,
                 shape(COLUMN_BLOCKS, CELLS, WIDTH, dtype=BF16),
             ),
-            in_specs=[vmem] * 3 + [anywhere],
+            in_specs=[vmem] * 2 + [anywhere],
             out_specs=(vmem, vmem, anywhere),
-            input_output_aliases={3: 2},
+            input_output_aliases={2: 2},
             compiler_params=pltpu.CompilerParams(vmem_limit_bytes=16 * 1024 * 1024),
             name="group_sums",
-        )(messages, own, other, targets)
+        )(messages, own, targets)
         targets = exchanged(targets)
-        mine = call(core_sums, row_parts, 2, name="core_sums")(sums, swapped(sums, "c"))
-        sums = (mine, swapped(mine, "z"), back(mine, 0), back(mine, 1))
+        sums, near = call(
+            core_sums, (row_parts, shape(2 * CELLS, WIDTH, dtype=BF16)), 4, name="core_sums"
+        )(sums, swapped(sums, "c"), own, swapped(own, "c"))
+        sums = (sums, swapped(sums, "z"), back(sums, 0), back(sums, 1))
         ready = call(
             prepared,
             (shape(ROWS, WIDTH, dtype=BF16), shape(ROWS, CELLS), row_parts),

time: 82.4 us -> 81.4 us (0.988)
  waiting for transfers between devices: 20.7 us -> 19.6 us
    ppermute x4, starting transfers between devices: 6.88 us -> 4.13 us  [swapped(): return lax.ppermute(value, axis, [(0, 1), (1, 0)])]
    all_to_all x2, starting transfers between devices: 8.68 us -> 11.3 us  [exchanged(): lax.all_to_all(copies, COLUMN_AXES, split_axis=0, concat_axis=0, tiled=True)]
    all_to_all x2, waiting for transfers between devices: 7.43 us -> 6.18 us  [exchanged(): lax.all_to_all(copies, COLUMN_AXES, split_axis=0, concat_axis=0, tiled=True)]
where the time goes in v7:
time: 81.4 us; the launch traced here: 80.9 us
  starting transfers between devices  31.3 us (38%)
  blocking collectives  19.7 us (24%)
  waiting for transfers between devices  19.6 us (24%)
  Pallas kernels  9.63 us (12%)
    all_to_all x2, blocking collectives, exchanged(): lax.all_to_all(copies, COLUMN_AXES, split_axis=0, concat_axis=0, tiled=True)  19.7 us
    ppermute x9, starting transfers between devices, across(): return lax.ppermute(value, ROW_AXES, [(d, d ^ k) for d in range(4)])  12 us
    all_to_all x2, starting transfers between devices, exchanged(): lax.all_to_all(copies, COLUMN_AXES, split_axis=0, concat_axis=0, tiled=True)  11.3 us
    ppermute x9, waiting for transfers between devices, across(): return lax.ppermute(value, ROW_AXES, [(d, d ^ k) for d in range(4)])  6.29 us
    all_to_all x2, waiting for transfers between devices, exchanged(): lax.all_to_all(copies, COLUMN_AXES, split_axis=0, concat_axis=0, tiled=True)  6.18 us
    ppermute x3, waiting for transfers between devices, back(): return lax.ppermute(value, ('z', 'g'), moves)  6.03 us
    ppermute x4, starting transfers between devices, swapped(): return lax.ppermute(value, axis, [(0, 1), (1, 0)])  4.13 us
    ppermute x3, starting transfers between devices, back(): return lax.ppermute(value, ('z', 'g'), moves)  3.86 us
  transfers between devices with their start and end apart: 18, of which 11 were waited for; matrix products, arithmetic and copies ran while one was open for 0% of the time, Pallas kernels for 2%

profile of v7, /device:TPU:1, one launch (start us, length us, event | category | flops | bytes accessed | tf_op | source)
XLA Modules:
  0.0 80.9 jit_solution(18445077401040477013)
XLA Ops:
  0.6 1.7 %local_sums.1 = (f32[16,8,128]{2,1,0:T(8,128)}, bf16[128,256]{1,0:T(8,128)(2,1)S(1)}, bf16[128,256]{1,0:T(8,128)(2,1)S(1)}, f32[24,128]{1,0:T(8,128)S(1)}) custom-call(bf16[1,128,256]{2,1,0:T(8,128)(2,1)} %features.1, bf16[128,256]{1,0:T(8,128)(2,1)} %last.1, f32[1,128]{1,0:T(1,128)} %growth.1, s32[5]{0:T(128)} %counts.1), custom_call_target="tpu_custom_call" | custom-call | tf_op jit(solution)/shard_map/moments/local_sums/pallas_call | solution.py:303
  2.3 1.3 %collective-permute-start = (bf16[128,256]{1,0:T(8,128)(2,1)S(1)}, bf16[128,256]{1,0:T(8,128)(2,1)S(1)}, u32[]{:S(2)}, u32[]{:S(2)}) collective-permute-start(bf16[128,256]{1,0:T(8,128)(2,1)S(1)} %get-tuple-element.29.own), channel_id=1, source_target_pairs={{1,0},{2,1},{3,2},{33,32},{34,33},{35,34},{5,4},{6,5},{7,6},{37,36... | collective-permute-start | bytes 196616 | tf_op jit(solution)/shard_map/gather/ppermute | solution.py:288
  3.6 7.6 %all-to-all-start = ((f32[16,8,128]{2,1,0:T(8,128)}), f32[16,8,128]{2,1,0:T(8,128)S(1)}, u32[]{:S(2)}, u32[]{:S(2)}) async-start(f32[16,8,128]{2,1,0:T(8,128)} %get-tuple-element.28), calls=%async_computation | async-start | bytes 131072 | tf_op jit(solution)/shard_map/moments/all_to_all | solution.py:292
  11.2 0.0 collective-permute-done.shifted
  11.2 1.1 %parcel.1.copies = bf16[16,128,256]{2,1,0:T(8,128)(2,1)} custom-call(f32[24,128]{1,0:T(8,128)S(1)} %get-tuple-element.27.frame, bf16[128,256]{1,0:T(8,128)(2,1)S(1)} %collective-permute-done.shifted, bf16[128,256]{1,0:T(8,128)(2,1)S(1)} %get-tuple-element.30.last), custom_call_target="tpu_custom_call" | custom-call | tf_op jit(solution)/shard_map/gather/parcel/pallas_call | solution.py:319
  12.3 5.4 %all-to-all-done.messages = f32[16,8,128]{2,1,0:T(8,128)S(1)} async-done(((f32[16,8,128]{2,1,0:T(8,128)}), f32[16,8,128]{2,1,0:T(8,128)S(1)}, u32[]{:S(2)}, u32[]{:S(2)}) %all-to-all-start) | async-done | bytes 65568 | tf_op jit(solution)/shard_map/moments/all_to_all | solution.py:292
  17.7 3.7 %all-to-all-start.1 = ((bf16[16,128,256]{2,1,0:T(8,128)(2,1)}), bf16[16,128,256]{2,1,0:T(8,128)(2,1)S(1)}, u32[]{:S(2)}, u32[]{:S(2)}) async-start(bf16[16,128,256]{2,1,0:T(8,128)(2,1)} %get-tuple-element.31), calls=%async_computation.1 | async-start | bytes 2097152 | tf_op jit(solution)/shard_map/gather/all_to_all | solution.py:292
  21.4 2.2 %collective-permute-start.2 = (bf16[128,256]{1,0:T(8,128)(2,1)S(1)}, bf16[128,256]{1,0:T(8,128)(2,1)S(1)}, u32[]{:S(2)}, u32[]{:S(2)}) collective-permute-start(bf16[128,256]{1,0:T(8,128)(2,1)S(1)} %get-tuple-element.33.own), channel_id=1, source_target_pairs={{0,4},{4,0},{1,5},{5,1},{2,6},{6,2},{3,7},{7,3},{8,12},{12,8},{9,1... | collective-permute-start | bytes 196616 | tf_op jit(solution)/shard_map/gather/ppermute | solution.py:279
  23.6 0.1 collective-permute-start.1
  23.7 1.1 %collective-permute-done.1.other = f32[8,128]{1,0:T(8,128)S(1)} collective-permute-done((f32[8,128]{1,0:T(8,128)S(1)}, f32[8,128]{1,0:T(8,128)S(1)}, u32[]{:S(2)}, u32[]{:S(2)}) %collective-permute-start.1) | collective-permute-done | bytes 4128 | tf_op jit(solution)/shard_map/gather/ppermute | solution.py:279
  24.8 0.0 collective-permute-done.2.other_own
  24.8 1.7 %collective-permute-start.6 = (bf16[256,256]{1,0:T(8,128)(2,1)S(1)}, bf16[256,256]{1,0:T(8,128)(2,1)S(1)}, u32[]{:S(2)}, u32[]{:S(2)}) collective-permute-start(bf16[256,256]{1,0:T(8,128)(2,1)S(1)} %get-tuple-element.35.near), channel_id=1, source_target_pairs={{0,32},{32,0},{1,33},{33,1},{2,34},{34,2},{3,35},{35,3},{4,36},{36... | collective-permute-start | bytes 393224 | tf_op jit(solution)/shard_map/gather/ppermute | solution.py:279
  26.5 1.3 %collective-permute-start.5 = (f32[8,128]{1,0:T(8,128)S(1)}, f32[8,128]{1,0:T(8,128)S(1)}, u32[]{:S(2)}, u32[]{:S(2)}) collective-permute-start(f32[8,128]{1,0:T(8,128)S(1)} %get-tuple-element.34.mine), channel_id=1, source_target_pairs={{1,32},{2,33},{3,34},{33,0},{34,1},{35,2},{5,36},{6,37},{7,38},{37... | collective-permute-start | bytes 12296 | tf_op jit(solution)/shard_map/gather/ppermute | solution.py:288
  27.8 1.3 %collective-permute-start.4 = (f32[8,128]{1,0:T(8,128)S(1)}, f32[8,128]{1,0:T(8,128)S(1)}, u32[]{:S(2)}, u32[]{:S(2)}) collective-permute-start(f32[8,128]{1,0:T(8,128)S(1)} %get-tuple-element.34.mine), channel_id=1, source_target_pairs={{1,0},{2,1},{3,2},{33,32},{34,33},{35,34},{5,4},{6,5},{7,6},{37,36... | collective-permute-start | bytes 12296 | tf_op jit(solution)/shard_map/gather/ppermute | solution.py:288
  29.1 0.1 collective-permute-start.3
  29.2 4.4 %collective-permute-done.5.back_across = f32[8,128]{1,0:T(8,128)S(1)} collective-permute-done((f32[8,128]{1,0:T(8,128)S(1)}, f32[8,128]{1,0:T(8,128)S(1)}, u32[]{:S(2)}, u32[]{:S(2)}) %collective-permute-start.5) | collective-permute-done | bytes 4128 | tf_op jit(solution)/shard_map/gather/ppermute | solution.py:288
  33.6 1.6 %collective-permute-done.4.back = f32[8,128]{1,0:T(8,128)S(1)} collective-permute-done((f32[8,128]{1,0:T(8,128)S(1)}, f32[8,128]{1,0:T(8,128)S(1)}, u32[]{:S(2)}, u32[]{:S(2)}) %collective-permute-start.4) | collective-permute-done | bytes 4128 | tf_op jit(solution)/shard_map/gather/ppermute | solution.py:288
  35.2 0.0 collective-permute-done.3.across
  35.2 0.0 collective-permute-done.6.far
  35.2 0.2 prepared.1
  35.4 0.8 all-to-all-done.1.targets
  36.2 2.5 %first_pass.1 = (f32[16,512,128]{2,1,0:T(8,128)S(1)}, f32[8,128]{1,0:T(8,128)S(1)}) custom-call(f32[24,128]{1,0:T(8,128)S(1)} %get-tuple-element.27.frame, bf16[16,128,256]{2,1,0:T(8,128)(2,1)S(1)} %all-to-all-done.1.targets, bf16[512,256]{1,0:T(8,128)(2,1)S(1)} %get-tuple-element.36.rows, f32[512,128]{1,0:T(8,128)S(1)} %get-tuple-element.37.weights, ...), custom_call_target="tpu_custom_call" | custom-call | tf_op jit(solution)/shard_map/first_rows/first_pass/pallas_call | solution.py:353
  38.7 4.8 %collective-permute-start.9 = (f32[8,128]{1,0:T(8,128)S(1)}, f32[8,128]{1,0:T(8,128)S(1)}, u32[]{:S(2)}, u32[]{:S(2)}) collective-permute-start(f32[8,128]{1,0:T(8,128)S(1)} %get-tuple-element.39.p0), channel_id=1, source_target_pairs={{0,36},{4,32},{32,4},{36,0},{1,37},{5,33},{33,5},{37,1},{2,38},{6,... | collective-permute-start | bytes 12296 | tf_op jit(solution)/shard_map/first_columns/ppermute | solution.py:283
  43.6 0.0 collective-permute-start.8
  43.6 0.5 collective-permute-start.7
  44.1 0.8 collective-permute-done.9.p3
  44.9 1.2 %collective-permute-done.8.p2 = f32[8,128]{1,0:T(8,128)S(1)} collective-permute-done((f32[8,128]{1,0:T(8,128)S(1)}, f32[8,128]{1,0:T(8,128)S(1)}, u32[]{:S(2)}, u32[]{:S(2)}) %collective-permute-start.8) | collective-permute-done | bytes 4128 | tf_op jit(solution)/shard_map/first_columns/ppermute | solution.py:283
  46.0 0.0 collective-permute-done.7.p1
  46.0 0.8 %first_columns.1 = (f32[4,128]{1,0:T(4,128)S(1)}, f32[16,16,128]{2,1,0:T(8,128)S(1)}) custom-call(f32[24,128]{1,0:T(8,128)S(1)} %get-tuple-element.27.frame, f32[8,128]{1,0:T(8,128)S(1)} %get-tuple-element.39.p0, f32[8,128]{1,0:T(8,128)S(1)} %collective-permute-done.7.p1, f32[8,128]{1,0:T(8,128)S(1)} %collective-permute-done.8.p2, ...), custom_call_target="tpu_custom_call" | custom-call | tf_op jit(solution)/shard_map/first_columns/first_columns/pallas_call | solution.py:361
  46.9 9.9 %all_to_all.20.parts = f32[16,16,128]{2,1,0:T(8,128)S(1)} all-to-all(f32[16,16,128]{2,1,0:T(8,128)S(1)} %get-tuple-element.42), channel_id=1, replica_groups=mesh['x'=4,'z'=2,'y'=4,'c'=2,'g'=4] {'x','y'}, dimensions={0} | all-to-all | bytes 262144 | tf_op jit(solution)/shard_map/first_columns/all_to_all | solution.py:292
  56.7 1.0 %second_rows.1.p0 = f32[4,128]{1,0:T(4,128)S(1)} custom-call(f32[24,128]{1,0:T(8,128)S(1)} %get-tuple-element.27.frame, f32[16,16,128]{2,1,0:T(8,128)S(1)} %all_to_all.20.parts, f32[16,512,128]{2,1,0:T(8,128)S(1)} %get-tuple-element.40.scores), custom_call_target="tpu_custom_call" | custom-call | tf_op jit(solution)/shard_map/second_rows/second_rows/pallas_call | solution.py:370
  57.7 2.7 %collective-permute-start.12 = (f32[4,128]{1,0:T(4,128)S(1)}, f32[4,128]{1,0:T(4,128)S(1)}, u32[]{:S(2)}, u32[]{:S(2)}) collective-permute-start(f32[4,128]{1,0:T(4,128)S(1)} %second_rows.1.p0), channel_id=1, source_target_pairs={{0,36},{4,32},{32,4},{36,0},{1,37},{5,33},{33,5},{37,1},{2,38},{6,... | collective-permute-start | bytes 6152 | tf_op jit(solution)/shard_map/last_columns/ppermute | solution.py:283
  60.5 0.3 collective-permute-start.11
  60.8 0.2 collective-permute-start.10
  60.9 0.8 collective-permute-done.12.p3
  61.7 1.2 %collective-permute-done.11.p2 = f32[4,128]{1,0:T(4,128)S(1)} collective-permute-done((f32[4,128]{1,0:T(4,128)S(1)}, f32[4,128]{1,0:T(4,128)S(1)}, u32[]{:S(2)}, u32[]{:S(2)}) %collective-permute-start.11) | collective-permute-done | bytes 2080 | tf_op jit(solution)/shard_map/last_columns/ppermute | solution.py:283
  62.9 0.0 collective-permute-done.10.p1
  62.9 0.8 %last_columns.1 = (f32[4,128]{1,0:T(4,128)S(1)}, f32[1,128]{1,0:T(1,128)S(1)}, f32[16,16,128]{2,1,0:T(8,128)S(1)}) custom-call(f32[24,128]{1,0:T(8,128)S(1)} %get-tuple-element.27.frame, f32[4,128]{1,0:T(4,128)S(1)} %get-tuple-element.41.log_p, f32[4,128]{1,0:T(4,128)S(1)} %second_rows.1.p0, f32[4,128]{1,0:T(4,128)S(1)} %collective-permute-done.10.p1, ...), custom_call_target="tpu_custom_call" | custom-call | tf_op jit(solution)/shard_map/last_columns/last_columns/pallas_call | solution.py:374
  63.7 9.8 %all_to_all.21.parts = f32[16,16,128]{2,1,0:T(8,128)S(1)} all-to-all(f32[16,16,128]{2,1,0:T(8,128)S(1)} %get-tuple-element.44), channel_id=1, replica_groups=mesh['x'=4,'z'=2,'y'=4,'c'=2,'g'=4] {'x','y'}, dimensions={0} | all-to-all | bytes 262144 | tf_op jit(solution)/shard_map/last_columns/all_to_all | solution.py:292
  73.6 1.0 %last_rows.1 = (f32[1,128]{1,0:T(1,128)S(1)}, f32[1,128]{1,0:T(1,128)S(1)}, f32[1,128]{1,0:T(1,128)S(1)}, f32[1,128]{1,0:T(1,128)S(1)}, f32[1,128]{1,0:T(1,128)S(1)}) custom-call(f32[24,128]{1,0:T(8,128)S(1)} %get-tuple-element.27.frame, f32[16,16,128]{2,1,0:T(8,128)S(1)} %all_to_all.21.parts, f32[16,512,128]{2,1,0:T(8,128)S(1)} %get-tuple-element.40.scores, ...), custom_call_target="tpu_custom_call" | custom-call | tf_op jit(solution)/shard_map/mass/last_rows/pallas_call | solution.py:383
  74.6 1.7 %collective-permute-start.13 = (f32[1,128]{1,0:T(1,128)S(1)}, f32[1,128]{1,0:T(1,128)S(1)}, u32[]{:S(2)}, u32[]{:S(2)}) collective-permute-start(f32[1,128]{1,0:T(1,128)S(1)} %get-tuple-element.48), channel_id=1, source_target_pairs={{0,4},{4,0},{32,36},{36,32},{1,5},{5,1},{33,37},{37,33},{2,6},{6,2... | collective-permute-start | bytes 1544 | tf_op jit(solution)/shard_map/mass/ppermute | solution.py:283
  76.3 1.2 %collective-permute-start.14 = (f32[1,128]{1,0:T(1,128)S(1)}, f32[1,128]{1,0:T(1,128)S(1)}, u32[]{:S(2)}, u32[]{:S(2)}) collective-permute-start(f32[1,128]{1,0:T(1,128)S(1)} %get-tuple-element.49), channel_id=1, source_target_pairs={{0,32},{4,36},{32,0},{36,4},{1,33},{5,37},{33,1},{37,5},{2,34},{6,... | collective-permute-start | bytes 1544 | tf_op jit(solution)/shard_map/mass/ppermute | solution.py:283
  77.4 0.6 collective-permute-start.15
  78.0 0.0 collective-permute-done.13.q1
  78.0 0.7 collective-permute-done.14.q2
  78.7 1.7 %collective-permute-done.15.q3 = f32[1,128]{1,0:T(1,128)S(1)} collective-permute-done((f32[1,128]{1,0:T(1,128)S(1)}, f32[1,128]{1,0:T(1,128)S(1)}, u32[]{:S(2)}, u32[]{:S(2)}) %collective-permute-start.15) | collective-permute-done | bytes 544 | tf_op jit(solution)/shard_map/mass/ppermute | solution.py:283
  80.4 0.5 outputs.1
  (2 shorter events, 0.0 us)
Async XLA Ops:
  2.3 8.9 %collective-permute-start = (bf16[128,256]{1,0:T(8,128)(2,1)S(1)}, bf16[128,256]{1,0:T(8,128)(2,1)S(1)}, u32[]{:S(2)}, u32[]{:S(2)}) collective-permute-start(bf16[128,256]{1,0:T(8,128)(2,1)S(1)} %get-tuple-element.29.own), channel_id=1, source_target_pairs={{1,0},{2,1},{3,2},{33,32},{34,33},{35,34},{5,4},{6,5},{7,6},{37,36... | collective-permute-start | bytes 196616 | tf_op jit(solution)/shard_map/gather/ppermute | solution.py:288
  3.6 14.1 %all-to-all-start = ((f32[16,8,128]{2,1,0:T(8,128)}), f32[16,8,128]{2,1,0:T(8,128)S(1)}, u32[]{:S(2)}, u32[]{:S(2)}) async-start(f32[16,8,128]{2,1,0:T(8,128)} %get-tuple-element.28), calls=%async_computation | async-start | bytes 131072 | tf_op jit(solution)/shard_map/moments/all_to_all | solution.py:292
  17.7 18.5 %all-to-all-start.1 = ((bf16[16,128,256]{2,1,0:T(8,128)(2,1)}), bf16[16,128,256]{2,1,0:T(8,128)(2,1)S(1)}, u32[]{:S(2)}, u32[]{:S(2)}) async-start(bf16[16,128,256]{2,1,0:T(8,128)(2,1)} %get-tuple-element.31), calls=%async_computation.1 | async-start | bytes 2097152 | tf_op jit(solution)/shard_map/gather/all_to_all | solution.py:292
  21.4 3.4 %collective-permute-start.2 = (bf16[128,256]{1,0:T(8,128)(2,1)S(1)}, bf16[128,256]{1,0:T(8,128)(2,1)S(1)}, u32[]{:S(2)}, u32[]{:S(2)}) collective-permute-start(bf16[128,256]{1,0:T(8,128)(2,1)S(1)} %get-tuple-element.33.own), channel_id=1, source_target_pairs={{0,4},{4,0},{1,5},{5,1},{2,6},{6,2},{3,7},{7,3},{8,12},{12,8},{9,1... | collective-permute-start | bytes 196616 | tf_op jit(solution)/shard_map/gather/ppermute | solution.py:279
  23.6 1.2 %collective-permute-start.1 = (f32[8,128]{1,0:T(8,128)S(1)}, f32[8,128]{1,0:T(8,128)S(1)}, u32[]{:S(2)}, u32[]{:S(2)}) collective-permute-start(f32[8,128]{1,0:T(8,128)S(1)} %get-tuple-element.32.mine), channel_id=1, source_target_pairs={{0,4},{4,0},{1,5},{5,1},{2,6},{6,2},{3,7},{7,3},{8,12},{12,8},{9,1... | collective-permute-start | bytes 12296 | tf_op jit(solution)/shard_map/gather/ppermute | solution.py:279
  24.8 10.5 %collective-permute-start.6 = (bf16[256,256]{1,0:T(8,128)(2,1)S(1)}, bf16[256,256]{1,0:T(8,128)(2,1)S(1)}, u32[]{:S(2)}, u32[]{:S(2)}) collective-permute-start(bf16[256,256]{1,0:T(8,128)(2,1)S(1)} %get-tuple-element.35.near), channel_id=1, source_target_pairs={{0,32},{32,0},{1,33},{33,1},{2,34},{34,2},{3,35},{35,3},{4,36},{36... | collective-permute-start | bytes 393224 | tf_op jit(solution)/shard_map/gather/ppermute | solution.py:279
  26.5 7.1 %collective-permute-start.5 = (f32[8,128]{1,0:T(8,128)S(1)}, f32[8,128]{1,0:T(8,128)S(1)}, u32[]{:S(2)}, u32[]{:S(2)}) collective-permute-start(f32[8,128]{1,0:T(8,128)S(1)} %get-tuple-element.34.mine), channel_id=1, source_target_pairs={{1,32},{2,33},{3,34},{33,0},{34,1},{35,2},{5,36},{6,37},{7,38},{37... | collective-permute-start | bytes 12296 | tf_op jit(solution)/shard_map/gather/ppermute | solution.py:288
  27.8 7.4 %collective-permute-start.4 = (f32[8,128]{1,0:T(8,128)S(1)}, f32[8,128]{1,0:T(8,128)S(1)}, u32[]{:S(2)}, u32[]{:S(2)}) collective-permute-start(f32[8,128]{1,0:T(8,128)S(1)} %get-tuple-element.34.mine), channel_id=1, source_target_pairs={{1,0},{2,1},{3,2},{33,32},{34,33},{35,34},{5,4},{6,5},{7,6},{37,36... | collective-permute-start | bytes 12296 | tf_op jit(solution)/shard_map/gather/ppermute | solution.py:288
  29.1 6.1 %collective-permute-start.3 = (f32[8,128]{1,0:T(8,128)S(1)}, f32[8,128]{1,0:T(8,128)S(1)}, u32[]{:S(2)}, u32[]{:S(2)}) collective-permute-start(f32[8,128]{1,0:T(8,128)S(1)} %get-tuple-element.34.mine), channel_id=1, source_target_pairs={{0,32},{32,0},{1,33},{33,1},{2,34},{34,2},{3,35},{35,3},{4,36},{36... | collective-permute-start | bytes 12296 | tf_op jit(solution)/shard_map/gather/ppermute | solution.py:279
  38.7 6.1 %collective-permute-start.9 = (f32[8,128]{1,0:T(8,128)S(1)}, f32[8,128]{1,0:T(8,128)S(1)}, u32[]{:S(2)}, u32[]{:S(2)}) collective-permute-start(f32[8,128]{1,0:T(8,128)S(1)} %get-tuple-element.39.p0), channel_id=1, source_target_pairs={{0,36},{4,32},{32,4},{36,0},{1,37},{5,33},{33,5},{37,1},{2,38},{6,... | collective-permute-start | bytes 12296 | tf_op jit(solution)/shard_map/first_columns/ppermute | solution.py:283
  43.6 2.5 %collective-permute-start.8 = (f32[8,128]{1,0:T(8,128)S(1)}, f32[8,128]{1,0:T(8,128)S(1)}, u32[]{:S(2)}, u32[]{:S(2)}) collective-permute-start(f32[8,128]{1,0:T(8,128)S(1)} %get-tuple-element.39.p0), channel_id=1, source_target_pairs={{0,32},{4,36},{32,0},{36,4},{1,33},{5,37},{33,1},{37,5},{2,34},{6,... | collective-permute-start | bytes 12296 | tf_op jit(solution)/shard_map/first_columns/ppermute | solution.py:283
  43.6 2.5 %collective-permute-start.7 = (f32[8,128]{1,0:T(8,128)S(1)}, f32[8,128]{1,0:T(8,128)S(1)}, u32[]{:S(2)}, u32[]{:S(2)}) collective-permute-start(f32[8,128]{1,0:T(8,128)S(1)} %get-tuple-element.39.p0), channel_id=1, source_target_pairs={{0,4},{4,0},{32,36},{36,32},{1,5},{5,1},{33,37},{37,33},{2,6},{6,2... | collective-permute-start | bytes 12296 | tf_op jit(solution)/shard_map/first_columns/ppermute | solution.py:283
  57.7 4.0 %collective-permute-start.12 = (f32[4,128]{1,0:T(4,128)S(1)}, f32[4,128]{1,0:T(4,128)S(1)}, u32[]{:S(2)}, u32[]{:S(2)}) collective-permute-start(f32[4,128]{1,0:T(4,128)S(1)} %second_rows.1.p0), channel_id=1, source_target_pairs={{0,36},{4,32},{32,4},{36,0},{1,37},{5,33},{33,5},{37,1},{2,38},{6,... | collective-permute-start | bytes 6152 | tf_op jit(solution)/shard_map/last_columns/ppermute | solution.py:283
  60.5 2.4 %collective-permute-start.11 = (f32[4,128]{1,0:T(4,128)S(1)}, f32[4,128]{1,0:T(4,128)S(1)}, u32[]{:S(2)}, u32[]{:S(2)}) collective-permute-start(f32[4,128]{1,0:T(4,128)S(1)} %second_rows.1.p0), channel_id=1, source_target_pairs={{0,32},{4,36},{32,0},{36,4},{1,33},{5,37},{33,1},{37,5},{2,34},{6,... | collective-permute-start | bytes 6152 | tf_op jit(solution)/shard_map/last_columns/ppermute | solution.py:283
  60.8 2.1 %collective-permute-start.10 = (f32[4,128]{1,0:T(4,128)S(1)}, f32[4,128]{1,0:T(4,128)S(1)}, u32[]{:S(2)}, u32[]{:S(2)}) collective-permute-start(f32[4,128]{1,0:T(4,128)S(1)} %second_rows.1.p0), channel_id=1, source_target_pairs={{0,4},{4,0},{32,36},{36,32},{1,5},{5,1},{33,37},{37,33},{2,6},{6,2... | collective-permute-start | bytes 6152 | tf_op jit(solution)/shard_map/last_columns/ppermute | solution.py:283
  74.6 3.4 %collective-permute-start.13 = (f32[1,128]{1,0:T(1,128)S(1)}, f32[1,128]{1,0:T(1,128)S(1)}, u32[]{:S(2)}, u32[]{:S(2)}) collective-permute-start(f32[1,128]{1,0:T(1,128)S(1)} %get-tuple-element.48), channel_id=1, source_target_pairs={{0,4},{4,0},{32,36},{36,32},{1,5},{5,1},{33,37},{37,33},{2,6},{6,2... | collective-permute-start | bytes 1544 | tf_op jit(solution)/shard_map/mass/ppermute | solution.py:283
  76.3 2.4 %collective-permute-start.14 = (f32[1,128]{1,0:T(1,128)S(1)}, f32[1,128]{1,0:T(1,128)S(1)}, u32[]{:S(2)}, u32[]{:S(2)}) collective-permute-start(f32[1,128]{1,0:T(1,128)S(1)} %get-tuple-element.49), channel_id=1, source_target_pairs={{0,32},{4,36},{32,0},{36,4},{1,33},{5,37},{33,1},{37,5},{2,34},{6,... | collective-permute-start | bytes 1544 | tf_op jit(solution)/shard_map/mass/ppermute | solution.py:283
  77.4 3.0 %collective-permute-start.15 = (f32[1,128]{1,0:T(1,128)S(1)}, f32[1,128]{1,0:T(1,128)S(1)}, u32[]{:S(2)}, u32[]{:S(2)}) collective-permute-start(f32[1,128]{1,0:T(1,128)S(1)} %get-tuple-element.50), channel_id=1, source_target_pairs={{0,36},{4,32},{32,4},{36,0},{1,37},{5,33},{33,5},{37,1},{2,38},{6,... | collective-permute-start | bytes 1544 | tf_op jit(solution)/shard_map/mass/ppermute | solution.py:283

commit v8 on v7

--- a/solution.py
+++ b/solution.py
@@ -153,7 +153,7 @@
     scale = scales[0:1, :]
     twice = 2.0 * scale
 
-    @pl.loop(0, COLUMN_BLOCKS // 2)
+    @pl.loop(0, COLUMN_BLOCKS // 2, unroll=8)
     def _(pair):
         first = pair * 2
         block = targets[pl.ds(first, 2)].reshape(2 * CELLS, WIDTH)
@@ -194,7 +194,7 @@
         return tuple(more)
 
     zeros = (jnp.zeros((8, CELLS), F32),) * COLUMN_BLOCKS
-    for i, total in enumerate(lax.fori_loop(0, ROWS // STRIP, strip, zeros)):
+    for i, total in enumerate(lax.fori_loop(0, ROWS // STRIP, strip, zeros, unroll=8)):
         gathered[i : i + 1, :] = jnp.sum(total, axis=0, keepdims=True)
     out[...] = jnp.broadcast_to(gathered[...][None], out.shape)
 
@@ -239,7 +239,7 @@
     present = frame[COLUMNS_AT : COLUMNS_AT + COLUMN_BLOCKS, :] > 0.0
     limits[...] = jnp.where(present, beta * LOG2E, ABSENT)
 
-    @pl.loop(0, ROWS // STRIP)
+    @pl.loop(0, ROWS // STRIP, unroll=8)
     def _(number):
         at = pl.ds(pl.multiple_of(number * STRIP, STRIP), STRIP)
         running = jnp.exp2(limits[0:1, :] - scores[0, at, :])

time: 81.4 us -> 79.4 us (0.975)
  Pallas kernels: 9.63 us -> 7.71 us
    pallas_call x1, Pallas kernels: 2.51 us -> 1.29 us  [local(): call(first_pass, (shape(COLUMN_BLOCKS, ROWS, CELLS), row_parts), 5, (part...]
where the time goes in v8:
time: 79.4 us; the launch traced here: 79 us
  starting transfers between devices  31.2 us (39%)
  blocking collectives  19.7 us (25%)
  waiting for transfers between devices  19.6 us (25%)
  Pallas kernels  7.71 us (10%)
    all_to_all x2, blocking collectives, exchanged(): lax.all_to_all(copies, COLUMN_AXES, split_axis=0, concat_axis=0, tiled=True)  19.7 us
    ppermute x9, starting transfers between devices, across(): return lax.ppermute(value, ROW_AXES, [(d, d ^ k) for d in range(4)])  12 us
    all_to_all x2, starting transfers between devices, exchanged(): lax.all_to_all(copies, COLUMN_AXES, split_axis=0, concat_axis=0, tiled=True)  11.3 us
    ppermute x9, waiting for transfers between devices, across(): return lax.ppermute(value, ROW_AXES, [(d, d ^ k) for d in range(4)])  6.31 us
    all_to_all x2, waiting for transfers between devices, exchanged(): lax.all_to_all(copies, COLUMN_AXES, split_axis=0, concat_axis=0, tiled=True)  6.18 us
    ppermute x3, waiting for transfers between devices, back(): return lax.ppermute(value, ('z', 'g'), moves)  6.03 us
    ppermute x4, starting transfers between devices, swapped(): return lax.ppermute(value, axis, [(0, 1), (1, 0)])  4.13 us
    ppermute x3, starting transfers between devices, back(): return lax.ppermute(value, ('z', 'g'), moves)  3.86 us
  transfers between devices with their start and end apart: 18, of which 11 were waited for; matrix products, arithmetic and copies ran while one was open for 0% of the time, Pallas kernels for 2%

profile of v8, /device:TPU:1, one launch (start us, length us, event | category | flops | bytes accessed | tf_op | source)
XLA Modules:
  0.0 79.0 jit_solution(875758145411951307)
XLA Ops:
  0.6 1.7 %local_sums.1 = (f32[16,8,128]{2,1,0:T(8,128)}, bf16[128,256]{1,0:T(8,128)(2,1)S(1)}, bf16[128,256]{1,0:T(8,128)(2,1)S(1)}, f32[24,128]{1,0:T(8,128)S(1)}) custom-call(bf16[1,128,256]{2,1,0:T(8,128)(2,1)} %features.1, bf16[128,256]{1,0:T(8,128)(2,1)} %last.1, f32[1,128]{1,0:T(1,128)} %growth.1, s32[5]{0:T(128)} %counts.1), custom_call_target="tpu_custom_call" | custom-call | tf_op jit(solution)/shard_map/moments/local_sums/pallas_call | solution.py:303
  2.3 1.3 %collective-permute-start = (bf16[128,256]{1,0:T(8,128)(2,1)S(1)}, bf16[128,256]{1,0:T(8,128)(2,1)S(1)}, u32[]{:S(2)}, u32[]{:S(2)}) collective-permute-start(bf16[128,256]{1,0:T(8,128)(2,1)S(1)} %get-tuple-element.29.own), channel_id=1, source_target_pairs={{1,0},{2,1},{3,2},{33,32},{34,33},{35,34},{5,4},{6,5},{7,6},{37,36... | collective-permute-start | bytes 196616 | tf_op jit(solution)/shard_map/gather/ppermute | solution.py:288
  3.6 7.6 %all-to-all-start = ((f32[16,8,128]{2,1,0:T(8,128)}), f32[16,8,128]{2,1,0:T(8,128)S(1)}, u32[]{:S(2)}, u32[]{:S(2)}) async-start(f32[16,8,128]{2,1,0:T(8,128)} %get-tuple-element.28), calls=%async_computation | async-start | bytes 131072 | tf_op jit(solution)/shard_map/moments/all_to_all | solution.py:292
  11.2 0.0 collective-permute-done.shifted
  11.2 1.1 %parcel.1.copies = bf16[16,128,256]{2,1,0:T(8,128)(2,1)} custom-call(f32[24,128]{1,0:T(8,128)S(1)} %get-tuple-element.27.frame, bf16[128,256]{1,0:T(8,128)(2,1)S(1)} %collective-permute-done.shifted, bf16[128,256]{1,0:T(8,128)(2,1)S(1)} %get-tuple-element.30.last), custom_call_target="tpu_custom_call" | custom-call | tf_op jit(solution)/shard_map/gather/parcel/pallas_call | solution.py:319
  12.3 5.4 %all-to-all-done.messages = f32[16,8,128]{2,1,0:T(8,128)S(1)} async-done(((f32[16,8,128]{2,1,0:T(8,128)}), f32[16,8,128]{2,1,0:T(8,128)S(1)}, u32[]{:S(2)}, u32[]{:S(2)}) %all-to-all-start) | async-done | bytes 65568 | tf_op jit(solution)/shard_map/moments/all_to_all | solution.py:292
  17.7 3.7 %all-to-all-start.1 = ((bf16[16,128,256]{2,1,0:T(8,128)(2,1)}), bf16[16,128,256]{2,1,0:T(8,128)(2,1)S(1)}, u32[]{:S(2)}, u32[]{:S(2)}) async-start(bf16[16,128,256]{2,1,0:T(8,128)(2,1)} %get-tuple-element.31), calls=%async_computation.1 | async-start | bytes 2097152 | tf_op jit(solution)/shard_map/gather/all_to_all | solution.py:292
  21.4 2.2 %collective-permute-start.2 = (bf16[128,256]{1,0:T(8,128)(2,1)S(1)}, bf16[128,256]{1,0:T(8,128)(2,1)S(1)}, u32[]{:S(2)}, u32[]{:S(2)}) collective-permute-start(bf16[128,256]{1,0:T(8,128)(2,1)S(1)} %get-tuple-element.33.own), channel_id=1, source_target_pairs={{0,4},{4,0},{1,5},{5,1},{2,6},{6,2},{3,7},{7,3},{8,12},{12,8},{9,1... | collective-permute-start | bytes 196616 | tf_op jit(solution)/shard_map/gather/ppermute | solution.py:279
  23.6 0.1 collective-permute-start.1
  23.7 1.1 %collective-permute-done.1.other = f32[8,128]{1,0:T(8,128)S(1)} collective-permute-done((f32[8,128]{1,0:T(8,128)S(1)}, f32[8,128]{1,0:T(8,128)S(1)}, u32[]{:S(2)}, u32[]{:S(2)}) %collective-permute-start.1) | collective-permute-done | bytes 4128 | tf_op jit(solution)/shard_map/gather/ppermute | solution.py:279
  24.8 0.0 collective-permute-done.2.other_own
  24.8 1.7 %collective-permute-start.6 = (bf16[256,256]{1,0:T(8,128)(2,1)S(1)}, bf16[256,256]{1,0:T(8,128)(2,1)S(1)}, u32[]{:S(2)}, u32[]{:S(2)}) collective-permute-start(bf16[256,256]{1,0:T(8,128)(2,1)S(1)} %get-tuple-element.35.near), channel_id=1, source_target_pairs={{0,32},{32,0},{1,33},{33,1},{2,34},{34,2},{3,35},{35,3},{4,36},{36... | collective-permute-start | bytes 393224 | tf_op jit(solution)/shard_map/gather/ppermute | solution.py:279
  26.5 1.3 %collective-permute-start.5 = (f32[8,128]{1,0:T(8,128)S(1)}, f32[8,128]{1,0:T(8,128)S(1)}, u32[]{:S(2)}, u32[]{:S(2)}) collective-permute-start(f32[8,128]{1,0:T(8,128)S(1)} %get-tuple-element.34.mine), channel_id=1, source_target_pairs={{1,32},{2,33},{3,34},{33,0},{34,1},{35,2},{5,36},{6,37},{7,38},{37... | collective-permute-start | bytes 12296 | tf_op jit(solution)/shard_map/gather/ppermute | solution.py:288
  27.8 1.3 %collective-permute-start.4 = (f32[8,128]{1,0:T(8,128)S(1)}, f32[8,128]{1,0:T(8,128)S(1)}, u32[]{:S(2)}, u32[]{:S(2)}) collective-permute-start(f32[8,128]{1,0:T(8,128)S(1)} %get-tuple-element.34.mine), channel_id=1, source_target_pairs={{1,0},{2,1},{3,2},{33,32},{34,33},{35,34},{5,4},{6,5},{7,6},{37,36... | collective-permute-start | bytes 12296 | tf_op jit(solution)/shard_map/gather/ppermute | solution.py:288
  29.1 0.1 collective-permute-start.3
  29.2 4.4 %collective-permute-done.5.back_across = f32[8,128]{1,0:T(8,128)S(1)} collective-permute-done((f32[8,128]{1,0:T(8,128)S(1)}, f32[8,128]{1,0:T(8,128)S(1)}, u32[]{:S(2)}, u32[]{:S(2)}) %collective-permute-start.5) | collective-permute-done | bytes 4128 | tf_op jit(solution)/shard_map/gather/ppermute | solution.py:288
  33.6 1.6 %collective-permute-done.4.back = f32[8,128]{1,0:T(8,128)S(1)} collective-permute-done((f32[8,128]{1,0:T(8,128)S(1)}, f32[8,128]{1,0:T(8,128)S(1)}, u32[]{:S(2)}, u32[]{:S(2)}) %collective-permute-start.4) | collective-permute-done | bytes 4128 | tf_op jit(solution)/shard_map/gather/ppermute | solution.py:288
  35.2 0.0 collective-permute-done.3.across
  35.2 0.0 collective-permute-done.6.far
  35.2 0.2 prepared.1
  35.4 0.8 %all-to-all-done.1.targets = bf16[16,128,256]{2,1,0:T(8,128)(2,1)S(1)} async-done(((bf16[16,128,256]{2,1,0:T(8,128)(2,1)}), bf16[16,128,256]{2,1,0:T(8,128)(2,1)S(1)}, u32[]{:S(2)}, u32[]{:S(2)}) %all-to-all-start.1) | async-done | bytes 1048608 | tf_op jit(solution)/shard_map/gather/all_to_all | solution.py:292
  36.2 1.3 %first_pass.1 = (f32[16,512,128]{2,1,0:T(8,128)S(1)}, f32[8,128]{1,0:T(8,128)S(1)}) custom-call(f32[24,128]{1,0:T(8,128)S(1)} %get-tuple-element.27.frame, bf16[16,128,256]{2,1,0:T(8,128)(2,1)S(1)} %all-to-all-done.1.targets, bf16[512,256]{1,0:T(8,128)(2,1)S(1)} %get-tuple-element.36.rows, f32[512,128]{1,0:T(8,128)S(1)} %get-tuple-element.37.weights, ...), custom_call_target="tpu_custom_call" | custom-call | tf_op jit(solution)/shard_map/first_rows/first_pass/pallas_call | solution.py:353
  37.5 4.8 %collective-permute-start.9 = (f32[8,128]{1,0:T(8,128)S(1)}, f32[8,128]{1,0:T(8,128)S(1)}, u32[]{:S(2)}, u32[]{:S(2)}) collective-permute-start(f32[8,128]{1,0:T(8,128)S(1)} %get-tuple-element.39.p0), channel_id=1, source_target_pairs={{0,36},{4,32},{32,4},{36,0},{1,37},{5,33},{33,5},{37,1},{2,38},{6,... | collective-permute-start | bytes 12296 | tf_op jit(solution)/shard_map/first_columns/ppermute | solution.py:283
  42.3 0.0 collective-permute-start.8
  42.3 0.5 collective-permute-start.7
  42.8 0.8 %collective-permute-done.9.p3 = f32[8,128]{1,0:T(8,128)S(1)} collective-permute-done((f32[8,128]{1,0:T(8,128)S(1)}, f32[8,128]{1,0:T(8,128)S(1)}, u32[]{:S(2)}, u32[]{:S(2)}) %collective-permute-start.9) | collective-permute-done | bytes 4128 | tf_op jit(solution)/shard_map/first_columns/ppermute | solution.py:283
  43.6 1.2 %collective-permute-done.8.p2 = f32[8,128]{1,0:T(8,128)S(1)} collective-permute-done((f32[8,128]{1,0:T(8,128)S(1)}, f32[8,128]{1,0:T(8,128)S(1)}, u32[]{:S(2)}, u32[]{:S(2)}) %collective-permute-start.8) | collective-permute-done | bytes 4128 | tf_op jit(solution)/shard_map/first_columns/ppermute | solution.py:283
  44.8 0.0 collective-permute-done.7.p1
  44.8 0.8 first_columns.1
  45.6 9.8 %all_to_all.20.parts = f32[16,16,128]{2,1,0:T(8,128)S(1)} all-to-all(f32[16,16,128]{2,1,0:T(8,128)S(1)} %get-tuple-element.42), channel_id=1, replica_groups=mesh['x'=4,'z'=2,'y'=4,'c'=2,'g'=4] {'x','y'}, dimensions={0} | all-to-all | bytes 262144 | tf_op jit(solution)/shard_map/first_columns/all_to_all | solution.py:292
  55.4 0.7 second_rows.1.p0
  56.1 2.7 %collective-permute-start.12 = (f32[4,128]{1,0:T(4,128)S(1)}, f32[4,128]{1,0:T(4,128)S(1)}, u32[]{:S(2)}, u32[]{:S(2)}) collective-permute-start(f32[4,128]{1,0:T(4,128)S(1)} %second_rows.1.p0), channel_id=1, source_target_pairs={{0,36},{4,32},{32,4},{36,0},{1,37},{5,33},{33,5},{37,1},{2,38},{6,... | collective-permute-start | bytes 6152 | tf_op jit(solution)/shard_map/last_columns/ppermute | solution.py:283
  58.8 0.3 collective-permute-start.11
  59.2 0.2 collective-permute-start.10
  59.3 1.1 %collective-permute-done.12.p3 = f32[4,128]{1,0:T(4,128)S(1)} collective-permute-done((f32[4,128]{1,0:T(4,128)S(1)}, f32[4,128]{1,0:T(4,128)S(1)}, u32[]{:S(2)}, u32[]{:S(2)}) %collective-permute-start.12) | collective-permute-done | bytes 2080 | tf_op jit(solution)/shard_map/last_columns/ppermute | solution.py:283
  60.4 0.9 %collective-permute-done.11.p2 = f32[4,128]{1,0:T(4,128)S(1)} collective-permute-done((f32[4,128]{1,0:T(4,128)S(1)}, f32[4,128]{1,0:T(4,128)S(1)}, u32[]{:S(2)}, u32[]{:S(2)}) %collective-permute-start.11) | collective-permute-done | bytes 2080 | tf_op jit(solution)/shard_map/last_columns/ppermute | solution.py:283
  61.3 0.0 collective-permute-done.10.p1
  61.3 0.8 last_columns.1
  62.1 9.8 %all_to_all.21.parts = f32[16,16,128]{2,1,0:T(8,128)S(1)} all-to-all(f32[16,16,128]{2,1,0:T(8,128)S(1)} %get-tuple-element.44), channel_id=1, replica_groups=mesh['x'=4,'z'=2,'y'=4,'c'=2,'g'=4] {'x','y'}, dimensions={0} | all-to-all | bytes 262144 | tf_op jit(solution)/shard_map/last_columns/all_to_all | solution.py:292
  71.9 0.7 last_rows.1
  72.6 1.7 %collective-permute-start.13 = (f32[1,128]{1,0:T(1,128)S(1)}, f32[1,128]{1,0:T(1,128)S(1)}, u32[]{:S(2)}, u32[]{:S(2)}) collective-permute-start(f32[1,128]{1,0:T(1,128)S(1)} %get-tuple-element.48), channel_id=1, source_target_pairs={{0,4},{4,0},{32,36},{36,32},{1,5},{5,1},{33,37},{37,33},{2,6},{6,2... | collective-permute-start | bytes 1544 | tf_op jit(solution)/shard_map/mass/ppermute | solution.py:283
  74.3 1.2 %collective-permute-start.14 = (f32[1,128]{1,0:T(1,128)S(1)}, f32[1,128]{1,0:T(1,128)S(1)}, u32[]{:S(2)}, u32[]{:S(2)}) collective-permute-start(f32[1,128]{1,0:T(1,128)S(1)} %get-tuple-element.49), channel_id=1, source_target_pairs={{0,32},{4,36},{32,0},{36,4},{1,33},{5,37},{33,1},{37,5},{2,34},{6,... | collective-permute-start | bytes 1544 | tf_op jit(solution)/shard_map/mass/ppermute | solution.py:283
  75.5 0.6 collective-permute-start.15
  76.0 0.0 collective-permute-done.13.q1
  76.0 0.7 collective-permute-done.14.q2
  76.7 1.7 %collective-permute-done.15.q3 = f32[1,128]{1,0:T(1,128)S(1)} collective-permute-done((f32[1,128]{1,0:T(1,128)S(1)}, f32[1,128]{1,0:T(1,128)S(1)}, u32[]{:S(2)}, u32[]{:S(2)}) %collective-permute-start.15) | collective-permute-done | bytes 544 | tf_op jit(solution)/shard_map/mass/ppermute | solution.py:283
  78.4 0.5 outputs.1
  (2 shorter events, 0.0 us)
Async XLA Ops:
  2.3 8.9 %collective-permute-start = (bf16[128,256]{1,0:T(8,128)(2,1)S(1)}, bf16[128,256]{1,0:T(8,128)(2,1)S(1)}, u32[]{:S(2)}, u32[]{:S(2)}) collective-permute-start(bf16[128,256]{1,0:T(8,128)(2,1)S(1)} %get-tuple-element.29.own), channel_id=1, source_target_pairs={{1,0},{2,1},{3,2},{33,32},{34,33},{35,34},{5,4},{6,5},{7,6},{37,36... | collective-permute-start | bytes 196616 | tf_op jit(solution)/shard_map/gather/ppermute | solution.py:288
  3.6 14.1 %all-to-all-start = ((f32[16,8,128]{2,1,0:T(8,128)}), f32[16,8,128]{2,1,0:T(8,128)S(1)}, u32[]{:S(2)}, u32[]{:S(2)}) async-start(f32[16,8,128]{2,1,0:T(8,128)} %get-tuple-element.28), calls=%async_computation | async-start | bytes 131072 | tf_op jit(solution)/shard_map/moments/all_to_all | solution.py:292
  17.7 18.5 %all-to-all-start.1 = ((bf16[16,128,256]{2,1,0:T(8,128)(2,1)}), bf16[16,128,256]{2,1,0:T(8,128)(2,1)S(1)}, u32[]{:S(2)}, u32[]{:S(2)}) async-start(bf16[16,128,256]{2,1,0:T(8,128)(2,1)} %get-tuple-element.31), calls=%async_computation.1 | async-start | bytes 2097152 | tf_op jit(solution)/shard_map/gather/all_to_all | solution.py:292
  21.4 3.4 %collective-permute-start.2 = (bf16[128,256]{1,0:T(8,128)(2,1)S(1)}, bf16[128,256]{1,0:T(8,128)(2,1)S(1)}, u32[]{:S(2)}, u32[]{:S(2)}) collective-permute-start(bf16[128,256]{1,0:T(8,128)(2,1)S(1)} %get-tuple-element.33.own), channel_id=1, source_target_pairs={{0,4},{4,0},{1,5},{5,1},{2,6},{6,2},{3,7},{7,3},{8,12},{12,8},{9,1... | collective-permute-start | bytes 196616 | tf_op jit(solution)/shard_map/gather/ppermute | solution.py:279
  23.6 1.2 %collective-permute-start.1 = (f32[8,128]{1,0:T(8,128)S(1)}, f32[8,128]{1,0:T(8,128)S(1)}, u32[]{:S(2)}, u32[]{:S(2)}) collective-permute-start(f32[8,128]{1,0:T(8,128)S(1)} %get-tuple-element.32.mine), channel_id=1, source_target_pairs={{0,4},{4,0},{1,5},{5,1},{2,6},{6,2},{3,7},{7,3},{8,12},{12,8},{9,1... | collective-permute-start | bytes 12296 | tf_op jit(solution)/shard_map/gather/ppermute | solution.py:279
  24.8 10.5 %collective-permute-start.6 = (bf16[256,256]{1,0:T(8,128)(2,1)S(1)}, bf16[256,256]{1,0:T(8,128)(2,1)S(1)}, u32[]{:S(2)}, u32[]{:S(2)}) collective-permute-start(bf16[256,256]{1,0:T(8,128)(2,1)S(1)} %get-tuple-element.35.near), channel_id=1, source_target_pairs={{0,32},{32,0},{1,33},{33,1},{2,34},{34,2},{3,35},{35,3},{4,36},{36... | collective-permute-start | bytes 393224 | tf_op jit(solution)/shard_map/gather/ppermute | solution.py:279
  26.5 7.1 %collective-permute-start.5 = (f32[8,128]{1,0:T(8,128)S(1)}, f32[8,128]{1,0:T(8,128)S(1)}, u32[]{:S(2)}, u32[]{:S(2)}) collective-permute-start(f32[8,128]{1,0:T(8,128)S(1)} %get-tuple-element.34.mine), channel_id=1, source_target_pairs={{1,32},{2,33},{3,34},{33,0},{34,1},{35,2},{5,36},{6,37},{7,38},{37... | collective-permute-start | bytes 12296 | tf_op jit(solution)/shard_map/gather/ppermute | solution.py:288
  27.8 7.4 %collective-permute-start.4 = (f32[8,128]{1,0:T(8,128)S(1)}, f32[8,128]{1,0:T(8,128)S(1)}, u32[]{:S(2)}, u32[]{:S(2)}) collective-permute-start(f32[8,128]{1,0:T(8,128)S(1)} %get-tuple-element.34.mine), channel_id=1, source_target_pairs={{1,0},{2,1},{3,2},{33,32},{34,33},{35,34},{5,4},{6,5},{7,6},{37,36... | collective-permute-start | bytes 12296 | tf_op jit(solution)/shard_map/gather/ppermute | solution.py:288
  29.1 6.1 %collective-permute-start.3 = (f32[8,128]{1,0:T(8,128)S(1)}, f32[8,128]{1,0:T(8,128)S(1)}, u32[]{:S(2)}, u32[]{:S(2)}) collective-permute-start(f32[8,128]{1,0:T(8,128)S(1)} %get-tuple-element.34.mine), channel_id=1, source_target_pairs={{0,32},{32,0},{1,33},{33,1},{2,34},{34,2},{3,35},{35,3},{4,36},{36... | collective-permute-start | bytes 12296 | tf_op jit(solution)/shard_map/gather/ppermute | solution.py:279
  37.5 6.1 %collective-permute-start.9 = (f32[8,128]{1,0:T(8,128)S(1)}, f32[8,128]{1,0:T(8,128)S(1)}, u32[]{:S(2)}, u32[]{:S(2)}) collective-permute-start(f32[8,128]{1,0:T(8,128)S(1)} %get-tuple-element.39.p0), channel_id=1, source_target_pairs={{0,36},{4,32},{32,4},{36,0},{1,37},{5,33},{33,5},{37,1},{2,38},{6,... | collective-permute-start | bytes 12296 | tf_op jit(solution)/shard_map/first_columns/ppermute | solution.py:283
  42.3 2.5 %collective-permute-start.8 = (f32[8,128]{1,0:T(8,128)S(1)}, f32[8,128]{1,0:T(8,128)S(1)}, u32[]{:S(2)}, u32[]{:S(2)}) collective-permute-start(f32[8,128]{1,0:T(8,128)S(1)} %get-tuple-element.39.p0), channel_id=1, source_target_pairs={{0,32},{4,36},{32,0},{36,4},{1,33},{5,37},{33,1},{37,5},{2,34},{6,... | collective-permute-start | bytes 12296 | tf_op jit(solution)/shard_map/first_columns/ppermute | solution.py:283
  42.3 2.5 %collective-permute-start.7 = (f32[8,128]{1,0:T(8,128)S(1)}, f32[8,128]{1,0:T(8,128)S(1)}, u32[]{:S(2)}, u32[]{:S(2)}) collective-permute-start(f32[8,128]{1,0:T(8,128)S(1)} %get-tuple-element.39.p0), channel_id=1, source_target_pairs={{0,4},{4,0},{32,36},{36,32},{1,5},{5,1},{33,37},{37,33},{2,6},{6,2... | collective-permute-start | bytes 12296 | tf_op jit(solution)/shard_map/first_columns/ppermute | solution.py:283
  56.1 4.3 %collective-permute-start.12 = (f32[4,128]{1,0:T(4,128)S(1)}, f32[4,128]{1,0:T(4,128)S(1)}, u32[]{:S(2)}, u32[]{:S(2)}) collective-permute-start(f32[4,128]{1,0:T(4,128)S(1)} %second_rows.1.p0), channel_id=1, source_target_pairs={{0,36},{4,32},{32,4},{36,0},{1,37},{5,33},{33,5},{37,1},{2,38},{6,... | collective-permute-start | bytes 6152 | tf_op jit(solution)/shard_map/last_columns/ppermute | solution.py:283
  58.8 2.4 %collective-permute-start.11 = (f32[4,128]{1,0:T(4,128)S(1)}, f32[4,128]{1,0:T(4,128)S(1)}, u32[]{:S(2)}, u32[]{:S(2)}) collective-permute-start(f32[4,128]{1,0:T(4,128)S(1)} %second_rows.1.p0), channel_id=1, source_target_pairs={{0,32},{4,36},{32,0},{36,4},{1,33},{5,37},{33,1},{37,5},{2,34},{6,... | collective-permute-start | bytes 6152 | tf_op jit(solution)/shard_map/last_columns/ppermute | solution.py:283
  59.2 2.1 %collective-permute-start.10 = (f32[4,128]{1,0:T(4,128)S(1)}, f32[4,128]{1,0:T(4,128)S(1)}, u32[]{:S(2)}, u32[]{:S(2)}) collective-permute-start(f32[4,128]{1,0:T(4,128)S(1)} %second_rows.1.p0), channel_id=1, source_target_pairs={{0,4},{4,0},{32,36},{36,32},{1,5},{5,1},{33,37},{37,33},{2,6},{6,2... | collective-permute-start | bytes 6152 | tf_op jit(solution)/shard_map/last_columns/ppermute | solution.py:283
  72.6 3.4 %collective-permute-start.13 = (f32[1,128]{1,0:T(1,128)S(1)}, f32[1,128]{1,0:T(1,128)S(1)}, u32[]{:S(2)}, u32[]{:S(2)}) collective-permute-start(f32[1,128]{1,0:T(1,128)S(1)} %get-tuple-element.48), channel_id=1, source_target_pairs={{0,4},{4,0},{32,36},{36,32},{1,5},{5,1},{33,37},{37,33},{2,6},{6,2... | collective-permute-start | bytes 1544 | tf_op jit(solution)/shard_map/mass/ppermute | solution.py:283
  74.3 2.4 %collective-permute-start.14 = (f32[1,128]{1,0:T(1,128)S(1)}, f32[1,128]{1,0:T(1,128)S(1)}, u32[]{:S(2)}, u32[]{:S(2)}) collective-permute-start(f32[1,128]{1,0:T(1,128)S(1)} %get-tuple-element.49), channel_id=1, source_target_pairs={{0,32},{4,36},{32,0},{36,4},{1,33},{5,37},{33,1},{37,5},{2,34},{6,... | collective-permute-start | bytes 1544 | tf_op jit(solution)/shard_map/mass/ppermute | solution.py:283
  75.5 3.0 %collective-permute-start.15 = (f32[1,128]{1,0:T(1,128)S(1)}, f32[1,128]{1,0:T(1,128)S(1)}, u32[]{:S(2)}, u32[]{:S(2)}) collective-permute-start(f32[1,128]{1,0:T(1,128)S(1)} %get-tuple-element.50), channel_id=1, source_target_pairs={{0,36},{4,32},{32,4},{36,0},{1,37},{5,33},{33,5},{37,1},{2,38},{6,... | collective-permute-start | bytes 1544 | tf_op jit(solution)/shard_map/mass/ppermute | solution.py:283

commit v9 on v8

--- a/solution.py
+++ b/solution.py
@@ -317,7 +317,7 @@
         messages = exchanged(copies)
     with jax.named_scope("gather"):
         targets = call(parcel, shape(COLUMN_BLOCKS, CELLS, WIDTH, dtype=BF16), 3, name="parcel")(
-            frame, back(own, 0), last
+            frame, back(features[0], 0), last
         )
         anywhere = pl.BlockSpec(memory_space=pl.ANY)
         vmem = pl.BlockSpec(memory_space=pltpu.VMEM)

time: 79.4 us -> 79.4 us (level)
  transfers between devices with their start and end apart: 18 -> 18, of which waited for: 11 -> 11; matrix products, arithmetic and copies ran while one was open for 0% -> 0% of each run, Pallas kernels for 2% -> 4%
where the time goes in v9:
time: 79.4 us; the launch traced here: 79 us
  starting transfers between devices  31.2 us (39%)
  blocking collectives  19.7 us (25%)
  waiting for transfers between devices  19.6 us (25%)
  Pallas kernels  7.71 us (10%)
    all_to_all x2, blocking collectives, exchanged(): lax.all_to_all(copies, COLUMN_AXES, split_axis=0, concat_axis=0, tiled=True)  19.7 us
    ppermute x9, starting transfers between devices, across(): return lax.ppermute(value, ROW_AXES, [(d, d ^ k) for d in range(4)])  12 us
    all_to_all x2, starting transfers between devices, exchanged(): lax.all_to_all(copies, COLUMN_AXES, split_axis=0, concat_axis=0, tiled=True)  11.3 us
    ppermute x9, waiting for transfers between devices, across(): return lax.ppermute(value, ROW_AXES, [(d, d ^ k) for d in range(4)])  6.31 us
    all_to_all x2, waiting for transfers between devices, exchanged(): lax.all_to_all(copies, COLUMN_AXES, split_axis=0, concat_axis=0, tiled=True)  6.18 us
    ppermute x3, waiting for transfers between devices, back(): return lax.ppermute(value, ('z', 'g'), moves)  6.03 us
    ppermute x4, starting transfers between devices, swapped(): return lax.ppermute(value, axis, [(0, 1), (1, 0)])  4.13 us
    ppermute x3, starting transfers between devices, back(): return lax.ppermute(value, ('z', 'g'), moves)  3.86 us
  transfers between devices with their start and end apart: 18, of which 11 were waited for; matrix products, arithmetic and copies ran while one was open for 0% of the time, Pallas kernels for 4%

profile of v9, /device:TPU:1, one launch (start us, length us, event | category | flops | bytes accessed | tf_op | source)
XLA Modules:
  0.0 79.0 jit_solution(11311925142878160374)
XLA Ops:
  0.6 1.3 %collective-permute-start = (bf16[128,256]{1,0:T(8,128)(2,1)}, bf16[128,256]{1,0:T(8,128)(2,1)S(1)}, u32[]{:S(2)}, u32[]{:S(2)}) collective-permute-start(bf16[128,256]{1,0:T(8,128)(2,1)} %bitcast.1), channel_id=1, source_target_pairs={{1,0},{2,1},{3,2},{33,32},{34,33},{35,34},{5,4},{6,5},{7,6},{37,36... | collective-permute-start | bytes 196616 | tf_op jit(solution)/shard_map/gather/ppermute | solution.py:288
  1.9 1.7 %local_sums.1 = (f32[16,8,128]{2,1,0:T(8,128)}, bf16[128,256]{1,0:T(8,128)(2,1)S(1)}, bf16[128,256]{1,0:T(8,128)(2,1)S(1)}, f32[24,128]{1,0:T(8,128)S(1)}) custom-call(bf16[1,128,256]{2,1,0:T(8,128)(2,1)} %features.1, bf16[128,256]{1,0:T(8,128)(2,1)} %last.1, f32[1,128]{1,0:T(1,128)} %growth.1, s32[5]{0:T(128)} %counts.1), custom_call_target="tpu_custom_call" | custom-call | tf_op jit(solution)/shard_map/moments/local_sums/pallas_call | solution.py:303
  3.6 7.6 %all-to-all-start = ((f32[16,8,128]{2,1,0:T(8,128)}), f32[16,8,128]{2,1,0:T(8,128)S(1)}, u32[]{:S(2)}, u32[]{:S(2)}) async-start(f32[16,8,128]{2,1,0:T(8,128)} %get-tuple-element.28), calls=%async_computation | async-start | bytes 131072 | tf_op jit(solution)/shard_map/moments/all_to_all | solution.py:292
  11.2 0.0 collective-permute-done.shifted
  11.2 1.1 %parcel.1.copies = bf16[16,128,256]{2,1,0:T(8,128)(2,1)} custom-call(f32[24,128]{1,0:T(8,128)S(1)} %get-tuple-element.27.frame, bf16[128,256]{1,0:T(8,128)(2,1)S(1)} %collective-permute-done.shifted, bf16[128,256]{1,0:T(8,128)(2,1)S(1)} %get-tuple-element.30.last), custom_call_target="tpu_custom_call" | custom-call | tf_op jit(solution)/shard_map/gather/parcel/pallas_call | solution.py:319
  12.3 5.4 %all-to-all-done.messages = f32[16,8,128]{2,1,0:T(8,128)S(1)} async-done(((f32[16,8,128]{2,1,0:T(8,128)}), f32[16,8,128]{2,1,0:T(8,128)S(1)}, u32[]{:S(2)}, u32[]{:S(2)}) %all-to-all-start) | async-done | bytes 65568 | tf_op jit(solution)/shard_map/moments/all_to_all | solution.py:292
  17.7 3.7 %all-to-all-start.1 = ((bf16[16,128,256]{2,1,0:T(8,128)(2,1)}), bf16[16,128,256]{2,1,0:T(8,128)(2,1)S(1)}, u32[]{:S(2)}, u32[]{:S(2)}) async-start(bf16[16,128,256]{2,1,0:T(8,128)(2,1)} %get-tuple-element.31), calls=%async_computation.1 | async-start | bytes 2097152 | tf_op jit(solution)/shard_map/gather/all_to_all | solution.py:292
  21.4 2.2 %collective-permute-start.2 = (bf16[128,256]{1,0:T(8,128)(2,1)S(1)}, bf16[128,256]{1,0:T(8,128)(2,1)S(1)}, u32[]{:S(2)}, u32[]{:S(2)}) collective-permute-start(bf16[128,256]{1,0:T(8,128)(2,1)S(1)} %get-tuple-element.33.own), channel_id=1, source_target_pairs={{0,4},{4,0},{1,5},{5,1},{2,6},{6,2},{3,7},{7,3},{8,12},{12,8},{9,1... | collective-permute-start | bytes 196616 | tf_op jit(solution)/shard_map/gather/ppermute | solution.py:279
  23.6 0.1 collective-permute-start.1
  23.7 1.1 %collective-permute-done.1.other = f32[8,128]{1,0:T(8,128)S(1)} collective-permute-done((f32[8,128]{1,0:T(8,128)S(1)}, f32[8,128]{1,0:T(8,128)S(1)}, u32[]{:S(2)}, u32[]{:S(2)}) %collective-permute-start.1) | collective-permute-done | bytes 4128 | tf_op jit(solution)/shard_map/gather/ppermute | solution.py:279
  24.8 0.0 collective-permute-done.2.other_own
  24.8 1.7 %collective-permute-start.6 = (bf16[256,256]{1,0:T(8,128)(2,1)S(1)}, bf16[256,256]{1,0:T(8,128)(2,1)S(1)}, u32[]{:S(2)}, u32[]{:S(2)}) collective-permute-start(bf16[256,256]{1,0:T(8,128)(2,1)S(1)} %get-tuple-element.35.near), channel_id=1, source_target_pairs={{0,32},{32,0},{1,33},{33,1},{2,34},{34,2},{3,35},{35,3},{4,36},{36... | collective-permute-start | bytes 393224 | tf_op jit(solution)/shard_map/gather/ppermute | solution.py:279
  26.5 1.3 %collective-permute-start.5 = (f32[8,128]{1,0:T(8,128)S(1)}, f32[8,128]{1,0:T(8,128)S(1)}, u32[]{:S(2)}, u32[]{:S(2)}) collective-permute-start(f32[8,128]{1,0:T(8,128)S(1)} %get-tuple-element.34.mine), channel_id=1, source_target_pairs={{1,32},{2,33},{3,34},{33,0},{34,1},{35,2},{5,36},{6,37},{7,38},{37... | collective-permute-start | bytes 12296 | tf_op jit(solution)/shard_map/gather/ppermute | solution.py:288
  27.8 1.3 %collective-permute-start.4 = (f32[8,128]{1,0:T(8,128)S(1)}, f32[8,128]{1,0:T(8,128)S(1)}, u32[]{:S(2)}, u32[]{:S(2)}) collective-permute-start(f32[8,128]{1,0:T(8,128)S(1)} %get-tuple-element.34.mine), channel_id=1, source_target_pairs={{1,0},{2,1},{3,2},{33,32},{34,33},{35,34},{5,4},{6,5},{7,6},{37,36... | collective-permute-start | bytes 12296 | tf_op jit(solution)/shard_map/gather/ppermute | solution.py:288
  29.1 0.1 collective-permute-start.3
  29.2 4.4 %collective-permute-done.5.back_across = f32[8,128]{1,0:T(8,128)S(1)} collective-permute-done((f32[8,128]{1,0:T(8,128)S(1)}, f32[8,128]{1,0:T(8,128)S(1)}, u32[]{:S(2)}, u32[]{:S(2)}) %collective-permute-start.5) | collective-permute-done | bytes 4128 | tf_op jit(solution)/shard_map/gather/ppermute | solution.py:288
  33.6 1.6 %collective-permute-done.4.back = f32[8,128]{1,0:T(8,128)S(1)} collective-permute-done((f32[8,128]{1,0:T(8,128)S(1)}, f32[8,128]{1,0:T(8,128)S(1)}, u32[]{:S(2)}, u32[]{:S(2)}) %collective-permute-start.4) | collective-permute-done | bytes 4128 | tf_op jit(solution)/shard_map/gather/ppermute | solution.py:288
  35.2 0.0 collective-permute-done.3.across
  35.2 0.0 collective-permute-done.6.far
  35.2 0.2 prepared.1
  35.4 0.8 %all-to-all-done.1.targets = bf16[16,128,256]{2,1,0:T(8,128)(2,1)S(1)} async-done(((bf16[16,128,256]{2,1,0:T(8,128)(2,1)}), bf16[16,128,256]{2,1,0:T(8,128)(2,1)S(1)}, u32[]{:S(2)}, u32[]{:S(2)}) %all-to-all-start.1) | async-done | bytes 1048608 | tf_op jit(solution)/shard_map/gather/all_to_all | solution.py:292
  36.2 1.3 %first_pass.1 = (f32[16,512,128]{2,1,0:T(8,128)S(1)}, f32[8,128]{1,0:T(8,128)S(1)}) custom-call(f32[24,128]{1,0:T(8,128)S(1)} %get-tuple-element.27.frame, bf16[16,128,256]{2,1,0:T(8,128)(2,1)S(1)} %all-to-all-done.1.targets, bf16[512,256]{1,0:T(8,128)(2,1)S(1)} %get-tuple-element.36.rows, f32[512,128]{1,0:T(8,128)S(1)} %get-tuple-element.37.weights, ...), custom_call_target="tpu_custom_call" | custom-call | tf_op jit(solution)/shard_map/first_rows/first_pass/pallas_call | solution.py:353
  37.5 4.8 %collective-permute-start.9 = (f32[8,128]{1,0:T(8,128)S(1)}, f32[8,128]{1,0:T(8,128)S(1)}, u32[]{:S(2)}, u32[]{:S(2)}) collective-permute-start(f32[8,128]{1,0:T(8,128)S(1)} %get-tuple-element.39.p0), channel_id=1, source_target_pairs={{0,36},{4,32},{32,4},{36,0},{1,37},{5,33},{33,5},{37,1},{2,38},{6,... | collective-permute-start | bytes 12296 | tf_op jit(solution)/shard_map/first_columns/ppermute | solution.py:283
  42.3 0.0 collective-permute-start.8
  42.3 0.5 collective-permute-start.7
  42.8 0.8 %collective-permute-done.9.p3 = f32[8,128]{1,0:T(8,128)S(1)} collective-permute-done((f32[8,128]{1,0:T(8,128)S(1)}, f32[8,128]{1,0:T(8,128)S(1)}, u32[]{:S(2)}, u32[]{:S(2)}) %collective-permute-start.9) | collective-permute-done | bytes 4128 | tf_op jit(solution)/shard_map/first_columns/ppermute | solution.py:283
  43.6 1.2 %collective-permute-done.8.p2 = f32[8,128]{1,0:T(8,128)S(1)} collective-permute-done((f32[8,128]{1,0:T(8,128)S(1)}, f32[8,128]{1,0:T(8,128)S(1)}, u32[]{:S(2)}, u32[]{:S(2)}) %collective-permute-start.8) | collective-permute-done | bytes 4128 | tf_op jit(solution)/shard_map/first_columns/ppermute | solution.py:283
  44.8 0.0 collective-permute-done.7.p1
  44.8 0.8 first_columns.1
  45.6 9.8 %all_to_all.20.parts = f32[16,16,128]{2,1,0:T(8,128)S(1)} all-to-all(f32[16,16,128]{2,1,0:T(8,128)S(1)} %get-tuple-element.42), channel_id=1, replica_groups=mesh['x'=4,'z'=2,'y'=4,'c'=2,'g'=4] {'x','y'}, dimensions={0} | all-to-all | bytes 262144 | tf_op jit(solution)/shard_map/first_columns/all_to_all | solution.py:292
  55.4 0.7 second_rows.1.p0
  56.1 2.7 %collective-permute-start.12 = (f32[4,128]{1,0:T(4,128)S(1)}, f32[4,128]{1,0:T(4,128)S(1)}, u32[]{:S(2)}, u32[]{:S(2)}) collective-permute-start(f32[4,128]{1,0:T(4,128)S(1)} %second_rows.1.p0), channel_id=1, source_target_pairs={{0,36},{4,32},{32,4},{36,0},{1,37},{5,33},{33,5},{37,1},{2,38},{6,... | collective-permute-start | bytes 6152 | tf_op jit(solution)/shard_map/last_columns/ppermute | solution.py:283
  58.8 0.3 collective-permute-start.11
  59.2 0.2 collective-permute-start.10
  59.3 1.1 %collective-permute-done.12.p3 = f32[4,128]{1,0:T(4,128)S(1)} collective-permute-done((f32[4,128]{1,0:T(4,128)S(1)}, f32[4,128]{1,0:T(4,128)S(1)}, u32[]{:S(2)}, u32[]{:S(2)}) %collective-permute-start.12) | collective-permute-done | bytes 2080 | tf_op jit(solution)/shard_map/last_columns/ppermute | solution.py:283
  60.4 0.9 %collective-permute-done.11.p2 = f32[4,128]{1,0:T(4,128)S(1)} collective-permute-done((f32[4,128]{1,0:T(4,128)S(1)}, f32[4,128]{1,0:T(4,128)S(1)}, u32[]{:S(2)}, u32[]{:S(2)}) %collective-permute-start.11) | collective-permute-done | bytes 2080 | tf_op jit(solution)/shard_map/last_columns/ppermute | solution.py:283
  61.3 0.0 collective-permute-done.10.p1
  61.3 0.8 last_columns.1
  62.1 9.8 %all_to_all.21.parts = f32[16,16,128]{2,1,0:T(8,128)S(1)} all-to-all(f32[16,16,128]{2,1,0:T(8,128)S(1)} %get-tuple-element.44), channel_id=1, replica_groups=mesh['x'=4,'z'=2,'y'=4,'c'=2,'g'=4] {'x','y'}, dimensions={0} | all-to-all | bytes 262144 | tf_op jit(solution)/shard_map/last_columns/all_to_all | solution.py:292
  71.9 0.7 last_rows.1
  72.6 1.7 %collective-permute-start.13 = (f32[1,128]{1,0:T(1,128)S(1)}, f32[1,128]{1,0:T(1,128)S(1)}, u32[]{:S(2)}, u32[]{:S(2)}) collective-permute-start(f32[1,128]{1,0:T(1,128)S(1)} %get-tuple-element.48), channel_id=1, source_target_pairs={{0,4},{4,0},{32,36},{36,32},{1,5},{5,1},{33,37},{37,33},{2,6},{6,2... | collective-permute-start | bytes 1544 | tf_op jit(solution)/shard_map/mass/ppermute | solution.py:283
  74.3 1.2 %collective-permute-start.14 = (f32[1,128]{1,0:T(1,128)S(1)}, f32[1,128]{1,0:T(1,128)S(1)}, u32[]{:S(2)}, u32[]{:S(2)}) collective-permute-start(f32[1,128]{1,0:T(1,128)S(1)} %get-tuple-element.49), channel_id=1, source_target_pairs={{0,32},{4,36},{32,0},{36,4},{1,33},{5,37},{33,1},{37,5},{2,34},{6,... | collective-permute-start | bytes 1544 | tf_op jit(solution)/shard_map/mass/ppermute | solution.py:283
  75.5 0.6 collective-permute-start.15
  76.0 0.0 collective-permute-done.13.q1
  76.0 0.7 collective-permute-done.14.q2
  76.7 1.7 %collective-permute-done.15.q3 = f32[1,128]{1,0:T(1,128)S(1)} collective-permute-done((f32[1,128]{1,0:T(1,128)S(1)}, f32[1,128]{1,0:T(1,128)S(1)}, u32[]{:S(2)}, u32[]{:S(2)}) %collective-permute-start.15) | collective-permute-done | bytes 544 | tf_op jit(solution)/shard_map/mass/ppermute | solution.py:283
  78.4 0.5 outputs.1
  (2 shorter events, 0.0 us)
Async XLA Ops:
  0.6 10.6 %collective-permute-start = (bf16[128,256]{1,0:T(8,128)(2,1)}, bf16[128,256]{1,0:T(8,128)(2,1)S(1)}, u32[]{:S(2)}, u32[]{:S(2)}) collective-permute-start(bf16[128,256]{1,0:T(8,128)(2,1)} %bitcast.1), channel_id=1, source_target_pairs={{1,0},{2,1},{3,2},{33,32},{34,33},{35,34},{5,4},{6,5},{7,6},{37,36... | collective-permute-start | bytes 196616 | tf_op jit(solution)/shard_map/gather/ppermute | solution.py:288
  3.6 14.1 %all-to-all-start = ((f32[16,8,128]{2,1,0:T(8,128)}), f32[16,8,128]{2,1,0:T(8,128)S(1)}, u32[]{:S(2)}, u32[]{:S(2)}) async-start(f32[16,8,128]{2,1,0:T(8,128)} %get-tuple-element.28), calls=%async_computation | async-start | bytes 131072 | tf_op jit(solution)/shard_map/moments/all_to_all | solution.py:292
  17.7 18.5 %all-to-all-start.1 = ((bf16[16,128,256]{2,1,0:T(8,128)(2,1)}), bf16[16,128,256]{2,1,0:T(8,128)(2,1)S(1)}, u32[]{:S(2)}, u32[]{:S(2)}) async-start(bf16[16,128,256]{2,1,0:T(8,128)(2,1)} %get-tuple-element.31), calls=%async_computation.1 | async-start | bytes 2097152 | tf_op jit(solution)/shard_map/gather/all_to_all | solution.py:292
  21.4 3.4 %collective-permute-start.2 = (bf16[128,256]{1,0:T(8,128)(2,1)S(1)}, bf16[128,256]{1,0:T(8,128)(2,1)S(1)}, u32[]{:S(2)}, u32[]{:S(2)}) collective-permute-start(bf16[128,256]{1,0:T(8,128)(2,1)S(1)} %get-tuple-element.33.own), channel_id=1, source_target_pairs={{0,4},{4,0},{1,5},{5,1},{2,6},{6,2},{3,7},{7,3},{8,12},{12,8},{9,1... | collective-permute-start | bytes 196616 | tf_op jit(solution)/shard_map/gather/ppermute | solution.py:279
  23.6 1.2 %collective-permute-start.1 = (f32[8,128]{1,0:T(8,128)S(1)}, f32[8,128]{1,0:T(8,128)S(1)}, u32[]{:S(2)}, u32[]{:S(2)}) collective-permute-start(f32[8,128]{1,0:T(8,128)S(1)} %get-tuple-element.32.mine), channel_id=1, source_target_pairs={{0,4},{4,0},{1,5},{5,1},{2,6},{6,2},{3,7},{7,3},{8,12},{12,8},{9,1... | collective-permute-start | bytes 12296 | tf_op jit(solution)/shard_map/gather/ppermute | solution.py:279
  24.8 10.5 %collective-permute-start.6 = (bf16[256,256]{1,0:T(8,128)(2,1)S(1)}, bf16[256,256]{1,0:T(8,128)(2,1)S(1)}, u32[]{:S(2)}, u32[]{:S(2)}) collective-permute-start(bf16[256,256]{1,0:T(8,128)(2,1)S(1)} %get-tuple-element.35.near), channel_id=1, source_target_pairs={{0,32},{32,0},{1,33},{33,1},{2,34},{34,2},{3,35},{35,3},{4,36},{36... | collective-permute-start | bytes 393224 | tf_op jit(solution)/shard_map/gather/ppermute | solution.py:279
  26.5 7.1 %collective-permute-start.5 = (f32[8,128]{1,0:T(8,128)S(1)}, f32[8,128]{1,0:T(8,128)S(1)}, u32[]{:S(2)}, u32[]{:S(2)}) collective-permute-start(f32[8,128]{1,0:T(8,128)S(1)} %get-tuple-element.34.mine), channel_id=1, source_target_pairs={{1,32},{2,33},{3,34},{33,0},{34,1},{35,2},{5,36},{6,37},{7,38},{37... | collective-permute-start | bytes 12296 | tf_op jit(solution)/shard_map/gather/ppermute | solution.py:288
  27.8 7.4 %collective-permute-start.4 = (f32[8,128]{1,0:T(8,128)S(1)}, f32[8,128]{1,0:T(8,128)S(1)}, u32[]{:S(2)}, u32[]{:S(2)}) collective-permute-start(f32[8,128]{1,0:T(8,128)S(1)} %get-tuple-element.34.mine), channel_id=1, source_target_pairs={{1,0},{2,1},{3,2},{33,32},{34,33},{35,34},{5,4},{6,5},{7,6},{37,36... | collective-permute-start | bytes 12296 | tf_op jit(solution)/shard_map/gather/ppermute | solution.py:288
  29.1 6.1 %collective-permute-start.3 = (f32[8,128]{1,0:T(8,128)S(1)}, f32[8,128]{1,0:T(8,128)S(1)}, u32[]{:S(2)}, u32[]{:S(2)}) collective-permute-start(f32[8,128]{1,0:T(8,128)S(1)} %get-tuple-element.34.mine), channel_id=1, source_target_pairs={{0,32},{32,0},{1,33},{33,1},{2,34},{34,2},{3,35},{35,3},{4,36},{36... | collective-permute-start | bytes 12296 | tf_op jit(solution)/shard_map/gather/ppermute | solution.py:279
  37.5 6.1 %collective-permute-start.9 = (f32[8,128]{1,0:T(8,128)S(1)}, f32[8,128]{1,0:T(8,128)S(1)}, u32[]{:S(2)}, u32[]{:S(2)}) collective-permute-start(f32[8,128]{1,0:T(8,128)S(1)} %get-tuple-element.39.p0), channel_id=1, source_target_pairs={{0,36},{4,32},{32,4},{36,0},{1,37},{5,33},{33,5},{37,1},{2,38},{6,... | collective-permute-start | bytes 12296 | tf_op jit(solution)/shard_map/first_columns/ppermute | solution.py:283
  42.3 2.5 %collective-permute-start.8 = (f32[8,128]{1,0:T(8,128)S(1)}, f32[8,128]{1,0:T(8,128)S(1)}, u32[]{:S(2)}, u32[]{:S(2)}) collective-permute-start(f32[8,128]{1,0:T(8,128)S(1)} %get-tuple-element.39.p0), channel_id=1, source_target_pairs={{0,32},{4,36},{32,0},{36,4},{1,33},{5,37},{33,1},{37,5},{2,34},{6,... | collective-permute-start | bytes 12296 | tf_op jit(solution)/shard_map/first_columns/ppermute | solution.py:283
  42.3 2.5 %collective-permute-start.7 = (f32[8,128]{1,0:T(8,128)S(1)}, f32[8,128]{1,0:T(8,128)S(1)}, u32[]{:S(2)}, u32[]{:S(2)}) collective-permute-start(f32[8,128]{1,0:T(8,128)S(1)} %get-tuple-element.39.p0), channel_id=1, source_target_pairs={{0,4},{4,0},{32,36},{36,32},{1,5},{5,1},{33,37},{37,33},{2,6},{6,2... | collective-permute-start | bytes 12296 | tf_op jit(solution)/shard_map/first_columns/ppermute | solution.py:283
  56.1 4.3 %collective-permute-start.12 = (f32[4,128]{1,0:T(4,128)S(1)}, f32[4,128]{1,0:T(4,128)S(1)}, u32[]{:S(2)}, u32[]{:S(2)}) collective-permute-start(f32[4,128]{1,0:T(4,128)S(1)} %second_rows.1.p0), channel_id=1, source_target_pairs={{0,36},{4,32},{32,4},{36,0},{1,37},{5,33},{33,5},{37,1},{2,38},{6,... | collective-permute-start | bytes 6152 | tf_op jit(solution)/shard_map/last_columns/ppermute | solution.py:283
  58.8 2.4 %collective-permute-start.11 = (f32[4,128]{1,0:T(4,128)S(1)}, f32[4,128]{1,0:T(4,128)S(1)}, u32[]{:S(2)}, u32[]{:S(2)}) collective-permute-start(f32[4,128]{1,0:T(4,128)S(1)} %second_rows.1.p0), channel_id=1, source_target_pairs={{0,32},{4,36},{32,0},{36,4},{1,33},{5,37},{33,1},{37,5},{2,34},{6,... | collective-permute-start | bytes 6152 | tf_op jit(solution)/shard_map/last_columns/ppermute | solution.py:283
  59.2 2.1 %collective-permute-start.10 = (f32[4,128]{1,0:T(4,128)S(1)}, f32[4,128]{1,0:T(4,128)S(1)}, u32[]{:S(2)}, u32[]{:S(2)}) collective-permute-start(f32[4,128]{1,0:T(4,128)S(1)} %second_rows.1.p0), channel_id=1, source_target_pairs={{0,4},{4,0},{32,36},{36,32},{1,5},{5,1},{33,37},{37,33},{2,6},{6,2... | collective-permute-start | bytes 6152 | tf_op jit(solution)/shard_map/last_columns/ppermute | solution.py:283
  72.6 3.4 %collective-permute-start.13 = (f32[1,128]{1,0:T(1,128)S(1)}, f32[1,128]{1,0:T(1,128)S(1)}, u32[]{:S(2)}, u32[]{:S(2)}) collective-permute-start(f32[1,128]{1,0:T(1,128)S(1)} %get-tuple-element.48), channel_id=1, source_target_pairs={{0,4},{4,0},{32,36},{36,32},{1,5},{5,1},{33,37},{37,33},{2,6},{6,2... | collective-permute-start | bytes 1544 | tf_op jit(solution)/shard_map/mass/ppermute | solution.py:283
  74.3 2.4 %collective-permute-start.14 = (f32[1,128]{1,0:T(1,128)S(1)}, f32[1,128]{1,0:T(1,128)S(1)}, u32[]{:S(2)}, u32[]{:S(2)}) collective-permute-start(f32[1,128]{1,0:T(1,128)S(1)} %get-tuple-element.49), channel_id=1, source_target_pairs={{0,32},{4,36},{32,0},{36,4},{1,33},{5,37},{33,1},{37,5},{2,34},{6,... | collective-permute-start | bytes 1544 | tf_op jit(solution)/shard_map/mass/ppermute | solution.py:283
  75.5 3.0 %collective-permute-start.15 = (f32[1,128]{1,0:T(1,128)S(1)}, f32[1,128]{1,0:T(1,128)S(1)}, u32[]{:S(2)}, u32[]{:S(2)}) collective-permute-start(f32[1,128]{1,0:T(1,128)S(1)} %get-tuple-element.50), channel_id=1, source_target_pairs={{0,36},{4,32},{32,4},{36,0},{1,37},{5,33},{33,5},{37,1},{2,38},{6,... | collective-permute-start | bytes 1544 | tf_op jit(solution)/shard_map/mass/ppermute | solution.py:283
